TPU v7x, 32 devices: a whole 2x2x4 slice. The times are simulated.
32 devices in a mesh: wide: 8 (over z, x), narrow: 4 (over y, core).
Axes of the slice: x: 2, y: 2, z: 4, core: 2. Of those that a mesh axis runs over, the one named last changes fastest.
Arguments:
- tokens: bfloat16 [32768, 512], P(('wide', 'narrow')), may hold values from -11 to 11
- cotangent: float32 [32768, 512], P(('wide', 'narrow')), may hold values from -6 to 6
- cells: int32 [32, 1024], P(('wide', 'narrow')), may hold values from 0 to 3, never falling along the last dimension, each value on 1 to 512 neighbouring positions
- present: int32 [32, 1024], P(('wide', 'narrow')), may hold values 0 or 1
- generate: int32 [32, 1024], P(('wide', 'narrow')), may hold values 0 or 1
- w_qkv: float32 [512, 1536], P('narrow'), may hold values from -0.25 to 0.25
- w_out: float32 [512, 512], P('narrow'), may hold values from -1 to 1
- w_up: float32 [512, 512], P('narrow'), may hold values from -0.25 to 0.25
- w_down: float32 [512, 512], P('narrow'), may hold values from -0.25 to 0.25
- vectors: float32 [9, 512], P(None, 'narrow'), may hold values from -1.5 to 3.2
- m_qkv: float32 [512, 1536], P('narrow'), may hold values from -2 to 2
- m_out: float32 [512, 512], P('narrow'), may hold values from -2 to 2
- m_up: float32 [512, 512], P('narrow'), may hold values from -2 to 2
- m_down: float32 [512, 512], P('narrow'), may hold values from -2 to 2
- m_vec: float32 [9, 512], P(None, 'narrow'), may hold values from -4 to 4
- v_qkv: float32 [512, 1536], P('narrow'), may hold values from 0.010386238 to 0.1661798
- v_out: float32 [512, 512], P('narrow'), may hold values from 0.010386238 to 0.1661798
- v_up: float32 [512, 512], P('narrow'), may hold values from 0.010386238 to 0.1661798
- v_down: float32 [512, 512], P('narrow'), may hold values from 0.010386238 to 0.1661798
- v_vec: float32 [9, 512], P(None, 'narrow'), may hold values from 0.09347615 to 1.4956183
Outputs:
- mixed: bfloat16 [32768, 512], P(('wide', 'narrow'))
- input_grad: float32 [32768, 512], P(('wide', 'narrow'))
- grad_norm: float32 [], replicated
- new_qkv: float32 [512, 1536], P('narrow')
- new_out: float32 [512, 512], P('narrow')
- new_up: float32 [512, 512], P('narrow')
- new_down: float32 [512, 512], P('narrow')
- new_vectors: float32 [9, 512], P(None, 'narrow')
- first_qkv: float32 [512, 1536], P('narrow')
- first_out: float32 [512, 512], P('narrow')
- first_up: float32 [512, 512], P('narrow')
- first_down: float32 [512, 512], P('narrow')
- first_vec: float32 [9, 512], P(None, 'narrow')
- second_qkv: float32 [512, 1536], P('narrow')
- second_out: float32 [512, 512], P('narrow')
- second_up: float32 [512, 512], P('narrow')
- second_down: float32 [512, 512], P('narrow')
- second_vec: float32 [9, 512], P(None, 'narrow')
- copy_qkv: bfloat16 [512, 1536], P('narrow')
- copy_out: bfloat16 [512, 512], P('narrow')
- copy_up: bfloat16 [512, 512], P('narrow')
- copy_down: bfloat16 [512, 512], P('narrow')
- copy_vec: bfloat16 [9, 512], P(None, 'narrow')
Inputs may be any that keep to these rules, and one draw needn't show every extreme that they name: `cells`: within a row cell numbers never fall; each cell holds 1 to 512 tokens, one exactly that many.
All inputs are finite; a program needn't handle non-finite values. No bound on the sum of `present` or of `generate` on one device may be relied on, other than what follows from the above.
Results may differ from a plain program's by a relative error of at most 0.012.
Values may be sent and summed in bfloat16 or wider, within the bound.
No kernel may reach another device: no remote copies, remote signals or barrier semaphores. Data moves between devices by JAX's collectives and lax.ppermute only.
A program may use at most 192 MiB of HBM per device.

v0:
```python
import math

import jax
import jax.numpy as jnp
from jax import lax
from jax.sharding import PartitionSpec as P

D = 512
HEADS = 8
HEAD_DIM = 64
TOK_DEV = 1024
STEP = 10


NORM_EPS = 1e-05
ADAM_EPS = 1e-08


def apply_layer_norm(value):
    center = value - jnp.mean(value, -1, keepdims=True)
    spread = jnp.mean(center * center, -1, keepdims=True)
    inverse_scale = lax.rsqrt(spread + NORM_EPS)
    return (center * inverse_scale, inverse_scale)


def layer_norm_backward(gradient_normalized, normalized_input, inverse_scale):
    return inverse_scale * (
        gradient_normalized
        - jnp.mean(gradient_normalized, -1, keepdims=True)
        - normalized_input * jnp.mean(gradient_normalized * normalized_input, -1, keepdims=True)
    )


def gelu_slope(value):
    cdf = 0.5 * (1.0 + lax.erf(value * (1.0 / math.sqrt(2.0))))
    dens = jnp.exp(-0.5 * value * value) * (1.0 / math.sqrt(2.0 * math.pi))
    return cdf + value * dens


def inner(left, right):
    return lax.dot_general(
        left, right, (((0,), (0,)), ((), ())), preferred_element_type=jnp.float32
    )


def outer_t(left, right):
    return lax.dot_general(
        left, right, (((1,), (1,)), ((), ())), preferred_element_type=jnp.float32
    )


def allowed_of(index_block, cell_block, cell_row, keep_key):
    positions = jnp.arange(cell_row.shape[0], dtype=jnp.int32)
    return (index_block[:, None] == positions[None, :]) | (
        cell_block[:, None] == cell_row[None, :]
    ) & keep_key[None, :]


def forward_pass(tokens, weights, cell_row, keep_key):
    w_qkv, w_out, w_up, w_down, vec_low = weights
    vector_parameters = vec_low.astype(jnp.float32)
    length = tokens.shape[0]
    scale = HEAD_DIM ** (-0.5)
    bias = jnp.concatenate(
        [vector_parameters[0], jnp.zeros_like(vector_parameters[0]), vector_parameters[1]]
    )
    query_key_value = (jnp.dot(tokens, w_qkv, preferred_element_type=jnp.float32) + bias).astype(
        jnp.bfloat16
    )
    queries = query_key_value[:, :D].reshape(length, HEADS, HEAD_DIM)
    keys = query_key_value[:, D : 2 * D].reshape(length, HEADS, HEAD_DIM)
    values = query_key_value[:, 2 * D :].reshape(length, HEADS, HEAD_DIM)
    block = min(512, length)
    count = length // block
    index = jnp.arange(length, dtype=jnp.int32).reshape(count, block)

    def one_block(args):
        q_block, index_block, cell_block = args
        allowed = allowed_of(index_block, cell_block, cell_row, keep_key)
        scores = (
            jnp.einsum("bhe,khe->hbk", q_block, keys, preferred_element_type=jnp.float32) * scale
        )
        scores = jnp.where(allowed[None], scores, -1e30)
        top = jnp.max(scores, -1, keepdims=True)
        expo = jnp.exp(scores - top)
        total = jnp.sum(expo, -1, keepdims=True)
        prob = (expo / total).astype(jnp.bfloat16)
        result = jnp.einsum("hbk,khe->bhe", prob, values, preferred_element_type=jnp.float32)
        return (result, (top + jnp.log(total))[..., 0])

    attention_result, logarithm_total = lax.map(
        one_block,
        (queries.reshape(count, block, HEADS, HEAD_DIM), index, cell_row.reshape(count, block)),
    )
    attention_result = attention_result.reshape(length, D).astype(jnp.bfloat16)
    residual_branch = (
        jnp.dot(attention_result, w_out, preferred_element_type=jnp.float32) + vector_parameters[2]
    )
    normalized_first, inverse_deviation_first = apply_layer_norm(
        tokens.astype(jnp.float32) + residual_branch
    )
    first_moment = normalized_first * vector_parameters[5] + vector_parameters[6]
    first_moment_reduced = first_moment.astype(jnp.bfloat16)
    preactivation = (
        jnp.dot(first_moment_reduced, w_up, preferred_element_type=jnp.float32)
        + vector_parameters[3]
    )
    hidden_activation = jax.nn.gelu(preactivation, approximate=False).astype(jnp.bfloat16)
    down_projection_output = (
        jnp.dot(hidden_activation, w_down, preferred_element_type=jnp.float32)
        + vector_parameters[4]
    )
    normalized_second, inverse_deviation_second = apply_layer_norm(
        first_moment + down_projection_output
    )
    mixed = (normalized_second * vector_parameters[7] + vector_parameters[8]).astype(jnp.bfloat16)
    saved_residuals = (
        query_key_value,
        logarithm_total,
        attention_result,
        normalized_first,
        inverse_deviation_first,
        first_moment_reduced,
        preactivation,
        hidden_activation,
        normalized_second,
        inverse_deviation_second,
    )
    return (mixed, saved_residuals)


def backward_pass(tokens, cotangent, weights, saved_residuals, cell_row, keep_key):
    w_qkv, w_out, w_up, w_down, vec_low = weights
    vector_parameters = vec_low.astype(jnp.float32)
    (
        query_key_value,
        logarithm_total,
        attention_result,
        normalized_first,
        inverse_deviation_first,
        first_moment_reduced,
        preactivation,
        hidden_activation,
        normalized_second,
        inverse_deviation_second,
    ) = saved_residuals
    length = tokens.shape[0]
    scale = HEAD_DIM ** (-0.5)
    gradient_second_gain = jnp.sum(cotangent * normalized_second, 0)
    d_shift_two = jnp.sum(cotangent, 0)
    gradient_hidden_second = layer_norm_backward(
        cotangent * vector_parameters[7], normalized_second, inverse_deviation_second
    )
    d_down = gradient_hidden_second.astype(jnp.bfloat16)
    d_b_down = jnp.sum(d_down, 0, dtype=jnp.float32)
    d_w_down = inner(hidden_activation, d_down)
    d_hidden = outer_t(d_down, w_down)
    d_pre = (d_hidden * gelu_slope(preactivation)).astype(jnp.bfloat16)
    d_b_up = jnp.sum(d_pre, 0, dtype=jnp.float32)
    d_w_up = inner(first_moment_reduced, d_pre)
    first_moment_gradient = gradient_hidden_second + outer_t(d_pre, w_up)
    gradient_first_gain = jnp.sum(first_moment_gradient * normalized_first, 0)
    d_shift_one = jnp.sum(first_moment_gradient, 0)
    gradient_hidden_first = layer_norm_backward(
        first_moment_gradient * vector_parameters[5], normalized_first, inverse_deviation_first
    )
    d_branch = gradient_hidden_first.astype(jnp.bfloat16)
    d_b_out = jnp.sum(d_branch, 0, dtype=jnp.float32)
    d_w_out = inner(attention_result, d_branch)
    d_attended = outer_t(d_branch, w_out).astype(jnp.bfloat16)
    queries = query_key_value[:, :D].reshape(length, HEADS, HEAD_DIM)
    keys = query_key_value[:, D : 2 * D].reshape(length, HEADS, HEAD_DIM)
    values = query_key_value[:, 2 * D :].reshape(length, HEADS, HEAD_DIM)
    block = min(512, length)
    count = length // block
    index = jnp.arange(length, dtype=jnp.int32).reshape(count, block)

    def back_block(carry, args):
        d_keys, d_values = carry
        q_block, do_block, lse_block, index_block, cell_block = args
        allowed = allowed_of(index_block, cell_block, cell_row, keep_key)
        scores = (
            jnp.einsum("bhe,khe->hbk", q_block, keys, preferred_element_type=jnp.float32) * scale
        )
        prob = jnp.where(allowed[None], jnp.exp(scores - lse_block[..., None]), 0.0)
        d_values = d_values + jnp.einsum(
            "hbk,bhe->khe", prob.astype(jnp.bfloat16), do_block, preferred_element_type=jnp.float32
        )
        d_prob = jnp.einsum("bhe,khe->hbk", do_block, values, preferred_element_type=jnp.float32)
        d_scores = (prob * (d_prob - jnp.sum(prob * d_prob, -1, keepdims=True))).astype(
            jnp.bfloat16
        )
        d_query = (
            jnp.einsum("hbk,khe->bhe", d_scores, keys, preferred_element_type=jnp.float32) * scale
        )
        d_keys = (
            d_keys
            + jnp.einsum("hbk,bhe->khe", d_scores, q_block, preferred_element_type=jnp.float32)
            * scale
        )
        return ((d_keys, d_values), d_query)

    empty = jnp.zeros((length, HEADS, HEAD_DIM), jnp.float32)
    (d_keys, d_values), d_queries = lax.scan(
        back_block,
        (empty, empty),
        (
            queries.reshape(count, block, HEADS, HEAD_DIM),
            d_attended.reshape(count, block, HEADS, HEAD_DIM),
            logarithm_total,
            index,
            cell_row.reshape(count, block),
        ),
    )
    d_qkv = jnp.concatenate(
        [d_queries.reshape(length, D), d_keys.reshape(length, D), d_values.reshape(length, D)], 1
    ).astype(jnp.bfloat16)
    d_bias = jnp.sum(d_qkv, 0, dtype=jnp.float32)
    d_w_qkv = inner(tokens, d_qkv)
    input_grad = gradient_hidden_first + outer_t(d_qkv, w_qkv)
    d_vec = jnp.stack(
        [
            d_bias[:D],
            d_bias[2 * D :],
            d_b_out,
            d_b_up,
            d_b_down,
            gradient_first_gain,
            d_shift_one,
            gradient_second_gain,
            d_shift_two,
        ]
    )
    return (input_grad, (d_w_qkv, d_w_out, d_w_up, d_w_down, d_vec))


def adamw(weight, grad, first_moment, second, rate, decay):
    first_moment = 0.5 * first_moment + 0.5 * grad
    second = 0.5 * second + 0.5 * grad * grad
    fix = 1.0 - 0.5**STEP
    update = first_moment / fix / (jnp.sqrt(second / fix) + ADAM_EPS)
    return (weight - rate * (update + decay * weight), first_moment, second)


def body(
    tokens,
    cotangent,
    cells,
    present,
    generate,
    w_qkv,
    w_out,
    w_up,
    w_down,
    vectors,
    m_qkv,
    m_out,
    m_up,
    m_down,
    m_vec,
    v_qkv,
    v_out,
    v_up,
    v_down,
    v_vec,
):
    params = (w_qkv, w_out, w_up, w_down, vectors)
    shards = tuple((p.astype(jnp.bfloat16) for p in params))
    cell_row = cells[0]
    keep_key = (present[0] == 1) & (generate[0] == 0)
    full = (
        lax.all_gather(shards[0], "narrow", axis=0, tiled=True),
        lax.all_gather(shards[1], "narrow", axis=0, tiled=True),
        lax.all_gather(shards[2], "narrow", axis=0, tiled=True),
        lax.all_gather(shards[3], "narrow", axis=0, tiled=True),
        lax.all_gather(shards[4], "narrow", axis=1, tiled=True),
    )
    mixed, saved_residuals = forward_pass(tokens, full, cell_row, keep_key)
    weights_again = (
        lax.all_gather(shards[0], "narrow", axis=0, tiled=True),
        lax.all_gather(shards[1], "narrow", axis=0, tiled=True),
        lax.all_gather(shards[2], "narrow", axis=0, tiled=True),
        lax.all_gather(shards[3], "narrow", axis=0, tiled=True),
        lax.all_gather(shards[4], "narrow", axis=1, tiled=True),
    )
    unused, saved_residuals = forward_pass(tokens, weights_again, cell_row, keep_key)
    input_grad, grads = backward_pass(
        tokens, cotangent, weights_again, saved_residuals, cell_row, keep_key
    )
    partial_sums = (
        lax.psum_scatter(
            grads[0].astype(jnp.bfloat16), "narrow", scatter_dimension=0, tiled=True
        ).astype(jnp.float32),
        lax.psum_scatter(
            grads[1].astype(jnp.bfloat16), "narrow", scatter_dimension=0, tiled=True
        ).astype(jnp.float32),
        lax.psum_scatter(
            grads[2].astype(jnp.bfloat16), "narrow", scatter_dimension=0, tiled=True
        ).astype(jnp.float32),
        lax.psum_scatter(
            grads[3].astype(jnp.bfloat16), "narrow", scatter_dimension=0, tiled=True
        ).astype(jnp.float32),
        lax.psum_scatter(
            grads[4].astype(jnp.bfloat16), "narrow", scatter_dimension=1, tiled=True
        ).astype(jnp.float32),
    )
    totals = lax.psum(
        (partial_sums[0], partial_sums[1], partial_sums[2], partial_sums[3], partial_sums[4]),
        "wide",
    )
    squares = jnp.float32(0.0)
    for grad in totals:
        squares = squares + jnp.sum(grad * grad)
    squares = lax.psum(squares, "narrow")
    grad_norm = jnp.sqrt(squares)
    limit = math.sqrt(TOK_DEV * lax.axis_size("wide") * lax.axis_size("narrow"))
    factor = limit / jnp.maximum(grad_norm, limit)
    firsts = (m_qkv, m_out, m_up, m_down, m_vec)
    seconds = (v_qkv, v_out, v_up, v_down, v_vec)
    news, new_firsts, new_seconds = ([], [], [])
    for number in range(5):
        rate = 0.5 if number == 4 else 0.1
        decay = 0.0 if number == 4 else 0.01
        neww, newm, newv = adamw(
            params[number], totals[number] * factor, firsts[number], seconds[number], rate, decay
        )
        news.append(neww)
        new_firsts.append(newm)
        new_seconds.append(newv)
    return (
        mixed,
        input_grad,
        grad_norm,
        news[0],
        news[1],
        news[2],
        news[3],
        news[4],
        new_firsts[0],
        new_firsts[1],
        new_firsts[2],
        new_firsts[3],
        new_firsts[4],
        new_seconds[0],
        new_seconds[1],
        new_seconds[2],
        new_seconds[3],
        new_seconds[4],
        news[0].astype(jnp.bfloat16),
        news[1].astype(jnp.bfloat16),
        news[2].astype(jnp.bfloat16),
        news[3].astype(jnp.bfloat16),
        news[4].astype(jnp.bfloat16),
    )


def solution(mesh):
    placed = (
        P(("wide", "narrow"), None),
        P(("wide", "narrow"), None),
        P(("wide", "narrow"), None),
        P(("wide", "narrow"), None),
        P(("wide", "narrow"), None),
        P("narrow", None),
        P("narrow", None),
        P("narrow", None),
        P("narrow", None),
        P(None, "narrow"),
        P("narrow", None),
        P("narrow", None),
        P("narrow", None),
        P("narrow", None),
        P(None, "narrow"),
        P("narrow", None),
        P("narrow", None),
        P("narrow", None),
        P("narrow", None),
        P(None, "narrow"),
    )
    return jax.shard_map(
        body,
        mesh=mesh,
        in_specs=placed,
        out_specs=(
            P(("wide", "narrow"), None),
            P(("wide", "narrow"), None),
            P(),
            P("narrow", None),
            P("narrow", None),
            P("narrow", None),
            P("narrow", None),
            P(None, "narrow"),
            P("narrow", None),
            P("narrow", None),
            P("narrow", None),
            P("narrow", None),
            P(None, "narrow"),
            P("narrow", None),
            P("narrow", None),
            P("narrow", None),
            P("narrow", None),
            P(None, "narrow"),
            P("narrow", None),
            P("narrow", None),
            P("narrow", None),
            P("narrow", None),
            P(None, "narrow"),
        ),
        check_vma=False,
    )
```

profile of v0, /device:TPU:0, one launch (start us, length us, event | category | flops | bytes accessed | tf_op | source)
XLA Modules:
  0.0 570.1 jit_solution(7205016221108010244)
XLA Ops:
  23.7 11.2 %all_gather.24 = bf16[512,512]{1,0:T(8,128)(2,1)} all-gather(bf16[128,512]{1,0:T(8,128)(2,1)S(1)} %convert_element_type.149), channel_id=1, replica_groups=mesh['wide'=8,'narrow'=4] {'narrow'}, dimensions={0}, use_global_device_ids=true | all-gather | bytes 655360 | tf_op jit(solution)/shard_map/all_gather | solution.py:275
  34.9 7.7 %all_gather.23 = bf16[512,512]{1,0:T(8,128)(2,1)} all-gather(bf16[128,512]{1,0:T(8,128)(2,1)S(1)} %convert_element_type.147), channel_id=1, replica_groups=mesh['wide'=8,'narrow'=4] {'narrow'}, dimensions={0}, use_global_device_ids=true | all-gather | bytes 655360 | tf_op jit(solution)/shard_map/all_gather | solution.py:274
  42.7 7.7 %all_gather.22 = bf16[512,512]{1,0:T(8,128)(2,1)} all-gather(bf16[128,512]{1,0:T(8,128)(2,1)S(1)} %convert_element_type.145), channel_id=1, replica_groups=mesh['wide'=8,'narrow'=4] {'narrow'}, dimensions={0}, use_global_device_ids=true | all-gather | bytes 655360 | tf_op jit(solution)/shard_map/all_gather | solution.py:273
  62.5 28.6 %while.38 = (s32[]{:T(128)}, bf16[2,512,8,64]{1,3,2,0:T(8,128)(2,1)}, f32[2,8,512]{2,1,0:T(8,128)}, s32[2,512]{1,0:T(2,128)S(1)}, s32[2,512]{1,0:T(2,128)S(1)}, ...) while((s32[]{:T(128)}, ...), condition=%wide.region_11.12_spmd, body=%wide.region_8.11_spmd.sunk | while | flops 1126166528 | bytes 64636092 | solution.py:91
  92.2 81.9 %while.37 = (s32[]{:T(128)}, bf16[2,512,8,64]{1,3,2,0:T(8,128)(2,1)}, s32[2,512]{1,0:T(2,128)S(1)}, s32[2,512]{1,0:T(2,128)S(1)}, s32[1,1024]{1,0:T(1,128)S(1)},...) while((s32[]{:T(128)}, ...), condition=%wide.region_3.4_spmd, body=%wide.region_0.3_spmd.sunk | while | flops 1109394432 | bytes 71877752 | solution.py:91
  93.9 8.1 %fusion.239 = f32[8,512,1024]{2,1,0:T(8,128)} fusion(bf16[1024,8,64]{0,2,1:T(8,128)(2,1)S(1)} %get-tuple-element.826, bf16[2,512,8,64]{1,3,2,0:T(8,128)(2,1)S(1)} %get-tuple-element.825, s32[]{:T(128)S(6)} %copy.152), kind=kOutput, calls=%fused_computation.13.clone.1 | convolution fusion | flops 536870912 | bytes 18350084 | tf_op jit(solution)/shard_map/while/body/eval_jaxpr/bhe,khe->hbk/dot_general | solution.py:81
  102.0 21.7 %fusion.241 = (f32[8,512]{1,0:T(8,128)S(1)}, f32[8,512,1024]{2,1,0:T(8,128)}) fusion(f32[8,512,1024]{2,1,0:T(8,128)} %fusion.239, pred[512,1024]{1,0:T(8,128)(4,1)} %fusion.240), kind=kOutput, calls=%fused_computation.264.clone.1 | output fusion | flops 25166848 | bytes 34095104 | tf_op jit(solution)/shard_map/while/body/eval_jaxpr/sub | solution.py:85
  123.7 9.3 %fusion.242 = bf16[2,512,8,64]{1,3,2,0:T(8,128)(2,1)} fusion(bf16[2,512,8,64]{1,3,2,0:T(8,128)(2,1)} %get-tuple-element.810, s32[]{:T(128)S(6)} %copy.152, bf16[1024,8,64]{0,2,1:T(8,128)(2,1)S(1)} %get-tuple-element.827, f32[8,512,1024]{2,1,0:T(8,128)} %get-tuple-element.733, f32[8,512]{1,0:T(8,128)S(1)} %get-tuple-element.734), kind=kOutput, calls=%fused_computation.12.clone.1 | convolution fusion | flops 545259520 | bytes 18890756 | tf_op jit(solution)/shard_map/while/body/eval_jaxpr/hbk,khe->bhe/dot_general | solution.py:88
  134.5 8.1 %fusion.239 = f32[8,512,1024]{2,1,0:T(8,128)} fusion(bf16[1024,8,64]{0,2,1:T(8,128)(2,1)S(1)} %get-tuple-element.826, bf16[2,512,8,64]{1,3,2,0:T(8,128)(2,1)S(1)} %get-tuple-element.825, s32[]{:T(128)S(6)} %copy.152), kind=kOutput, calls=%fused_computation.13.clone.1 | convolution fusion | flops 536870912 | bytes 18350084 | tf_op jit(solution)/shard_map/while/body/eval_jaxpr/bhe,khe->hbk/dot_general | solution.py:81
  142.6 21.7 %fusion.241 = (f32[8,512]{1,0:T(8,128)S(1)}, f32[8,512,1024]{2,1,0:T(8,128)}) fusion(f32[8,512,1024]{2,1,0:T(8,128)} %fusion.239, pred[512,1024]{1,0:T(8,128)(4,1)} %fusion.240), kind=kOutput, calls=%fused_computation.264.clone.1 | output fusion | flops 25166848 | bytes 34095104 | tf_op jit(solution)/shard_map/while/body/eval_jaxpr/sub | solution.py:85
  164.3 9.3 %fusion.242 = bf16[2,512,8,64]{1,3,2,0:T(8,128)(2,1)} fusion(bf16[2,512,8,64]{1,3,2,0:T(8,128)(2,1)} %get-tuple-element.810, s32[]{:T(128)S(6)} %copy.152, bf16[1024,8,64]{0,2,1:T(8,128)(2,1)S(1)} %get-tuple-element.827, f32[8,512,1024]{2,1,0:T(8,128)} %get-tuple-element.733, f32[8,512]{1,0:T(8,128)S(1)} %get-tuple-element.734), kind=kOutput, calls=%fused_computation.12.clone.1 | convolution fusion | flops 545259520 | bytes 18890756 | tf_op jit(solution)/shard_map/while/body/eval_jaxpr/hbk,khe->bhe/dot_general | solution.py:88
  181.6 9.9 %fusion.178 = (f32[1024]{0:T(1024)S(1)}, f32[1024,512]{0,1:T(8,128)}) fusion(f32[512]{0:T(512)S(1)} %bitcast.225, bf16[512,512]{1,0:T(8,128)(2,1)} %all_gather.24, bf16[512,512]{1,0:T(8,128)(2,1)} %all_gather.23, f32[1024,512]{0,1:T(8,128)} %copy-done.37, f32[512]{0:T(512)S(1)} %bitcast.222, f32[512]{0:T(512)S(1)} %bitcast.218, f32[512]{0:T(512)S(1)} %bitcast.207, ...), kind=kOutput, calls=%fused_computation.271 | convolution fusion | flops 1114635264 | bytes 5263360 | tf_op jit(solution)/shard_map/dot_general | solution.py:110
  226.9 85.2 %while.39 = (s32[]{:T(128)}, f32[1024,8,64]{0,2,1:T(8,128)}, f32[1024,8,64]{0,2,1:T(8,128)}, bf16[2,512,8,64]{1,3,2,0:T(8,128)(2,1)}, bf16[2,512,8,64]{1,3,2,0:T...) while((s32[]{:T(128)}, f32[1024,8,64]{0,2,1:T(8,128)}, ...), condition=%wide.region_22.23_spmd.clone, body=%wide.region_20.22_spmd.clone.sunk | while | flops 2727079936 | bytes 221357616 | solution.py:204
  233.5 11.3 %multiply_reduce_fusion.17 = (f32[8,512]{1,0:T(8,128)}, f32[8,512,1024]{2,1,0:T(8,128)}) fusion(f32[8,512,1024]{2,1,0:T(8,128)S(1)} %fusion.258, f32[8,512]{1,0:T(8,128)} %dynamic-slice_bitcast_fusion.2, bf16[1024,8,64]{0,2,1:T(8,128)(2,1)S(1)} %get-tuple-element.868, bf16[2,512,8,64]{1,3,2,0:T(8,128)(2,1)} %copy-done.4, s32[]{:T(128)S(6)} %copy.160, ...), kind=kOutput, calls=%fused_computation.41.clone.1 | convolution fusion | flops 557838336 | bytes 35684356 | tf_op jit(solution)/shard_map/while/body/eval_jaxpr/bhe,khe->hbk/dot_general | solution.py:183
  244.8 9.4 %multiply_convert_fusion.2 = bf16[8,512,1024]{2,1,0:T(8,128)(2,1)} fusion(f32[8,512,1024]{2,1,0:T(8,128)} %get-tuple-element.764, f32[8,512,1024]{2,1,0:T(8,128)S(1)} %fusion.258, f32[8,512]{1,0:T(8,128)} %get-tuple-element.765), kind=kLoop, calls=%fused_computation.40.clone.1 | loop fusion | flops 12582912 | bytes 41959424 | tf_op jit(solution)/shard_map/while/body/eval_jaxpr/convert_element_type | solution.py:190
  254.3 8.9 %bitcast_add_fusion.5 = f32[1024,8,64]{0,2,1:T(8,128)} fusion(f32[1024,8,64]{0,2,1:T(8,128)} %get-tuple-element.846, f32[8,512,1024]{2,1,0:T(8,128)} %get-tuple-element.764, pred[]{:T(512)S(6)} %compare.3, bf16[2,512,8,64]{1,3,2,0:T(8,128)(2,1)S(1)} %copy-done.8, s32[]{:T(128)S(6)} %copy.160), kind=kOutput, calls=%fused_computation.45.clone.1 | convolution fusion | flops 542113792 | bytes 21495812 | tf_op jit(solution)/shard_map/while/body/eval_jaxpr/hbk,bhe->khe/dot_general | solution.py:186
  275.6 11.3 %multiply_reduce_fusion.17 = (f32[8,512]{1,0:T(8,128)}, f32[8,512,1024]{2,1,0:T(8,128)}) fusion(f32[8,512,1024]{2,1,0:T(8,128)S(1)} %fusion.258, f32[8,512]{1,0:T(8,128)} %dynamic-slice_bitcast_fusion.2, bf16[1024,8,64]{0,2,1:T(8,128)(2,1)S(1)} %get-tuple-element.868, bf16[2,512,8,64]{1,3,2,0:T(8,128)(2,1)} %copy-done.4, s32[]{:T(128)S(6)} %copy.160, ...), kind=kOutput, calls=%fused_computation.41.clone.1 | convolution fusion | flops 557838336 | bytes 35684356 | tf_op jit(solution)/shard_map/while/body/eval_jaxpr/bhe,khe->hbk/dot_general | solution.py:183
  287.0 9.4 %multiply_convert_fusion.2 = bf16[8,512,1024]{2,1,0:T(8,128)(2,1)} fusion(f32[8,512,1024]{2,1,0:T(8,128)} %get-tuple-element.764, f32[8,512,1024]{2,1,0:T(8,128)S(1)} %fusion.258, f32[8,512]{1,0:T(8,128)} %get-tuple-element.765), kind=kLoop, calls=%fused_computation.40.clone.1 | loop fusion | flops 12582912 | bytes 41959424 | tf_op jit(solution)/shard_map/while/body/eval_jaxpr/convert_element_type | solution.py:190
  296.4 9.5 %bitcast_add_fusion.5 = f32[1024,8,64]{0,2,1:T(8,128)} fusion(f32[1024,8,64]{0,2,1:T(8,128)} %get-tuple-element.846, f32[8,512,1024]{2,1,0:T(8,128)} %get-tuple-element.764, pred[]{:T(512)S(6)} %compare.3, bf16[2,512,8,64]{1,3,2,0:T(8,128)(2,1)S(1)} %copy-done.8, s32[]{:T(128)S(6)} %copy.160), kind=kOutput, calls=%fused_computation.45.clone.1 | convolution fusion | flops 542113792 | bytes 21495812 | tf_op jit(solution)/shard_map/while/body/eval_jaxpr/hbk,bhe->khe/dot_general | solution.py:186
  350.1 13.6 %reduce-scatter.14.cloned.1.call-done = bf16[128,512]{1,0:T(8,128)(2,1)} async-done(((bf16[512,512]{1,0:T(8,128)(2,1)}), bf16[128,512]{1,0:T(8,128)(2,1)}) %reduce-scatter.14.cloned.1.call-update) | async-done | bytes 131088 | tf_op jit(solution)/shard_map/reduce_scatter | solution.py:300
  363.7 24.6 %reduce-scatter.10.cloned.1.call-done = bf16[128,512]{1,0:T(8,128)(2,1)} async-done(((bf16[512,512]{1,0:T(8,128)(2,1)}), bf16[128,512]{1,0:T(8,128)(2,1)}) %reduce-scatter.10.cloned.1.call-update) | async-done | bytes 131088 | tf_op jit(solution)/shard_map/reduce_scatter | solution.py:294
  388.3 24.8 %reduce-scatter.12.cloned.1.call-done = bf16[128,512]{1,0:T(8,128)(2,1)} async-done(((bf16[512,512]{1,0:T(8,128)(2,1)}), bf16[128,512]{1,0:T(8,128)(2,1)}) %reduce-scatter.12.cloned.1.call-update) | async-done | bytes 131088 | tf_op jit(solution)/shard_map/reduce_scatter | solution.py:297
  413.1 30.6 %reduce-scatter.16.cloned.1.call-done = bf16[128,1536]{1,0:T(8,128)(2,1)} async-done(((bf16[512,1536]{1,0:T(8,128)(2,1)}), bf16[128,1536]{1,0:T(8,128)(2,1)}) %reduce-scatter.16.cloned.1.call-update) | async-done | bytes 393232
  445.6 83.5 %all-reduce.2 = (f32[128,1536]{0,1:T(8,128)}, f32[128,512]{1,0:T(8,128)}, f32[128,512]{1,0:T(8,128)}, f32[128,512]{1,0:T(8,128)}, f32[9,128]{1,0:T(8,128)S(1)}) all-reduce(bf16[128,1536]{0,1:T(8,128)(2,1)} %copy.129, bf16[128,512]{1,0:T(8,128)(2,1)} %reduce-scatter.10.cloned.1.call-done, ...), channel_id=1, replica_groups=mesh['wide'=8,'narrow'=4] {'wide'}, use_global_device_ids=true, to_apply=%region_24.25 | all-reduce | flops 394368 | bytes 2366208 | tf_op jit(solution)/shard_map/psum | solution.py:307
  (349 shorter events, 196.3 us)
Async XLA Ops:
  7.2 43.2 %all-gather.2.cloned.1.call-start = ((), (), s32[]{:S(2)}) async-start(), calls=%async_computation.5 | async-start | bytes 1966080 | tf_op jit(solution)/shard_map/all_gather | solution.py:272
  9.2 340.1 %reduce-scatter.18.cloned.1.call-start = ((), (), s32[]{:S(2)}) async-start(), calls=%async_computation.10 | async-start | bytes 163840
  12.6 11.1 %copy-start.80 = (s32[1,1024]{1,0:T(1,128)S(1)}, s32[1,1024]{1,0:T(1,128)}, u32[]{:S(2)}) copy-start(s32[1,1024]{1,0:T(1,128)} %param.30) | copy-start | bytes 12292
  12.6 11.1 %copy-start.81 = (s32[1,1024]{1,0:T(1,128)S(1)}, s32[1,1024]{1,0:T(1,128)}, u32[]{:S(2)}) copy-start(s32[1,1024]{1,0:T(1,128)} %param.29) | copy-start | bytes 12292
  14.5 35.9 %copy-start.50 = (bf16[1024,512]{1,0:T(8,128)(2,1)S(1)}, bf16[1024,512]{1,0:T(8,128)(2,1)}, u32[]{:S(2)}) copy-start(bf16[1024,512]{1,0:T(8,128)(2,1)} %param.26) | copy-start | bytes 3145732
  195.6 18.9 %copy-start.9 = (f32[1024,512]{0,1:T(8,128)}, f32[1024,512]{0,1:T(8,128)S(1)}, u32[]{:S(2)}) copy-start(f32[1024,512]{0,1:T(8,128)S(1)} %get-tuple-element.533) | copy-start | bytes 6291460
  195.6 18.9 %copy-start.61 = (f32[1024]{0:T(1024)}, f32[1024]{0:T(1024)S(1)}, u32[]{:S(2)}) copy-start(f32[1024]{0:T(1024)S(1)} %broadcast_multiply_fusion.5) | copy-start | bytes 12292
  197.0 17.5 %copy-start.63 = (f32[1024]{0:T(1024)}, f32[1024]{0:T(1024)S(1)}, u32[]{:S(2)}) copy-start(f32[1024]{0:T(1024)S(1)} %add_rsqrt_fusion.1) | copy-start | bytes 12292
  197.0 6.3 %copy-start.52 = (bf16[512,512]{1,0:T(8,128)(2,1)S(1)}, bf16[512,512]{1,0:T(8,128)(2,1)}, u32[]{:S(2)}) copy-start(bf16[512,512]{1,0:T(8,128)(2,1)} %all_gather.24) | copy-start | bytes 1572868
  244.8 9.4 %copy-start.8 = (bf16[2,512,8,64]{1,3,2,0:T(8,128)(2,1)S(1)}, bf16[2,512,8,64]{1,3,2,0:T(8,128)(2,1)}, u32[]{:S(2)}) copy-start(bf16[2,512,8,64]{1,3,2,0:T(8,128)(2,1)} %get-tuple-element.870) | copy-start | bytes 3145732 | tf_op jit(solution)/shard_map/while
  254.3 8.9 %copy-start = (bf16[8,512,1024]{2,1,0:T(8,128)(2,1)S(1)}, bf16[8,512,1024]{2,1,0:T(8,128)(2,1)}, u32[]{:S(2)}) copy-start(bf16[8,512,1024]{2,1,0:T(8,128)(2,1)} %multiply_convert_fusion.2) | copy-start | bytes 25165828 | tf_op jit(solution)/shard_map/while
  254.3 8.9 %copy-start.24 = (bf16[2,512,8,64]{1,3,2,0:T(8,128)(2,1)S(1)}, bf16[2,512,8,64]{1,3,2,0:T(8,128)(2,1)}, u32[]{:S(2)}) copy-start(bf16[2,512,8,64]{1,3,2,0:T(8,128)(2,1)} %get-tuple-element.847) | copy-start | bytes 3145732 | tf_op jit(solution)/shard_map/while
  287.0 9.4 %copy-start.8 = (bf16[2,512,8,64]{1,3,2,0:T(8,128)(2,1)S(1)}, bf16[2,512,8,64]{1,3,2,0:T(8,128)(2,1)}, u32[]{:S(2)}) copy-start(bf16[2,512,8,64]{1,3,2,0:T(8,128)(2,1)} %get-tuple-element.870) | copy-start | bytes 3145732 | tf_op jit(solution)/shard_map/while
  296.4 9.5 %copy-start = (bf16[8,512,1024]{2,1,0:T(8,128)(2,1)S(1)}, bf16[8,512,1024]{2,1,0:T(8,128)(2,1)}, u32[]{:S(2)}) copy-start(bf16[8,512,1024]{2,1,0:T(8,128)(2,1)} %multiply_convert_fusion.2) | copy-start | bytes 25165828 | tf_op jit(solution)/shard_map/while
  296.4 9.5 %copy-start.24 = (bf16[2,512,8,64]{1,3,2,0:T(8,128)(2,1)S(1)}, bf16[2,512,8,64]{1,3,2,0:T(8,128)(2,1)}, u32[]{:S(2)}) copy-start(bf16[2,512,8,64]{1,3,2,0:T(8,128)(2,1)} %get-tuple-element.847) | copy-start | bytes 3145732 | tf_op jit(solution)/shard_map/while
  319.3 44.4 %reduce-scatter.14.cloned.1.call-start = ((), (), s32[]{:S(2)}) async-start(), calls=%async_computation.8 | async-start | bytes 655360 | tf_op jit(solution)/shard_map/reduce_scatter | solution.py:300
  322.4 65.9 %reduce-scatter.10.cloned.1.call-start = ((), (), s32[]{:S(2)}) async-start(), calls=%async_computation.6 | async-start | bytes 655360 | tf_op jit(solution)/shard_map/reduce_scatter | solution.py:294
  325.8 87.3 %reduce-scatter.12.cloned.1.call-start = ((), (), s32[]{:S(2)}) async-start(), calls=%async_computation.7 | async-start | bytes 655360 | tf_op jit(solution)/shard_map/reduce_scatter | solution.py:297
  328.8 114.9 %reduce-scatter.16.cloned.1.call-start = ((), (), s32[]{:S(2)}) async-start(), calls=%async_computation.9 | async-start | bytes 1966080
  334.1 7.1 %copy-start.12 = (f32[1024,512]{0,1:T(8,128)S(1)}, f32[1024,512]{0,1:T(8,128)}, u32[]{:S(2)}) copy-start(f32[1024,512]{0,1:T(8,128)} %copy-done.11) | copy-start | bytes 6291460
  349.2 190.5 %copy-start.29 = (bf16[1024,512]{0,1:T(8,128)(2,1)S(1)}, bf16[1024,512]{0,1:T(8,128)(2,1)}, u32[]{:S(2)}) copy-start(bf16[1024,512]{0,1:T(8,128)(2,1)} %get-tuple-element.531) | copy-start | bytes 3145732
  445.6 102.6 %copy-start.30 = (f32[128,1536]{0,1:T(8,128)S(1)}, f32[128,1536]{0,1:T(8,128)}, u32[]{:S(2)}) copy-start(f32[128,1536]{0,1:T(8,128)} %copy.116) | copy-start | bytes 2359300
  445.6 102.6 %copy-start.31 = (f32[128,1536]{0,1:T(8,128)S(1)}, f32[128,1536]{0,1:T(8,128)}, u32[]{:S(2)}) copy-start(f32[128,1536]{0,1:T(8,128)} %copy.113) | copy-start | bytes 2359300
  445.6 102.6 %copy-start.32 = (f32[128,1536]{0,1:T(8,128)S(1)}, f32[128,1536]{0,1:T(8,128)}, u32[]{:S(2)}) copy-start(f32[128,1536]{0,1:T(8,128)} %copy.114) | copy-start | bytes 2359300
  (83 other events, 201.0 us)
Sparse Core Ops, SparseCore 0:
  10.2 25.1 all-gather.1
  319.4 19.9 reduce-scatter.17
  342.0 21.6 reduce-scatter.13
  366.6 21.6 reduce-scatter.9
  391.4 21.6 reduce-scatter.11
  415.5 28.1 reduce-scatter.15
where the time goes:
time: 580 us; the launch traced here: 570 us
  matrix products  154 us (27%)
  blocking collectives  123 us (21%)
  other arithmetic  106 us (18%)
  waiting for transfers between devices  93.7 us (16%)
  local copies, waits for them, and re-layouts  72.2 us (12%)
  between operations  20.4 us (4%)
    psum x1, blocking collectives, body(): lax.psum((partial_sums[0], partial_sums[1], partial_sums[2], partial_sums...  83.5 us
    sub x2, other arithmetic, one_block(): expo = jnp.exp(scores - top)  43.4 us
    unnamed x166, local copies, waits for them, and re-layouts  40.2 us
    unnamed x8, waiting for transfers between devices  30.7 us
    dot_general x4, matrix products, one_block(): jnp.einsum('hbk,khe->bhe', prob, values, preferred_element_type=jnp.float32)  29.3 us
    reduce_scatter x1, waiting for transfers between devices, body(): lax.psum_scatter(grads[2].astype(jnp.bfloat16), 'narrow', scatter_dimensi...  24.8 us
    reduce_scatter x1, waiting for transfers between devices, body(): lax.psum_scatter(grads[1].astype(jnp.bfloat16), 'narrow', scatter_dimensi...  24.6 us
    dot_general x2, matrix products, back_block(): jnp.einsum('bhe,khe->hbk', q_block, keys, preferred_element_type=jnp.floa...  22.7 us
  transfers between devices with their start and end apart: 6, of which 4 were waited for; matrix products, arithmetic and copies ran while one was open for 7% of the time, Pallas kernels for 0%

commit v1 on v0

v1 whole, which is shorter than its diff:
```python
import functools
import math

import jax
import jax.numpy as jnp
from jax import lax
from jax.experimental import pallas as pl
from jax.experimental.pallas import tpu as pltpu
from jax.sharding import PartitionSpec as P

D = 512
HEADS = 8
HEAD_DIM = 64
PAIR = 2 * HEAD_DIM
PAIRS = HEADS // 2
TRIO = 3 * PAIR
TOK_DEV = 1024
QT = 256
HALF = TOK_DEV // 2
TILES = 1
MT = 512
STEP = 10
NORM_EPS = 1e-05
ADAM_EPS = 1e-08
MASKED = -1e30
BF = jnp.bfloat16
F32 = jnp.float32
MIB = 1024 * 1024
GROUP = 2
HW = GROUP * TRIO
FORWARD_MIB, MIDDLE_MIB, BACKWARD_MIB = 16, 20, 24

NN = (((1,), (0,)), ((), ()))
NT = (((1,), (1,)), ((), ()))
TN = (((0,), (0,)), ((), ()))
TT = (((0,), (1,)), ((), ()))


def dot(a, b, dims):
    return lax.dot_general(a, b, dims, preferred_element_type=F32)


def params(mib=20):
    return pltpu.CompilerParams(vmem_limit_bytes=mib * MIB)


def sds(shape, dtype):
    return jax.ShapeDtypeStruct(shape, dtype)


SMEM = pl.BlockSpec(memory_space=pltpu.SMEM)
VM = pl.BlockSpec(memory_space=pltpu.VMEM)
ANY = pl.BlockSpec(memory_space=pl.ANY)
HBM = pl.BlockSpec(memory_space=pltpu.HBM)


def whole(shape):
    return pl.BlockSpec(shape, lambda i: (0,) * len(shape))


def cost(flops, moved, exps=0):
    return pl.CostEstimate(flops=int(flops), bytes_accessed=int(moved), transcendentals=int(exps))


def fetch(pairs, sems):
    copies = [
        pltpu.make_async_copy(source, target, sems.at[number])
        for number, (source, target) in enumerate(pairs)
    ]
    for copy in copies:
        copy.start()
    return copies


def trio_columns(base):
    return [
        (local * TRIO + t * PAIR, t * D + (base + local) * PAIR)
        for local in range(GROUP)
        for t in range(3)
    ]


def pack_first_kernel(w_hbm, vec_hbm, out_ref, w_ref, vec_ref, sems):
    rows, vec_cols = w_hbm.shape[0], vec_hbm.shape[1]
    width = GROUP * PAIR
    copies = fetch(
        [(w_hbm.at[:, t * D : t * D + width], w_ref.at[t]) for t in range(3)] + [(vec_hbm, vec_ref)], sems
    )
    for copy in copies:
        copy.wait()
    for local in range(GROUP):
        for t in range(3):
            target = local * TRIO + t * PAIR
            out_ref[:rows, target : target + PAIR] = w_ref[t, :, local * PAIR : (local + 1) * PAIR].astype(BF)
    out_ref[rows:, :] = jnp.zeros((16, HW), BF)
    vec = jnp.concatenate([vec_ref[...], jnp.zeros((7, vec_cols), F32)], 0)
    out_ref[rows:, :vec_cols] = vec.astype(BF)


def pack_first(w_qkv, vectors):
    rows = w_qkv.shape[0]
    return pl.pallas_call(
        pack_first_kernel,
        in_specs=[HBM, HBM],
        out_specs=VM,
        out_shape=sds((rows + 16, HW), BF),
        scratch_shapes=[
            pltpu.VMEM((3, rows, GROUP * PAIR), F32),
            pltpu.VMEM(vectors.shape, F32),
            pltpu.SemaphoreType.DMA((4,)),
        ],
        compiler_params=params(60),
        name="pack_first",
    )(w_qkv, vectors)


def pack_second_kernel(w_ref, w_out_ref, w_up_ref, w_down_ref, *refs):
    second_ref, rest_ref = refs[-2:]
    for target, source in trio_columns(GROUP):
        second_ref[:, target : target + PAIR] = w_ref[:, source : source + PAIR].astype(BF)
    rest_ref[:, :D] = w_out_ref[...].astype(BF)
    rest_ref[:, D : 2 * D] = w_up_ref[...].astype(BF)
    rest_ref[:, 2 * D :] = w_down_ref[...].astype(BF)


def pick(piece, lead, rows):
    return piece[rows, :] if lead is None else piece[lead, rows, :]


def assemble(order, pieces, place, w_full):
    rows = D // len(order)
    for number, (piece, lead, mask) in enumerate(order):
        at = number if mask is None else jnp.bitwise_xor(place[0], mask)
        w_full[pl.ds(pl.multiple_of(at * rows, rows), rows), :] = pick(
            pieces[piece], lead, slice(0, rows)
        )


def turn_rows(source, start, write):
    blocks = source.shape[0] // 8
    whole_blocks, rest = start >> 3, start & 7
    inside = lax.broadcasted_iota(jnp.int32, (8, source.shape[1]), 0) < 8 - rest

    def rolled(block):
        at = pl.multiple_of(((block + whole_blocks) & (blocks - 1)) * 8, 8)
        return pltpu.roll(source[pl.ds(at, 8), :], (8 - rest) & 7, 0)

    def step(i, first):
        second, third = rolled(2 * i + 1), rolled(2 * i + 2)
        write(i, jnp.where(inside, first, second), jnp.where(inside, second, third))
        return third

    lax.fori_loop(0, blocks // 2, step, rolled(0), unroll=8)


def write_into(out):
    def write(i, upper, lower):
        at = pl.multiple_of(i * 16, 16)
        out[pl.ds(at, 16), :] = jnp.concatenate([upper, lower], 0).astype(out.dtype)

    return write


def turn_tokens_kernel(tokens, both, *refs):
    tokens_out, turned_out, cells_out, start_out, wide_tokens = refs[-5:]
    cell = both[0:1, :]
    start = jnp.int32(TOK_DEV)
    for c in range(4):
        size = jnp.sum((cell == c).astype(jnp.int32))
        first = jnp.sum((cell < c).astype(jnp.int32))
        start = jnp.where(size == HALF, jnp.minimum(start, first), start)
    start_out[0] = start
    shift = jnp.where(start == 0, 0, TOK_DEV - start)
    row = lax.broadcasted_iota(jnp.int32, (8, TOK_DEV), 0)
    cells_out[...] = pltpu.roll(jnp.where(row == 0, cell, both[1:2, :]), shift, 1)
    wide_tokens[...] = tokens[...].astype(F32)
    turn_rows(wide_tokens, start, write_into(tokens_out))
    turned_out[...] = tokens_out[...].T


def turn_tokens(tokens, both, later):
    return pl.pallas_call(
        turn_tokens_kernel,
        in_specs=[VM, VM] + [ANY] * len(later),
        out_specs=[VM] * 3 + [SMEM],
        out_shape=[
            sds((TOK_DEV, D), BF),
            sds((D, TOK_DEV), BF),
            sds((8, TOK_DEV), jnp.int32),
            sds((1,), jnp.int32),
        ],
        scratch_shapes=[pltpu.VMEM((TOK_DEV, D), F32)],
        compiler_params=params(16),
        cost_estimate=cost(1e7, 3e6),
        name="turn_tokens",
    )(tokens, both, *later)


def turn_cotangent_kernel(start, cot_ref, *refs):
    turn_rows(cot_ref, start[0], write_into(refs[-1]))


def turn_cotangent(start, cot, later):
    return pl.pallas_call(
        turn_cotangent_kernel,
        in_specs=[SMEM, VM] + [ANY] * len(later),
        out_specs=VM,
        out_shape=sds((TOK_DEV, D), F32),
        compiler_params=params(16),
        cost_estimate=cost(1e7, 4e6),
        name="turn_cotangent",
    )(start, cot, *later)


def turn_back_kernel(start, grad_ref, mixed_ref, *refs):
    grad_out, mixed_out, wide_mixed = refs[-3:]
    back = (TOK_DEV - start[0]) & (TOK_DEV - 1)
    wide_mixed[...] = mixed_ref[...].astype(F32)
    turn_rows(wide_mixed, back, write_into(mixed_out))
    turn_rows(grad_ref, back, write_into(grad_out))


def turn_back(start, grad, mixed, later):
    return pl.pallas_call(
        turn_back_kernel,
        in_specs=[SMEM, VM, VM] + [ANY] * len(later),
        out_specs=[VM, VM],
        out_shape=[sds(grad.shape, F32), sds(mixed.shape, BF)],
        scratch_shapes=[pltpu.VMEM(mixed.shape, F32)],
        compiler_params=params(),
        cost_estimate=cost(1, 1),
        name="turn_back",
    )(start, grad, mixed, *later)


def make_bias(cells_ref, bias):
    for half in range(2):
        mine = slice(half * HALF, (half + 1) * HALF)
        number = lax.broadcasted_iota(jnp.int32, (16, HALF), 0)
        of_key = jnp.where(cells_ref[1:2, mine] == number, 1.0, 0.0).astype(BF)
        of_query = jnp.where(cells_ref[0:1, mine] == number, 1.0, 0.0).astype(BF)
        keys = lax.broadcasted_iota(jnp.int32, (HALF, HALF), 0)
        queries = lax.broadcasted_iota(jnp.int32, (HALF, HALF), 1)
        seen = (dot(of_key, of_query, TN) > 0.5) | (keys == queries)
        bias[mine, :] = jnp.where(seen, 0.0, MASKED)


def column_of(row):
    eye = lax.broadcasted_iota(jnp.int32, (PAIR, PAIR), 0) == lax.broadcasted_iota(
        jnp.int32, (PAIR, PAIR), 1
    )
    return jnp.sum(jnp.where(eye, row, 0.0), 1, keepdims=True)


def both_heads(pair_t):
    zero = jnp.zeros((HEAD_DIM, pair_t.shape[1]), pair_t.dtype)
    return jnp.concatenate(
        [
            jnp.concatenate([pair_t[:HEAD_DIM], zero], 0),
            jnp.concatenate([zero, pair_t[HEAD_DIM:]], 0),
        ],
        1,
    )


def forward_kernel(order, n_pieces, base, *refs):
    place, tokens, cells_ref, vec_in = refs[:4]
    pieces = refs[4 : 4 + n_pieces]
    att_out, lse_out, krow_out, vrow_out, qt_out, kt_out, w_full, vec_full, bias = refs[4 + n_pieces :]
    assemble(order, pieces, place, w_full)
    if vec_in.shape[1] == D:
        vec_full[...] = vec_in[...].astype(F32)
    else:
        rows = D // len(order)
        for piece, lead, mask in order:
            at = pl.multiple_of(jnp.bitwise_xor(place[0], mask) * rows, rows)
            vec_full[:, pl.ds(at, rows)] = pick(pieces[piece], lead, slice(rows, rows + 16))[
                :, :rows
            ].astype(F32)
    make_bias(cells_ref, bias)
    x = tokens[...]
    halves = [slice(0, HALF), slice(HALF, TOK_DEV)]
    chains = []
    for local in range(GROUP):
        lane = slice((base + local) * PAIR, (base + local + 1) * PAIR)
        w = w_full[:, local * TRIO : (local + 1) * TRIO]
        b_q = vec_full[0:1, lane]
        b_v = vec_full[1:2, lane]
        trio = dot(w, x, TT)
        rows = dot(x, w[:, PAIR:], NN)
        here = slice(local * PAIR, (local + 1) * PAIR)
        q_t = ((trio[:PAIR] + column_of(b_q)) * (HEAD_DIM**-0.5)).astype(BF)
        v_t = (trio[2 * PAIR :] + column_of(b_v)).astype(BF)
        k_row = rows[:, :PAIR].astype(BF)
        krow_out[local] = k_row
        vrow_out[local] = (rows[:, PAIR:] + b_v).astype(BF)
        qt_out[here, :] = q_t
        kt_out[here, :] = trio[PAIR : 2 * PAIR].astype(BF)
        for mine in halves:
            chains.append((local, mine, v_t, dot(k_row[mine], both_heads(q_t[:, mine]), NN)))
    for local, mine, v_t, s in chains:
        mask = bias[mine, :]
        s = s + jnp.concatenate([mask, mask], 1)
        top = jnp.max(s, 0, keepdims=True)
        e = jnp.exp(s - top)
        total = jnp.sum(e, 0, keepdims=True)
        lse = top + jnp.log(total)
        e_low = e.astype(BF)
        for h in range(2):
            cols = slice(h * HALF, (h + 1) * HALF)
            head = slice(h * HEAD_DIM, (h + 1) * HEAD_DIM)
            o = dot(v_t[head, mine], e_low[:, cols], NN)
            at = local * PAIR + h * HEAD_DIM
            att_out[at : at + HEAD_DIM, mine] = (o / total[:, cols]).astype(BF)
            lse_out[local, h : h + 1, mine] = lse[:, cols]


def forward_attention(base, place, tokens, cells, vec, pieces, order):
    wide_t, tall = sds((GROUP * PAIR, TOK_DEV), BF), sds((GROUP, TOK_DEV, PAIR), BF)
    return pl.pallas_call(
        functools.partial(forward_kernel, order, len(pieces), base),
        in_specs=[SMEM] + [VM] * (3 + len(pieces)),
        out_specs=[VM] * 8,
        out_shape=[
            wide_t, sds((GROUP, 8, TOK_DEV), F32), tall, tall, wide_t, wide_t, sds((D, HW), BF), sds((16, D), F32)
        ],
        scratch_shapes=[pltpu.VMEM((TOK_DEV, HALF), F32)],
        compiler_params=params(FORWARD_MIB),
        cost_estimate=cost(6e9, 8e6, 2**21),
        name="forward_attention",
    )(place, tokens, cells, vec, *pieces)


def normalize(value):
    center = value - jnp.mean(value, -1, keepdims=True)
    inverse = lax.rsqrt(jnp.mean(center * center, -1, keepdims=True) + NORM_EPS)
    return center * inverse, inverse


def normalize_back(grad, normal, inverse):
    return inverse * (
        grad
        - jnp.mean(grad, -1, keepdims=True)
        - normal * jnp.mean(grad * normal, -1, keepdims=True)
    )


def column_sum(value):
    return jnp.sum(value, 0, keepdims=True)


def row_sources(place, n_shards, stages):
    if not stages:
        return [(0, 0, D)]
    rows = D // n_shards
    piece = D >> len(stages)
    found = []
    for block in range(1 << len(stages)):
        masks = {"narrow": 0, "wide": 0}
        for number, (axis, mask) in enumerate(stages):
            if block >> (len(stages) - 1 - number) & 1:
                masks[axis] |= mask
        source = jnp.bitwise_xor(place[0], masks["narrow"]) * rows
        if piece < rows:
            source = source + jnp.bitwise_xor(place[1], masks["wide"]) * piece
        found.append((block * piece, pl.multiple_of(source, piece), piece))
    return found


def store_rows(outs, place, n_shards, stages, matrix, cols):
    height = outs[0].shape[0]
    for target, source, rows in row_sources(place, n_shards, stages):
        out = outs[target // height]
        at = target % height
        out[at : at + rows, cols] = matrix[pl.ds(source, rows), :].astype(BF)


def gelu_parts(value):
    density = jnp.exp(-0.5 * value * value)
    t = 1.0 / (1.0 + (0.3275911 / math.sqrt(2.0)) * jnp.abs(value))
    poly = 1.061405429
    for factor in (-1.453152027, 1.421413741, -0.284496736, 0.254829592):
        poly = poly * t + factor
    tail = 0.5 * poly * t * density
    return jnp.where(value >= 0.0, 1.0 - tail, tail), value * density * (1.0 / math.sqrt(2.0 * math.pi))


def middle_kernel(order, n_pieces, n_shards, stages, *refs):
    n_g = 2 if stages else 1
    place, tokens, cot_ref, att_a, att_b, vec_ref = refs[:6]
    pieces = refs[6 : 6 + n_pieces]
    mixed_out, dh1_out, datt_out, vec_out = refs[6 + n_pieces : 10 + n_pieces]
    g_outs = refs[10 + n_pieces : 10 + n_pieces + n_g]
    w_full, att_all, first_all, hidden_all, branch_all, pre_all, down_all, dw, sums = refs[
        10 + n_pieces + n_g :
    ]
    step = pl.program_id(0)

    @pl.when(step == 0)
    def _():
        assemble(order, pieces, place, w_full)
        sums[...] = jnp.zeros_like(sums)

    w_out, w_up, w_down = w_full[:, :D], w_full[:, D : 2 * D], w_full[:, 2 * D :]

    def vec(row):
        return vec_ref[row : row + 1, :]

    def tile(number):
        at = pl.ds(pl.multiple_of(step * (TILES * MT) + number * MT, MT), MT)
        att_t = jnp.concatenate([att_a[:, at], att_b[:, at]], 0)
        att_all[:, at] = att_t
        branch = dot(att_t, w_out, TN)
        yield
        normal_1, inverse_1 = normalize(tokens[at, :].astype(F32) + (branch + vec(2)))
        first = normal_1 * vec(5) + vec(6)
        first_low = first.astype(BF)
        first_all[at, :] = first_low
        pre = dot(first_low, w_up, NN)
        yield
        pre = pre + vec(3)
        cdf, bump = gelu_parts(pre)
        hidden = (pre * cdf).astype(BF)
        hidden_all[at, :] = hidden
        slope = cdf + bump
        down = dot(hidden, w_down, NN)
        yield
        normal_2, inverse_2 = normalize(first + (down + vec(4)))
        mixed_out[at, :] = (normal_2 * vec(7) + vec(8)).astype(BF)
        cot = cot_ref[at, :]
        d_h2 = normalize_back(cot * vec(7), normal_2, inverse_2)
        d_down = d_h2.astype(BF)
        down_all[at, :] = d_down
        d_hidden = dot(d_down, w_down, NT)
        yield
        sums[7:8, :] += column_sum(cot * normal_2)
        sums[8:9, :] += column_sum(cot)
        d_pre = (d_hidden * slope).astype(BF)
        pre_all[at, :] = d_pre
        d_up = dot(d_pre, w_up, NT)
        yield
        d_first = d_h2 + d_up
        d_h1 = normalize_back(d_first * vec(5), normal_1, inverse_1)
        dh1_out[at, :] = d_h1
        d_branch = d_h1.astype(BF)
        branch_all[at, :] = d_branch
        datt_out[:, at] = dot(w_out, d_branch, NT).astype(BF)
        yield
        sums[5:6, :] += column_sum(d_first * normal_1)
        sums[6:7, :] += column_sum(d_first)

    tiles = [tile(number) for number in range(TILES)]
    while tiles:
        tiles = [one for one in tiles if next(one, True) is None]

    @pl.when(step == pl.num_programs(0) - 1)
    def _():
        ones = jnp.ones((16, TOK_DEV), BF)
        sums[2:3, :] = dot(ones, branch_all[...], NN)[:1]
        sums[3:4, :] = dot(ones, pre_all[...], NN)[:1]
        sums[4:5, :] = dot(ones, down_all[...], NN)[:1]
        vec_out[...] = sums[...]
        dw[0] = dot(att_all[...], branch_all[...], NN)
        dw[1] = dot(first_all[...], pre_all[...], TN)
        dw[2] = dot(hidden_all[...], down_all[...], TN)
        for number in range(3):
            store_rows(
                g_outs, place, n_shards, stages, dw.at[number], slice(number * D, (number + 1) * D)
            )


def middle(place, tokens, cot, atts, vec, pieces, order, stages):
    height = TILES * MT
    g_shapes = [(D // 2, 3 * D)] * 2 if stages else [(D, 3 * D)]
    return pl.pallas_call(
        functools.partial(middle_kernel, order, len(pieces), len(order), stages),
        grid=(TOK_DEV // height,),
        in_specs=[SMEM] + [VM] * (5 + len(pieces)),
        out_specs=[VM] * (4 + len(g_shapes)),
        out_shape=[
            sds((TOK_DEV, D), BF),
            sds((TOK_DEV, D), F32),
            sds((D, TOK_DEV), BF),
            sds((16, D), F32),
        ]
        + [sds(shape, BF) for shape in g_shapes],
        scratch_shapes=[pltpu.VMEM((D, 3 * D), BF), pltpu.VMEM((D, TOK_DEV), BF)]
        + [pltpu.VMEM((TOK_DEV, D), BF)] * 5
        + [pltpu.VMEM((3, D, D), F32), pltpu.VMEM((16, D), F32)],
        compiler_params=params(MIDDLE_MIB),
        cost_estimate=cost(1e10, 1.2e7, 2**20),
        name="middle",
    )(place, tokens, cot, *atts, vec, *pieces)


def backward_kernel(n_shards, stages, base, n_before, place, cells_ref, tokens_t, vec_ref, att_ref, lse_ref,
                    krow_ref, vrow_ref, qt_ref, kt_ref, datt_ref, *refs):
    before = refs[:n_before]
    bias, dw = refs[-2:]
    n_g = 2 if stages else 1
    d_out, vec = refs[-4 - n_g : -2 - n_g]
    g_outs = refs[-2 - n_g : -2]
    make_bias(cells_ref, bias)
    vec[...] = vec_ref[...]
    halves = [slice(0, HALF), slice(HALF, TOK_DEV)]
    chains = []
    for local in range(GROUP):
        here = slice(local * PAIR, (local + 1) * PAIR)
        q_t, k_t = qt_ref[here, :], kt_ref[here, :]
        d_t = datt_ref[(base + local) * PAIR : (base + local + 1) * PAIR, :]
        k_row, v_row = krow_ref[local], vrow_ref[local]
        product = d_t.astype(F32) * att_ref[here, :].astype(F32)
        for mine in halves:
            s = dot(k_row[mine], both_heads(q_t[:, mine]), NN)
            d_prob = dot(v_row[mine], both_heads(d_t[:, mine]), NN)
            chains.append((local, mine, q_t, k_t, d_t, product, s, d_prob))
    for local, mine, q_t, k_t, d_t, product, s, d_prob in chains:
        mask = bias[mine, :]
        lse = jnp.concatenate([lse_ref[local, 0:1, mine], lse_ref[local, 1:2, mine]], 1)
        delta = jnp.concatenate(
            [column_sum(product[:HEAD_DIM, mine]), column_sum(product[HEAD_DIM:, mine])], 1
        )
        prob = jnp.exp(s + jnp.concatenate([mask, mask], 1) - lse)
        d_s = (prob * (d_prob - delta)).astype(BF)
        prob_low = prob.astype(BF)
        for h in range(2):
            cols = slice(h * HALF, (h + 1) * HALF)
            head = slice(h * HEAD_DIM, (h + 1) * HEAD_DIM)
            d_q = dot(k_t[head, mine], d_s[:, cols], NN) * (HEAD_DIM**-0.5)
            d_k = dot(q_t[head, mine], d_s[:, cols], NT)
            d_v = dot(d_t[head, mine], prob_low[:, cols], NT)
            for t, value in enumerate((d_q, d_k, d_v)):
                at = t * PAIR + h * HEAD_DIM
                d_out[local, at : at + HEAD_DIM, mine] = value.astype(BF)
    ones = jnp.ones((16, TOK_DEV), BF)
    for out, ref in zip(g_outs, before):
        out[:, : ref.shape[1]] = ref[...]
    first = before[0].shape[1] if before else 0
    for local in range(GROUP):
        pair = base + local
        trio = d_out[local]
        dw[local] = dot(tokens_t[...], trio, NT)
        at = first + local * TRIO
        store_rows(g_outs, place, n_shards, stages, dw.at[local], slice(at, at + TRIO))
        total = dot(ones, trio, NT)
        lanes = slice(pair * PAIR, (pair + 1) * PAIR)
        vec[0:1, lanes] = total[:1, :PAIR]
        vec[1:2, lanes] = total[:1, 2 * PAIR :]
    if stages and base + GROUP == PAIRS:
        height = g_outs[0].shape[0]
        rows = D // n_shards
        for target, source, count in row_sources(place, n_shards, stages):
            at = pl.multiple_of(source // rows * rows, rows)
            g_outs[target // height][target % height : target % height + count, HW:] = vec[
                :, pl.ds(at, rows)
            ].astype(BF)


def backward_attention(base, place, cells, tokens_t, vec_sums, saved, d_t, before, n_shards, stages, later):
    width = HW + (before[0].shape[1] if before else 0)
    if stages:
        width += PAIR if base + GROUP == PAIRS else 0
        shapes = [sds((D // 2, width), BF)] * 2
    else:
        shapes = [sds((D, width), BF)]
    return pl.pallas_call(
        functools.partial(backward_kernel, n_shards, stages, base, len(before)),
        in_specs=[SMEM] + [VM] * (10 + len(before)) + [ANY] * len(later),
        out_specs=[VM] * (2 + len(shapes)),
        out_shape=[sds((GROUP, TRIO, TOK_DEV), BF), sds((16, D), F32)] + shapes,
        scratch_shapes=[pltpu.VMEM((TOK_DEV, HALF), F32), pltpu.VMEM((GROUP, D, TRIO), F32)],
        compiler_params=params(BACKWARD_MIB),
        cost_estimate=cost(1e10, 8e6, 2**21),
        name="backward_attention",
    )(place, cells, tokens_t, vec_sums, *saved, d_t, *before, *later)


def input_grad_kernel(w_a, w_b, dh1_ref, trio_a, trio_b, *refs):
    out = refs[-1]
    for part in range(TOK_DEV // QT):
        here = slice(part * QT, (part + 1) * QT)
        total = None
        for w_ref, trio in ((w_a, trio_a), (w_b, trio_b)):
            term = dot(w_ref[...], jnp.concatenate([trio[0, :, here], trio[1, :, here]], 0), NN)
            total = term if total is None else total + term
        out[here, :] = dh1_ref[here, :] + total.T


def input_gradient(weights, d_h1, trios, later):
    return pl.pallas_call(
        input_grad_kernel,
        in_specs=[VM] * 5 + [ANY] * len(later),
        out_specs=VM,
        out_shape=sds((TOK_DEV, D), F32),
        compiler_params=params(24),
        cost_estimate=cost(1, 1),
        name="input_gradient",
    )(*weights, d_h1, *trios, *later)


def adam(weight, grad, first, second, rate, decay):
    first = 0.5 * first + 0.5 * grad
    second = 0.5 * second + 0.5 * grad * grad
    fix = 1.0 - 0.5**STEP
    update = first * (1.0 / fix) / (jnp.sqrt(second * (1.0 / fix)) + ADAM_EPS)
    return weight - rate * (update + decay * weight), first, second


def pair_parts(first, base):
    return [
        (slice(first + target, first + target + PAIR), 0, source) for target, source in trio_columns(base)
    ]


EARLY_PARTS = [(slice(i * D, (i + 1) * D), i + 1, 0) for i in range(3)] + pair_parts(3 * D, 0)
LATE_PARTS = pair_parts(0, GROUP)


def adam_kernel(quick, limit, place, square_ref, *refs):
    n_grads = 4 if quick else 2
    grads = refs[:n_grads]
    vec_ref = refs[n_grads]
    states = refs[n_grads + 1 : n_grads + 16]
    outs = refs[n_grads + 16 : n_grads + 36]
    norm_out = refs[-1]
    step = pl.program_id(0)
    norm = jnp.sqrt(square_ref[0:1, 0:1])
    factor = limit / jnp.maximum(norm, limit)

    def write(number, where, grad, rate, decay):
        new, first, second = adam(
            states[number][where], grad * factor, states[5 + number][where],
            states[10 + number][where], rate, decay,
        )
        outs[number][where] = new
        outs[5 + number][where] = first
        outs[10 + number][where] = second
        outs[15 + number][where] = new.astype(BF)

    height = states[0].shape[0]
    pieces = height // 16 if quick else 1
    rows = height // pieces
    for piece in range(pieces):
        if quick:
            mask = jnp.bitwise_xor(place[1], step * pieces + piece)
            at = pl.multiple_of(((mask >> 2) & 1) * 16 + ((mask >> 1) & 1) * 32, 16)
            odd = (mask & 1) == 1
        else:
            at = pl.multiple_of(step * rows, rows)
        for group, parts in enumerate((EARLY_PARTS, LATE_PARTS)):
            for cols, number, target in parts:
                if quick:
                    low, high = grads[2 * group], grads[2 * group + 1]
                    grad = jnp.where(odd, high[pl.ds(at, rows), cols], low[pl.ds(at, rows), cols])
                else:
                    grad = grads[group][pl.ds(at, rows), cols]
                where = (
                    slice(piece * rows, (piece + 1) * rows),
                    slice(target, target + cols.stop - cols.start),
                )
                write(number, where, grad.astype(F32), 0.1, 0.01)

    @pl.when(step == 0)
    def _():
        norm_out[0, 0] = norm[0, 0]
        vec_cols = states[4].shape[1]
        write(4, (slice(0, 9), slice(0, vec_cols)), vec_ref[0:9, :vec_cols].astype(F32), 0.5, 0.0)


def adam_step(place, squares, limit, grads, vec_grad, weights, firsts, seconds, quick):
    steps = 4

    def spec(value):
        if value.shape[0] == 9:
            return whole(value.shape)
        return pl.BlockSpec((value.shape[0] // steps, value.shape[1]), lambda i: (i, 0))

    state = [spec(w) for w in weights]
    shapes = [sds(w.shape, F32) for w in weights]
    return pl.pallas_call(
        functools.partial(adam_kernel, quick, limit),
        grid=(steps,),
        in_specs=[SMEM] + [VM] * (2 + len(grads)) + state * 3,
        out_specs=state * 4 + [SMEM],
        out_shape=shapes * 3 + [sds(w.shape, BF) for w in weights] + [sds((1, 1), F32)],
        compiler_params=params(),
        name="adam",
    )(place, squares, *grads, vec_grad, *weights, *firsts, *seconds)


def swap(value, axis, mask):
    size = lax.axis_size(axis)
    return lax.ppermute(value, axis, [(i, i ^ mask) for i in range(size)])


def add_low(a, b):
    return (a.astype(F32) + b.astype(F32)).astype(BF)


def after(value, *others):
    return lax.optimization_barrier((value, others))[0]


def fold(keep, arrived):
    rows = keep.shape[0] // 2
    send = add_low(keep[rows:], arrived[rows:])
    return add_low(keep[:rows], arrived[:rows]), send


def finish_kernel(place, early_ref, keep, arrived, piece_out, vec_out, square_out):
    late = add_low(keep[:, :HW], arrived[:, :HW])
    vec = keep[:, HW:].astype(F32) + arrived[:, HW:].astype(F32)
    piece_out[...] = late
    vec_out[...] = vec
    early, late = early_ref[...].astype(F32), late.astype(F32)
    total = jnp.sum(early * early) + jnp.sum(late * late)
    total = total + jnp.where(place[1] == 0, jnp.sum(vec * vec), 0.0)
    square_out[...] = jnp.full(square_out.shape, total, F32)


def finish(place, early, keep, arrived):
    return pl.pallas_call(
        finish_kernel,
        in_specs=[SMEM] + [VM] * 3,
        out_specs=[VM] * 3,
        out_shape=[sds((16, HW), BF), sds((16, PAIR), F32), sds((8, PAIR), F32)],
        compiler_params=params(),
        name="finish",
    )(place, early, keep, arrived)


def directly(value, axis, masks):
    return [swap(value, axis, mask) for mask in masks]


def four(value, others):
    return (value + others[0]) + (others[1] + others[2])


def join(held, arrived):
    return jnp.concatenate([held, arrived], 0)


def squares_of(value):
    value = value.astype(F32)
    return jnp.sum(value * value)


STAGES = (("narrow", 1), ("narrow", 2), ("wide", 1), ("wide", 2), ("wide", 4))


def body(
    tokens, cotangent, cells, present, generate,
    w_qkv, w_out, w_up, w_down, vectors,
    m_qkv, m_out, m_up, m_down, m_vec,
    v_qkv, v_out, v_up, v_down, v_vec,
):
    narrow, wide = lax.axis_size("narrow"), lax.axis_size("wide")
    quick = narrow == 4 and wide == 8
    stages = STAGES if quick else ()
    place = jnp.stack([lax.axis_index("narrow"), lax.axis_index("wide")]).astype(jnp.int32)
    shard = w_qkv.shape[0]

    low_a = pack_first(w_qkv, vectors)
    keys = jnp.where((present == 1) & (generate == 0), cells, -1)
    tokens, tokens_t, cells, start = turn_tokens(
        tokens, after(jnp.concatenate([cells, keys], 0), low_a), []
    )
    low_b, low_rest = pl.pallas_call(
        pack_second_kernel,
        in_specs=[VM] * 4 + [ANY],
        out_specs=[VM, VM],
        out_shape=[sds((shard, HW), BF), sds((shard, 3 * D), BF)],
        compiler_params=params(),
        name="pack_second",
    )(w_qkv, w_out, w_up, w_down, cells)
    if quick:
        y_a = after(swap(low_a, "narrow", 2), (tokens, low_b))
        pieces_a = [low_a, swap(low_a, "narrow", 1), y_a, swap(y_a, "narrow", 1)]
        y_b = swap(after(low_b, y_a), "narrow", 2)
        c_b = swap(low_b, "narrow", 1)
        order = [(j, None, j) for j in range(4)]
        vec = jnp.zeros((8, PAIR), BF)
    else:
        pieces_a, pieces_b = [lax.all_gather(low_a, "narrow")], [lax.all_gather(low_b, "narrow")]
        pieces_rest = [lax.all_gather(low_rest, "narrow")]
        order = [(0, j, None) for j in range(narrow)]
        vec = lax.all_gather(vectors.astype(BF), "narrow", axis=1, tiled=True)
        vec = jnp.pad(vec, ((0, 7), (0, 0)))

    *saved_a, w_a, vec_full = forward_attention(0, place, tokens, cells, vec, pieces_a, order)
    if quick:
        y_b, c_b = after(y_b, saved_a), after(c_b, saved_a)
        pieces_b = [low_b, c_b, y_b, swap(y_b, "narrow", 1)]
        y_rest = swap(after(low_rest, y_b), "narrow", 2)
        c_rest = swap(low_rest, "narrow", 1)
    *saved_b, w_b, vec_full = forward_attention(GROUP, place, tokens, cells, vec_full, pieces_b, order)
    cotangent = turn_cotangent(start, cotangent, [saved_b[0]])
    if quick:
        y_rest, c_rest = after(y_rest, (saved_b, cotangent)), after(c_rest, saved_b)
        pieces_rest = [low_rest, c_rest, y_rest, swap(y_rest, "narrow", 1)]
    mixed, d_h1, d_t, vec_sums, *g_rest = middle(
        place, tokens, cotangent, (saved_a[0], saved_b[0]), vec_full, pieces_rest, order, stages
    )
    trio_a, vec_sums, *early = backward_attention(
        0, place, cells, tokens_t, vec_sums, saved_a, d_t, g_rest, narrow, stages, []
    )
    later = []
    if quick:
        e_keep, e_send = early
        e_keep, e_send = fold(e_keep, swap(e_send, "narrow", 1))
        e_arrived = swap(e_send, "narrow", 2)
        later = [e_send]
    trio_b, vec_sums, *late = backward_attention(
        GROUP, place, cells, tokens_t, vec_sums, saved_b, d_t, [], narrow, stages, later
    )
    weights, trios = (w_a, w_b), (trio_a, trio_b)

    if quick:
        b_keep, b_send = late
        b_arrived = swap(b_send, "narrow", 1)
        e_keep, e_send = fold(e_keep, after(e_arrived, trio_b))
        e_arrived = swap(e_send, "wide", 1)
        b_keep, b_send = fold(b_keep, after(b_arrived, e_send))
        b_arrived = swap(b_send, "narrow", 2)
        turned_grad = input_gradient(weights, d_h1, trios, [b_send])
        input_grad, mixed = turn_back(start, turned_grad, mixed, [])
        b_keep, b_send = fold(b_keep, after(b_arrived, input_grad))
        b_arrived = swap(b_send, "wide", 1)
        e_keep, e_send = fold(e_keep, after(e_arrived, b_send))
        e_arrived = swap(e_send, "wide", 2)
        b_keep, b_send = fold(b_keep, after(b_arrived, e_send))
        b_arrived = swap(b_send, "wide", 2)
        e_keep, e_send = fold(e_keep, after(e_arrived, b_send))
        e_arrived = swap(e_send, "wide", 4)
        b_keep, b_send = fold(b_keep, after(b_arrived, e_send))
        b_arrived = swap(b_send, "wide", 4)
        e_low = add_low(e_keep, after(e_arrived, b_send))
        e_arrived = swap(e_low, "wide", 4)
        b_low, vec_total, squares = finish(place, e_low, b_keep, b_arrived)
        b_arrived = swap(b_low, "wide", 4)
        squares = four(squares, directly(squares, "narrow", (1, 2, 3)))
        e_low = join(e_low, after(e_arrived, squares))
        e_arrived, square = swap(e_low, "wide", 2), swap(squares, "wide", 1)
        b_low = join(b_low, after(b_arrived, e_low))
        b_arrived = swap(b_low, "wide", 2)
        squares = squares + after(square, b_low)
        e_low = join(e_low, after(e_arrived, squares))
        e_arrived, others = swap(e_low, "wide", 1), directly(squares, "wide", (2, 4, 6))
        b_low = join(b_low, after(b_arrived, e_low))
        b_arrived = swap(b_low, "wide", 1)
        squares = four(squares, after(others, b_low))
        grads = [e_low, after(e_arrived, squares), b_low, after(b_arrived, squares)]
    else:
        turned_grad = input_gradient(weights, d_h1, trios, [])
        input_grad, mixed = turn_back(start, turned_grad, mixed, [])
        vec_total = lax.psum_scatter(vec_sums, "narrow", scatter_dimension=1, tiled=True)
        vec_total = lax.psum(vec_total, "wide")
        grads = []
        for every in (early[0], late[0]):
            total = lax.psum_scatter(every, "narrow", scatter_dimension=0, tiled=True)
            grads.append(lax.psum(total.astype(F32), "wide"))
        squares = lax.psum(sum(squares_of(v) for v in grads + [vec_total]), "narrow")
        squares = jnp.full((8, PAIR), squares, F32)
    *updated, grad_norm = adam_step(
        place, squares, math.sqrt(TOK_DEV * wide * narrow), grads, vec_total,
        (w_qkv, w_out, w_up, w_down, vectors),
        (m_qkv, m_out, m_up, m_down, m_vec),
        (v_qkv, v_out, v_up, v_down, v_vec),
        quick,
    )
    return (mixed, input_grad, grad_norm[0, 0], *updated)


def solution(mesh):
    split = P(("wide", "narrow"), None)
    state = (P("narrow", None),) * 4 + (P(None, "narrow"),)
    return jax.shard_map(
        body,
        mesh=mesh,
        in_specs=(split,) * 5 + state * 3,
        out_specs=(split, split, P()) + state * 4,
        check_vma=False,
    )
```

time: 580 us -> 129 us (0.22); the launches traced: 570 us -> 128 us
  matrix products: 154 us -> 0 us
  blocking collectives: 123 us -> 0 us
  other arithmetic: 106 us -> 2.31 us
  local copies, waits for them, and re-layouts: 72.2 us -> 3.5 us
  waiting for transfers between devices: 93.7 us -> 28.7 us
  Pallas kernels: 0 us -> 55.9 us
  starting transfers between devices: 0.25 us -> 36.8 us
  between operations: 20.4 us -> 1.26 us
    dot_general x32 -> x0, matrix products: 154 us -> none  [the longest x4 29.3 us: one_block(): jnp.einsum('hbk,khe->bhe', prob, values, preferred_element_type=jnp.float32)]
    psum x2 -> x0, blocking collectives: 89.9 us -> none  [the longest x1 83.5 us: body(): lax.psum((partial_sums[0], partial_sums[1], partial_sums[2], partial_sums...]
    reduce_scatter x3 -> x0, waiting for transfers between devices: 63 us -> none  [the longest x1 24.8 us: body(): lax.psum_scatter(grads[2].astype(jnp.bfloat16), 'narrow', scatter_dimensi...]
    pallas_call x0 -> x13, Pallas kernels: none -> 55.9 us  [the longest x2 17.1 us: backward_attention(): pl.pallas_call(functools.partial(backward_kernel, n_shards, stages, base,...]
    sub x2 -> x0, other arithmetic: 43.4 us -> none  [one_block(): expo = jnp.exp(scores - top)]
    ppermute x0 -> x32, starting transfers between devices: none -> 36.8 us  [swap(): return lax.ppermute(value, axis, [(i, i ^ mask) for i in range(size)])]
    unnamed x166 -> x44, local copies, waits for them, and re-layouts: 40.2 us -> 3.49 us
    all_gather x4 -> x0, blocking collectives: 32.8 us -> none  [the longest x1 11.2 us: body(): lax.all_gather(shards[3], 'narrow', axis=0, tiled=True)]
  transfers between devices with their start and end apart: 6 -> 32, of which waited for: 4 -> 14; matrix products, arithmetic and copies ran while one was open for 7% -> 2% of each run, Pallas kernels for 0% -> 23%
where the time goes in v1:
time: 129 us; the launch traced here: 128 us
  Pallas kernels  55.9 us (43%)
  starting transfers between devices  36.8 us (29%)
  waiting for transfers between devices  28.7 us (22%)
  local copies, waits for them, and re-layouts  3.5 us (3%)
  other arithmetic  2.31 us (2%)
    ppermute x32, starting transfers between devices, swap(): return lax.ppermute(value, axis, [(i, i ^ mask) for i in range(size)])  36.8 us
    ppermute x32, waiting for transfers between devices, swap(): return lax.ppermute(value, axis, [(i, i ^ mask) for i in range(size)])  28.7 us
    pallas_call x2, Pallas kernels, backward_attention(): pl.pallas_call(functools.partial(backward_kernel, n_shards, stages, base,...  17.1 us
    pallas_call x2, Pallas kernels, forward_attention(): pl.pallas_call(functools.partial(forward_kernel, order, len(pieces), base...  12.2 us
    pallas_call x1, Pallas kernels, middle(): pl.pallas_call(functools.partial(middle_kernel, order, len(pieces), len(o...  11.4 us
    pallas_call x1, Pallas kernels, adam_step(): pl.pallas_call(functools.partial(adam_kernel, quick, limit), grid=(steps,...  4.2 us
    unnamed x44, local copies, waits for them, and re-layouts  3.49 us
    pallas_call x1, Pallas kernels, turn_back(): pl.pallas_call(turn_back_kernel, in_specs=[SMEM, VM, VM] + [ANY] * len(la...  3.23 us
  transfers between devices with their start and end apart: 32, of which 14 were waited for; matrix products, arithmetic and copies ran while one was open for 2% of the time, Pallas kernels for 23%

profile of v1, /device:TPU:0, one launch (start us, length us, event | category | flops | bytes accessed | tf_op | source)
XLA Modules:
  0.0 128.4 jit_solution(11513169373974107439)
XLA Ops:
  0.7 1.9 %pack_first.1.refs_4_ = bf16[144,768]{1,0:T(8,128)(2,1)} custom-call(f32[128,1536]{1,0:T(8,128)} %refs_5_.1, f32[9,128]{1,0:T(8,128)} %refs_9_.1), custom_call_target="tpu_custom_call" | custom-call | tf_op jit(solution)/shard_map/pack_first/pallas_call | solution.py:102
  2.6 3.0 %collective-permute-start.1 = (bf16[144,768]{1,0:T(8,128)(2,1)}, bf16[144,768]{1,0:T(8,128)(2,1)S(1)}, u32[]{:S(2)}, u32[]{:S(2)}) collective-permute-start(bf16[144,768]{1,0:T(8,128)(2,1)} %pack_first.1.refs_4_), channel_id=1, source_target_pairs={{0,2},{1,3},{2,0},{3,1},{4,6},{5,7},{6,4},{7,5},{8,10},{9,11},{10,... | collective-permute-start | bytes 663560 | tf_op jit(solution)/shard_map/ppermute | solution.py:693
  11.9 1.7 %collective-permute-start.4 = (bf16[128,768]{1,0:T(8,128)(2,1)}, bf16[128,768]{1,0:T(8,128)(2,1)S(1)}, u32[]{:S(2)}, u32[]{:S(2)}) collective-permute-start(bf16[128,768]{1,0:T(8,128)(2,1)} %get-tuple-element.125.refs_4_), channel_id=1, source_target_pairs={{0,2},{1,3},{2,0},{3,1},{4,6},{5,7},{6,4},{7,5},{8,10},{9,11},{10,... | collective-permute-start | bytes 589832 | tf_op jit(solution)/shard_map/ppermute | solution.py:693
  14.8 6.1 %forward_attention.2 = (bf16[256,1024]{1,0:T(8,128)(2,1)S(1)}, f32[2,8,1024]{2,1,0:T(8,128)S(1)}, bf16[2,1024,128]{2,1,0:T(8,128)(2,1)S(1)}, bf16[2,1024,128]{2,...) custom-call(s32[2]{0:T(128)S(1)} %pad_add_fusion.1.refs_0_.place, ...), custom_call_target="tpu_custom_call" | custom-call | flops 6000000000 | bytes 8000000 | tf_op jit(solution)/shard_map/forward_attention/pallas_call | solution.py:320
  22.8 6.1 %forward_attention.3 = (bf16[256,1024]{1,0:T(8,128)(2,1)S(1)}, f32[2,8,1024]{2,1,0:T(8,128)S(1)}, bf16[2,1024,128]{2,1,0:T(8,128)(2,1)S(1)}, bf16[2,1024,128]{2,...) custom-call(s32[2]{0:T(128)S(1)} %pad_add_fusion.1.refs_0_.place, ...), custom_call_target="tpu_custom_call" | custom-call | flops 6000000000 | bytes 8000000 | tf_op jit(solution)/shard_map/forward_attention/pallas_call | solution.py:320
  30.2 2.5 %collective-permute-done.7.refs_8_ = bf16[128,1536]{1,0:T(8,128)(2,1)S(1)} collective-permute-done((bf16[128,1536]{1,0:T(8,128)(2,1)S(1)}, bf16[128,1536]{1,0:T(8,128)(2,1)S(1)}, u32[]{:S(2)}, u32[]{:S(2)}) %collective-permute-start.7) | collective-permute-done | bytes 393248 | tf_op jit(solution)/shard_map/ppermute | solution.py:693
  32.6 1.7 %collective-permute-done.8.refs_9_ = bf16[128,1536]{1,0:T(8,128)(2,1)S(1)} collective-permute-done((bf16[128,1536]{1,0:T(8,128)(2,1)S(1)}, bf16[128,1536]{1,0:T(8,128)(2,1)S(1)}, u32[]{:S(2)}, u32[]{:S(2)}) %collective-permute-start.8) | collective-permute-done | bytes 393248 | tf_op jit(solution)/shard_map/ppermute | solution.py:693
  34.4 11.4 %middle.1 = (bf16[1024,512]{1,0:T(8,128)(2,1)S(1)}, f32[1024,512]{1,0:T(8,128)S(1)}, bf16[512,1024]{1,0:T(8,128)(2,1)S(1)}, f32[16,512]{1,0:T(8,128)S(1)}, bf16[...) custom-call(s32[2]{0:T(128)S(1)} %pad_add_fusion.1.refs_0_.place, bf16[1024,512]{1,0:T(8,128)(2,1)S(1)} %copy-done.20, ...), custom_call_target="tpu_custom_call" | custom-call | flops 10000000000 | bytes 12000000 | tf_op jit(solution)/shard_map/middle/pallas_call | solution.py:475
  45.7 8.1 %backward_attention.2 = (bf16[2,384,1024]{2,1,0:T(8,128)(2,1)S(1)}, f32[16,512]{1,0:T(8,128)S(1)}, bf16[256,2304]{1,0:T(8,128)(2,1)S(1)}, bf16[256,2304]{1,0:T(8,128)(2,1)S(1)}) custom-call(s32[2]{0:T(128)S(1)} %pad_add_fusion.1.refs_0_.place, s32[8,1024]{1,0:T(8,128)S(1)} %get-tuple-element.113.refs_0_.refs_2_.cells_ref, ...), custom_call_target="tpu_custom_call" | custom-call | flops 10000000000 | bytes 8000000 | tf_op jit(solution)/shard_map/backward_attention/pallas_call | solution.py:566
  54.0 2.7 %collective-permute-done.9 = bf16[256,2304]{1,0:T(8,128)(2,1)S(1)} collective-permute-done((bf16[256,2304]{1,0:T(8,128)(2,1)S(1)}, bf16[256,2304]{1,0:T(8,128)(2,1)S(1)}, u32[]{:S(2)}, u32[]{:S(2)}) %collective-permute-start.9) | collective-permute-done | bytes 1179680 | tf_op jit(solution)/shard_map/ppermute | solution.py:693
  58.4 9.0 %backward_attention.3 = (bf16[2,384,1024]{2,1,0:T(8,128)(2,1)S(1)}, f32[16,512]{1,0:T(8,128)}, bf16[256,896]{1,0:T(8,128)(2,1)S(1)}, bf16[256,896]{1,0:T(8,128)(2,1)S(1)}) custom-call(s32[2]{0:T(128)S(1)} %pad_add_fusion.1.refs_0_.place, s32[8,1024]{1,0:T(8,128)S(1)} %get-tuple-element.113.refs_0_.refs_2_.cells_ref, ...), custom_call_target="tpu_custom_call" | custom-call | flops 10000000000 | bytes 8000000 | tf_op jit(solution)/shard_map/backward_attention/pallas_call | solution.py:566
  67.4 5.0 %collective-permute-done.11 = bf16[128,2304]{1,0:T(8,128)(2,1)S(1)} collective-permute-done((bf16[128,2304]{1,0:T(8,128)(2,1)S(1)}, bf16[128,2304]{1,0:T(8,128)(2,1)S(1)}, u32[]{:S(2)}, u32[]{:S(2)}) %collective-permute-start.11) | collective-permute-done | bytes 589856 | tf_op jit(solution)/shard_map/ppermute | solution.py:693
  75.6 2.0 %input_gradient.1.grad_ref = f32[1024,512]{1,0:T(8,128)S(1)} custom-call(bf16[512,768]{1,0:T(8,128)(2,1)S(1)} %get-tuple-element.116.w_a, bf16[512,768]{1,0:T(8,128)(2,1)S(1)} %get-tuple-element.127.w_b, f32[1024,512]{1,0:T(8,128)S(1)} %get-tuple-element.139.dh1_ref, bf16[2,384,1024]{2,1,0:T(8,128)(2,1)S(1)} %get-tuple-element.145.trio_a, ...), custom_call_target="tpu_custom_call" | custom-call | flops 1 | bytes 1 | tf_op jit(solution)/shard_map/input_gradient/pallas_call | solution.py:590
  77.6 3.2 %turn_back.1 = (f32[1024,512]{1,0:T(8,128)}, bf16[1024,512]{1,0:T(8,128)(2,1)}) custom-call(s32[1]{0:T(128)} %get-tuple-element.111.start, f32[1024,512]{1,0:T(8,128)S(1)} %input_gradient.1.grad_ref, bf16[1024,512]{1,0:T(8,128)(2,1)S(1)} %get-tuple-element.154.mixed_ref), custom_call_target="tpu_custom_call" | custom-call | flops 1 | bytes 1 | tf_op jit(solution)/shard_map/turn_back/pallas_call | solution.py:224
  83.8 2.0 %collective-permute-done.15 = bf16[64,896]{1,0:T(8,128)(2,1)S(1)} collective-permute-done((bf16[64,896]{1,0:T(8,128)(2,1)S(1)}, bf16[64,896]{1,0:T(8,128)(2,1)S(1)}, u32[]{:S(2)}, u32[]{:S(2)}) %collective-permute-start.15) | collective-permute-done | bytes 114720 | tf_op jit(solution)/shard_map/ppermute | solution.py:693
  88.0 3.3 %collective-permute-start.16 = (bf16[16,2304]{1,0:T(8,128)(2,1)S(1)}, bf16[16,2304]{1,0:T(8,128)(2,1)S(1)}, u32[]{:S(2)}, u32[]{:S(2)}) collective-permute-start(bf16[16,2304]{1,0:T(8,128)(2,1)S(1)} %add_convert_fusion.11), channel_id=1, source_target_pairs={{0,16},{4,20},{8,24},{12,28},{16,0},{20,4},{24,8},{28,12},{1,17},{... | collective-permute-start | bytes 221192 | tf_op jit(solution)/shard_map/ppermute | solution.py:693
  93.7 2.5 %collective-permute-done.18.arrived = bf16[16,896]{1,0:T(8,128)(2,1)S(1)} collective-permute-done((bf16[16,896]{1,0:T(8,128)(2,1)S(1)}, bf16[16,896]{1,0:T(8,128)(2,1)S(1)}, u32[]{:S(2)}, u32[]{:S(2)}) %collective-permute-start.18) | collective-permute-done | bytes 28704 | tf_op jit(solution)/shard_map/ppermute | solution.py:693
  101.7 4.2 %collective-permute-done.24 = bf16[16,2304]{1,0:T(8,128)(2,1)S(1)} collective-permute-done((bf16[16,2304]{1,0:T(8,128)(2,1)S(1)}, bf16[16,2304]{1,0:T(8,128)(2,1)S(1)}, u32[]{:S(2)}, u32[]{:S(2)}) %collective-permute-start.24) | collective-permute-done | bytes 73760 | tf_op jit(solution)/shard_map/ppermute | solution.py:693
  106.1 2.1 %collective-permute-start.22 = (f32[8,128]{1,0:T(8,128)S(1)}, f32[8,128]{1,0:T(8,128)S(1)}, u32[]{:S(2)}, u32[]{:S(2)}) collective-permute-start(f32[8,128]{1,0:T(8,128)S(1)} %add_add_fusion.1), channel_id=1, source_target_pairs={{0,4},{4,0},{8,12},{12,8},{16,20},{20,16},{24,28},{28,24},{1,5},{5... | collective-permute-start | bytes 12296 | tf_op jit(solution)/shard_map/ppermute | solution.py:693
  109.8 2.7 %collective-permute-start.27 = (f32[8,128]{1,0:T(8,128)S(1)}, f32[8,128]{1,0:T(8,128)S(1)}, u32[]{:S(2)}, u32[]{:S(2)}) collective-permute-start(f32[8,128]{1,0:T(8,128)S(1)} %add.92), channel_id=1, source_target_pairs={{0,24},{4,28},{8,16},{12,20},{16,8},{20,12},{24,0},{28,4},{1,25},{... | collective-permute-start | bytes 12296 | tf_op jit(solution)/shard_map/ppermute | solution.py:693
  115.2 2.1 %collective-permute-start.30 = (bf16[64,2304]{1,0:T(8,128)(2,1)S(1)}, bf16[64,2304]{1,0:T(8,128)(2,1)S(1)}, u32[]{:S(2)}, u32[]{:S(2)}) collective-permute-start(bf16[64,2304]{1,0:T(8,128)(2,1)S(1)} %pad_maximum_fusion.refs_0_), channel_id=1, source_target_pairs={{0,4},{4,0},{8,12},{12,8},{16,20},{20,16},{24,28},{28,24},{1,5},{5... | collective-permute-start | bytes 884744 | tf_op jit(solution)/shard_map/ppermute | solution.py:693
  118.2 2.0 %collective-permute-start.31 = (bf16[64,768]{1,0:T(8,128)(2,1)S(1)}, bf16[64,768]{1,0:T(8,128)(2,1)S(1)}, u32[]{:S(2)}, u32[]{:S(2)}) collective-permute-start(bf16[64,768]{1,0:T(8,128)(2,1)S(1)} %constant_dynamic-update-slice_fusion.2.refs_2_), channel_id=1, source_target_pairs={{0,4},{4,0},{8,12},{12,8},{16,20},{20,16},{24,28},{28,24},{1,5},{5... | collective-permute-start | bytes 294920 | tf_op jit(solution)/shard_map/ppermute | solution.py:693
  120.3 3.7 %collective-permute-done.31.refs_3_ = bf16[64,768]{1,0:T(8,128)(2,1)S(1)} collective-permute-done((bf16[64,768]{1,0:T(8,128)(2,1)S(1)}, bf16[64,768]{1,0:T(8,128)(2,1)S(1)}, u32[]{:S(2)}, u32[]{:S(2)}) %collective-permute-start.31) | collective-permute-done | bytes 98336 | tf_op jit(solution)/shard_map/ppermute | solution.py:693
  124.0 4.2 %adam.1 = (f32[128,1536]{1,0:T(8,128)}, f32[128,512]{1,0:T(8,128)}, f32[128,512]{1,0:T(8,128)}, f32[128,512]{1,0:T(8,128)}, f32[9,128]{1,0:T(8,128)}, /*index=5*...) custom-call(s32[2]{0:T(128)S(1)} %pad_add_fusion.1.refs_0_.place, ...), custom_call_target="tpu_custom_call" | custom-call | tf_op jit(solution)/shard_map/adam/pallas_call | solution.py:680
  (116 shorter events, 33.8 us)
Async XLA Ops:
  2.6 8.7 %collective-permute-start.1 = (bf16[144,768]{1,0:T(8,128)(2,1)}, bf16[144,768]{1,0:T(8,128)(2,1)S(1)}, u32[]{:S(2)}, u32[]{:S(2)}) collective-permute-start(bf16[144,768]{1,0:T(8,128)(2,1)} %pack_first.1.refs_4_), channel_id=1, source_target_pairs={{0,2},{1,3},{2,0},{3,1},{4,6},{5,7},{6,4},{7,5},{8,10},{9,11},{10,... | collective-permute-start | bytes 663560 | tf_op jit(solution)/shard_map/ppermute | solution.py:693
  5.6 8.0 %collective-permute-start = (bf16[144,768]{1,0:T(8,128)(2,1)}, bf16[144,768]{1,0:T(8,128)(2,1)}, u32[]{:S(2)}, u32[]{:S(2)}) collective-permute-start(bf16[144,768]{1,0:T(8,128)(2,1)} %pack_first.1.refs_4_), channel_id=1, source_target_pairs={{0,1},{1,0},{2,3},{3,2},{4,5},{5,4},{6,7},{7,6},{8,9},{9,8},{10,11... | collective-permute-start | bytes 663560 | tf_op jit(solution)/shard_map/ppermute | solution.py:693
  11.7 9.8 %collective-permute-start.3 = (bf16[128,768]{1,0:T(8,128)(2,1)}, bf16[128,768]{1,0:T(8,128)(2,1)}, u32[]{:S(2)}, u32[]{:S(2)}) collective-permute-start(bf16[128,768]{1,0:T(8,128)(2,1)} %get-tuple-element.125.refs_4_), channel_id=1, source_target_pairs={{0,1},{1,0},{2,3},{3,2},{4,5},{5,4},{6,7},{7,6},{8,9},{9,8},{10,11... | collective-permute-start | bytes 589832 | tf_op jit(solution)/shard_map/ppermute | solution.py:693
  11.9 9.1 %collective-permute-start.4 = (bf16[128,768]{1,0:T(8,128)(2,1)}, bf16[128,768]{1,0:T(8,128)(2,1)S(1)}, u32[]{:S(2)}, u32[]{:S(2)}) collective-permute-start(bf16[128,768]{1,0:T(8,128)(2,1)} %get-tuple-element.125.refs_4_), channel_id=1, source_target_pairs={{0,2},{1,3},{2,0},{3,1},{4,6},{5,7},{6,4},{7,5},{8,10},{9,11},{10,... | collective-permute-start | bytes 589832 | tf_op jit(solution)/shard_map/ppermute | solution.py:693
  21.0 11.6 %collective-permute-start.6 = (bf16[128,1536]{1,0:T(8,128)(2,1)S(1)}, bf16[128,1536]{1,0:T(8,128)(2,1)S(1)}, u32[]{:S(2)}, u32[]{:S(2)}) collective-permute-start(bf16[128,1536]{1,0:T(8,128)(2,1)S(1)} %get-tuple-element.137.refs_6_), channel_id=1, source_target_pairs={{0,1},{1,0},{2,3},{3,2},{4,5},{5,4},{6,7},{7,6},{8,9},{9,8},{10,11... | collective-permute-start | bytes 1179656 | tf_op jit(solution)/shard_map/ppermute | solution.py:693
  21.5 11.1 %collective-permute-start.7 = (bf16[128,1536]{1,0:T(8,128)(2,1)S(1)}, bf16[128,1536]{1,0:T(8,128)(2,1)S(1)}, u32[]{:S(2)}, u32[]{:S(2)}) collective-permute-start(bf16[128,1536]{1,0:T(8,128)(2,1)S(1)} %get-tuple-element.137.refs_6_), channel_id=1, source_target_pairs={{0,2},{1,3},{2,0},{3,1},{4,6},{5,7},{6,4},{7,5},{8,10},{9,11},{10,... | collective-permute-start | bytes 1179656 | tf_op jit(solution)/shard_map/ppermute | solution.py:693
  57.0 15.4 %collective-permute-start.11 = (bf16[128,2304]{1,0:T(8,128)(2,1)S(1)}, bf16[128,2304]{1,0:T(8,128)(2,1)S(1)}, u32[]{:S(2)}, u32[]{:S(2)}) collective-permute-start(bf16[128,2304]{1,0:T(8,128)(2,1)S(1)} %get-tuple-element.198.refs_0_), channel_id=1, source_target_pairs={{0,2},{1,3},{2,0},{3,1},{4,6},{5,7},{6,4},{7,5},{8,10},{9,11},{10,... | collective-permute-start | bytes 1769480 | tf_op jit(solution)/shard_map/ppermute | solution.py:693
  67.4 5.2 %collective-permute-start.10 = (bf16[256,896]{1,0:T(8,128)(2,1)S(1)}, bf16[256,896]{1,0:T(8,128)(2,1)S(1)}, u32[]{:S(2)}, u32[]{:S(2)}) collective-permute-start(bf16[256,896]{1,0:T(8,128)(2,1)S(1)} %get-tuple-element.151), channel_id=1, source_target_pairs={{0,1},{1,0},{2,3},{3,2},{4,5},{5,4},{6,7},{7,6},{8,9},{9,8},{10,11... | collective-permute-start | bytes 1376264 | tf_op jit(solution)/shard_map/ppermute | solution.py:693
  72.7 8.1 %collective-permute-start.13 = (bf16[128,896]{1,0:T(8,128)(2,1)S(1)}, bf16[128,896]{1,0:T(8,128)(2,1)S(1)}, u32[]{:S(2)}, u32[]{:S(2)}) collective-permute-start(bf16[128,896]{1,0:T(8,128)(2,1)S(1)} %get-tuple-element.202.refs_0_), channel_id=1, source_target_pairs={{0,2},{1,3},{2,0},{3,1},{4,6},{5,7},{6,4},{7,5},{8,10},{9,11},{10,... | collective-permute-start | bytes 688136 | tf_op jit(solution)/shard_map/ppermute | solution.py:693
  74.1 8.0 %collective-permute-start.12 = (bf16[64,2304]{1,0:T(8,128)(2,1)S(1)}, bf16[64,2304]{1,0:T(8,128)(2,1)S(1)}, u32[]{:S(2)}, u32[]{:S(2)}) collective-permute-start(bf16[64,2304]{1,0:T(8,128)(2,1)S(1)} %get-tuple-element.200), channel_id=1, source_target_pairs={{0,4},{4,0},{8,12},{12,8},{16,20},{20,16},{24,28},{28,24},{1,5},{5... | collective-permute-start | bytes 884744 | tf_op jit(solution)/shard_map/ppermute | solution.py:693
  80.9 4.9 %collective-permute-start.15 = (bf16[64,896]{1,0:T(8,128)(2,1)S(1)}, bf16[64,896]{1,0:T(8,128)(2,1)S(1)}, u32[]{:S(2)}, u32[]{:S(2)}) collective-permute-start(bf16[64,896]{1,0:T(8,128)(2,1)S(1)} %get-tuple-element.206), channel_id=1, source_target_pairs={{0,4},{4,0},{8,12},{12,8},{16,20},{20,16},{24,28},{28,24},{1,5},{5... | collective-permute-start | bytes 344072 | tf_op jit(solution)/shard_map/ppermute | solution.py:693
  82.2 5.8 %collective-permute-start.14 = (bf16[32,2304]{1,0:T(8,128)(2,1)S(1)}, bf16[32,2304]{1,0:T(8,128)(2,1)S(1)}, u32[]{:S(2)}, u32[]{:S(2)}) collective-permute-start(bf16[32,2304]{1,0:T(8,128)(2,1)S(1)} %get-tuple-element.203), channel_id=1, source_target_pairs={{0,8},{4,12},{8,0},{12,4},{16,24},{20,28},{24,16},{28,20},{1,9},{5... | collective-permute-start | bytes 442376 | tf_op jit(solution)/shard_map/ppermute | solution.py:693
  85.9 5.4 %collective-permute-start.17 = (bf16[32,896]{1,0:T(8,128)(2,1)S(1)}, bf16[32,896]{1,0:T(8,128)(2,1)S(1)}, u32[]{:S(2)}, u32[]{:S(2)}) collective-permute-start(bf16[32,896]{1,0:T(8,128)(2,1)S(1)} %get-tuple-element.208), channel_id=1, source_target_pairs={{0,8},{4,12},{8,0},{12,4},{16,24},{20,28},{24,16},{28,20},{1,9},{5... | collective-permute-start | bytes 172040 | tf_op jit(solution)/shard_map/ppermute | solution.py:693
  88.0 5.6 %collective-permute-start.16 = (bf16[16,2304]{1,0:T(8,128)(2,1)S(1)}, bf16[16,2304]{1,0:T(8,128)(2,1)S(1)}, u32[]{:S(2)}, u32[]{:S(2)}) collective-permute-start(bf16[16,2304]{1,0:T(8,128)(2,1)S(1)} %add_convert_fusion.11), channel_id=1, source_target_pairs={{0,16},{4,20},{8,24},{12,28},{16,0},{20,4},{24,8},{28,12},{1,17},{... | collective-permute-start | bytes 221192 | tf_op jit(solution)/shard_map/ppermute | solution.py:693
  91.3 4.8 %collective-permute-start.18 = (bf16[16,896]{1,0:T(8,128)(2,1)S(1)}, bf16[16,896]{1,0:T(8,128)(2,1)S(1)}, u32[]{:S(2)}, u32[]{:S(2)}) collective-permute-start(bf16[16,896]{1,0:T(8,128)(2,1)S(1)} %get-tuple-element.210), channel_id=1, source_target_pairs={{0,16},{4,20},{8,24},{12,28},{16,0},{20,4},{24,8},{28,12},{1,17},{... | collective-permute-start | bytes 86024 | tf_op jit(solution)/shard_map/ppermute | solution.py:693
  96.9 4.9 %collective-permute-start.21 = (f32[8,128]{1,0:T(8,128)S(1)}, f32[8,128]{1,0:T(8,128)S(1)}, u32[]{:S(2)}, u32[]{:S(2)}) collective-permute-start(f32[8,128]{1,0:T(8,128)S(1)} %get-tuple-element.163), channel_id=1, source_target_pairs={{0,3},{1,2},{2,1},{3,0},{4,7},{5,6},{6,5},{7,4},{8,11},{9,10},{10,... | collective-permute-start | bytes 12296 | tf_op jit(solution)/shard_map/ppermute | solution.py:693
  98.8 7.2 %collective-permute-start.24 = (bf16[16,2304]{1,0:T(8,128)(2,1)S(1)}, bf16[16,2304]{1,0:T(8,128)(2,1)S(1)}, u32[]{:S(2)}, u32[]{:S(2)}) collective-permute-start(bf16[16,2304]{1,0:T(8,128)(2,1)S(1)} %add_convert_fusion.10.early_ref), channel_id=1, source_target_pairs={{0,16},{4,20},{8,24},{12,28},{16,0},{20,4},{24,8},{28,12},{1,17},{... | collective-permute-start | bytes 221192 | tf_op jit(solution)/shard_map/ppermute | solution.py:693
  100.5 7.7 %collective-permute-start.23 = (bf16[16,768]{1,0:T(8,128)(2,1)S(1)}, bf16[16,768]{1,0:T(8,128)(2,1)S(1)}, u32[]{:S(2)}, u32[]{:S(2)}) collective-permute-start(bf16[16,768]{1,0:T(8,128)(2,1)S(1)} %get-tuple-element.164), channel_id=1, source_target_pairs={{0,16},{4,20},{8,24},{12,28},{16,0},{20,4},{24,8},{28,12},{1,17},{... | collective-permute-start | bytes 73736 | tf_op jit(solution)/shard_map/ppermute | solution.py:693
  106.0 9.2 %collective-permute-start.29 = (bf16[32,2304]{1,0:T(8,128)(2,1)S(1)}, bf16[32,2304]{1,0:T(8,128)(2,1)S(1)}, u32[]{:S(2)}, u32[]{:S(2)}) collective-permute-start(bf16[32,2304]{1,0:T(8,128)(2,1)S(1)} %pad_maximum_fusion.1), channel_id=1, source_target_pairs={{0,8},{4,12},{8,0},{12,4},{16,24},{20,28},{24,16},{28,20},{1,9},{5... | collective-permute-start | bytes 442376 | tf_op jit(solution)/shard_map/ppermute | solution.py:693
  109.8 10.5 %collective-permute-start.27 = (f32[8,128]{1,0:T(8,128)S(1)}, f32[8,128]{1,0:T(8,128)S(1)}, u32[]{:S(2)}, u32[]{:S(2)}) collective-permute-start(f32[8,128]{1,0:T(8,128)S(1)} %add.92), channel_id=1, source_target_pairs={{0,24},{4,28},{8,16},{12,20},{16,8},{20,12},{24,0},{28,4},{1,25},{... | collective-permute-start | bytes 12296 | tf_op jit(solution)/shard_map/ppermute | solution.py:693
  112.5 7.7 %collective-permute-start.26 = (f32[8,128]{1,0:T(8,128)S(1)}, f32[8,128]{1,0:T(8,128)S(1)}, u32[]{:S(2)}, u32[]{:S(2)}) collective-permute-start(f32[8,128]{1,0:T(8,128)S(1)} %add.92), channel_id=1, source_target_pairs={{0,16},{4,20},{8,24},{12,28},{16,0},{20,4},{24,8},{28,12},{1,17},{... | collective-permute-start | bytes 12296 | tf_op jit(solution)/shard_map/ppermute | solution.py:693
  113.2 7.1 %collective-permute-start.25 = (f32[8,128]{1,0:T(8,128)S(1)}, f32[8,128]{1,0:T(8,128)S(1)}, u32[]{:S(2)}, u32[]{:S(2)}) collective-permute-start(f32[8,128]{1,0:T(8,128)S(1)} %add.92), channel_id=1, source_target_pairs={{0,8},{4,12},{8,0},{12,4},{16,24},{20,28},{24,16},{28,20},{1,9},{5... | collective-permute-start | bytes 12296 | tf_op jit(solution)/shard_map/ppermute | solution.py:693
  115.2 8.7 %collective-permute-start.30 = (bf16[64,2304]{1,0:T(8,128)(2,1)S(1)}, bf16[64,2304]{1,0:T(8,128)(2,1)S(1)}, u32[]{:S(2)}, u32[]{:S(2)}) collective-permute-start(bf16[64,2304]{1,0:T(8,128)(2,1)S(1)} %pad_maximum_fusion.refs_0_), channel_id=1, source_target_pairs={{0,4},{4,0},{8,12},{12,8},{16,20},{20,16},{24,28},{28,24},{1,5},{5... | collective-permute-start | bytes 884744 | tf_op jit(solution)/shard_map/ppermute | solution.py:693
  118.2 5.7 %collective-permute-start.31 = (bf16[64,768]{1,0:T(8,128)(2,1)S(1)}, bf16[64,768]{1,0:T(8,128)(2,1)S(1)}, u32[]{:S(2)}, u32[]{:S(2)}) collective-permute-start(bf16[64,768]{1,0:T(8,128)(2,1)S(1)} %constant_dynamic-update-slice_fusion.2.refs_2_), channel_id=1, source_target_pairs={{0,4},{4,0},{8,12},{12,8},{16,20},{20,16},{24,28},{28,24},{1,5},{5... | collective-permute-start | bytes 294920 | tf_op jit(solution)/shard_map/ppermute | solution.py:693
  (29 other events, 523.2 us)

commit v2 on v1

--- a/solution.py
+++ b/solution.py
@@ -23,12 +23,15 @@
 NORM_EPS = 1e-05
 ADAM_EPS = 1e-08
 MASKED = -1e30
+HIDDEN = 16
 BF = jnp.bfloat16
 F32 = jnp.float32
 MIB = 1024 * 1024
 GROUP = 2
 HW = GROUP * TRIO
-FORWARD_MIB, MIDDLE_MIB, BACKWARD_MIB = 16, 20, 24
+FIRST = 1
+LATE = (PAIRS - FIRST) * TRIO
+FORWARD_MIB, MIDDLE_MIB, BACKWARD_MIB = 12, 20, 22
 
 NN = (((1,), (0,)), ((), ()))
 NT = (((1,), (1,)), ((), ()))
@@ -40,7 +43,7 @@
     return lax.dot_general(a, b, dims, preferred_element_type=F32)
 
 
-def params(mib=20):
+def params(mib=8):
     return pltpu.CompilerParams(vmem_limit_bytes=mib * MIB)
 
 
@@ -161,9 +164,10 @@
     return write
 
 
-def turn_tokens_kernel(tokens, both, *refs):
+def turn_tokens_kernel(tokens, coded, *refs):
     tokens_out, turned_out, cells_out, start_out, wide_tokens = refs[-5:]
-    cell = both[0:1, :]
+    seen = coded[...] < HIDDEN
+    cell = jnp.where(seen, coded[...], coded[...] - HIDDEN)
     start = jnp.int32(TOK_DEV)
     for c in range(4):
         size = jnp.sum((cell == c).astype(jnp.int32))
@@ -172,16 +176,16 @@
     start_out[0] = start
     shift = jnp.where(start == 0, 0, TOK_DEV - start)
     row = lax.broadcasted_iota(jnp.int32, (8, TOK_DEV), 0)
-    cells_out[...] = pltpu.roll(jnp.where(row == 0, cell, both[1:2, :]), shift, 1)
+    cells_out[...] = pltpu.roll(jnp.where((row == 0) | seen, cell, -1), shift, 1)
     wide_tokens[...] = tokens[...].astype(F32)
     turn_rows(wide_tokens, start, write_into(tokens_out))
     turned_out[...] = tokens_out[...].T
 
 
-def turn_tokens(tokens, both, later):
+def turn_tokens(tokens, coded):
     return pl.pallas_call(
         turn_tokens_kernel,
-        in_specs=[VM, VM] + [ANY] * len(later),
+        in_specs=[VM, VM],
         out_specs=[VM] * 3 + [SMEM],
         out_shape=[
             sds((TOK_DEV, D), BF),
@@ -190,10 +194,10 @@
             sds((1,), jnp.int32),
         ],
         scratch_shapes=[pltpu.VMEM((TOK_DEV, D), F32)],
-        compiler_params=params(16),
+        compiler_params=params(),
         cost_estimate=cost(1e7, 3e6),
         name="turn_tokens",
-    )(tokens, both, *later)
+    )(tokens, coded)
 
 
 def turn_cotangent_kernel(start, cot_ref, *refs):
@@ -206,7 +210,7 @@
         in_specs=[SMEM, VM] + [ANY] * len(later),
         out_specs=VM,
         out_shape=sds((TOK_DEV, D), F32),
-        compiler_params=params(16),
+        compiler_params=params(),
         cost_estimate=cost(1e7, 4e6),
         name="turn_cotangent",
     )(start, cot, *later)
@@ -493,9 +497,10 @@
     )(place, tokens, cot, *atts, vec, *pieces)
 
 
-def backward_kernel(n_shards, stages, base, n_before, place, cells_ref, tokens_t, vec_ref, att_ref, lse_ref,
-                    krow_ref, vrow_ref, qt_ref, kt_ref, datt_ref, *refs):
-    before = refs[:n_before]
+def backward_kernel(n_shards, stages, plan, n_sets, n_before, last, place, cells_ref, tokens_t, vec_ref,
+                    datt_ref, *refs):
+    sets = [refs[6 * number : 6 * (number + 1)] for number in range(n_sets)]
+    before = refs[6 * n_sets : 6 * n_sets + n_before]
     bias, dw = refs[-2:]
     n_g = 2 if stages else 1
     d_out, vec = refs[-4 - n_g : -2 - n_g]
@@ -504,19 +509,20 @@
     vec[...] = vec_ref[...]
     halves = [slice(0, HALF), slice(HALF, TOK_DEV)]
     chains = []
-    for local in range(GROUP):
+    for place_out, (number, local, pair) in enumerate(plan):
+        att_ref, lse_ref, krow_ref, vrow_ref, qt_ref, kt_ref = sets[number]
         here = slice(local * PAIR, (local + 1) * PAIR)
         q_t, k_t = qt_ref[here, :], kt_ref[here, :]
-        d_t = datt_ref[(base + local) * PAIR : (base + local + 1) * PAIR, :]
+        d_t = datt_ref[pair * PAIR : (pair + 1) * PAIR, :]
         k_row, v_row = krow_ref[local], vrow_ref[local]
         product = d_t.astype(F32) * att_ref[here, :].astype(F32)
         for mine in halves:
             s = dot(k_row[mine], both_heads(q_t[:, mine]), NN)
             d_prob = dot(v_row[mine], both_heads(d_t[:, mine]), NN)
-            chains.append((local, mine, q_t, k_t, d_t, product, s, d_prob))
-    for local, mine, q_t, k_t, d_t, product, s, d_prob in chains:
+            lse = jnp.concatenate([lse_ref[local, 0:1, mine], lse_ref[local, 1:2, mine]], 1)
+            chains.append((place_out, mine, q_t, k_t, d_t, product, s, d_prob, lse))
+    for place_out, mine, q_t, k_t, d_t, product, s, d_prob, lse in chains:
         mask = bias[mine, :]
-        lse = jnp.concatenate([lse_ref[local, 0:1, mine], lse_ref[local, 1:2, mine]], 1)
         delta = jnp.concatenate(
             [column_sum(product[:HEAD_DIM, mine]), column_sum(product[HEAD_DIM:, mine])], 1
         )
@@ -531,57 +537,57 @@
             d_v = dot(d_t[head, mine], prob_low[:, cols], NT)
             for t, value in enumerate((d_q, d_k, d_v)):
                 at = t * PAIR + h * HEAD_DIM
-                d_out[local, at : at + HEAD_DIM, mine] = value.astype(BF)
+                d_out[place_out, at : at + HEAD_DIM, mine] = value.astype(BF)
     ones = jnp.ones((16, TOK_DEV), BF)
     for out, ref in zip(g_outs, before):
         out[:, : ref.shape[1]] = ref[...]
     first = before[0].shape[1] if before else 0
-    for local in range(GROUP):
-        pair = base + local
-        trio = d_out[local]
-        dw[local] = dot(tokens_t[...], trio, NT)
-        at = first + local * TRIO
-        store_rows(g_outs, place, n_shards, stages, dw.at[local], slice(at, at + TRIO))
+    for place_out, (number, local, pair) in enumerate(plan):
+        trio = d_out[place_out]
+        dw[place_out] = dot(tokens_t[...], trio, NT)
+        at = first + place_out * TRIO
+        store_rows(g_outs, place, n_shards, stages, dw.at[place_out], slice(at, at + TRIO))
         total = dot(ones, trio, NT)
         lanes = slice(pair * PAIR, (pair + 1) * PAIR)
         vec[0:1, lanes] = total[:1, :PAIR]
         vec[1:2, lanes] = total[:1, 2 * PAIR :]
-    if stages and base + GROUP == PAIRS:
+    if stages and last:
         height = g_outs[0].shape[0]
         rows = D // n_shards
         for target, source, count in row_sources(place, n_shards, stages):
             at = pl.multiple_of(source // rows * rows, rows)
-            g_outs[target // height][target % height : target % height + count, HW:] = vec[
+            g_outs[target // height][target % height : target % height + count, LATE:] = vec[
                 :, pl.ds(at, rows)
             ].astype(BF)
 
 
-def backward_attention(base, place, cells, tokens_t, vec_sums, saved, d_t, before, n_shards, stages, later):
-    width = HW + (before[0].shape[1] if before else 0)
+def backward_attention(plan, last, place, cells, tokens_t, vec_sums, sets, d_t, before, n_shards, stages, later):
+    width = len(plan) * TRIO + (before[0].shape[1] if before else 0)
     if stages:
-        width += PAIR if base + GROUP == PAIRS else 0
-        shapes = [sds((D // 2, width), BF)] * 2
+        shapes = [sds((D // 2, width + (PAIR if last else 0)), BF)] * 2
     else:
         shapes = [sds((D, width), BF)]
-    return pl.pallas_call(
-        functools.partial(backward_kernel, n_shards, stages, base, len(before)),
-        in_specs=[SMEM] + [VM] * (10 + len(before)) + [ANY] * len(later),
+    flat = [value for saved in sets for value in saved]
+    return pl.pallas_call(
+        functools.partial(backward_kernel, n_shards, stages, plan, len(sets), len(before), last),
+        in_specs=[SMEM] + [VM] * (4 + len(flat) + len(before)) + [ANY] * len(later),
         out_specs=[VM] * (2 + len(shapes)),
-        out_shape=[sds((GROUP, TRIO, TOK_DEV), BF), sds((16, D), F32)] + shapes,
-        scratch_shapes=[pltpu.VMEM((TOK_DEV, HALF), F32), pltpu.VMEM((GROUP, D, TRIO), F32)],
+        out_shape=[sds((len(plan), TRIO, TOK_DEV), BF), sds((16, D), F32)] + shapes,
+        scratch_shapes=[pltpu.VMEM((TOK_DEV, HALF), F32), pltpu.VMEM((len(plan), D, TRIO), F32)],
         compiler_params=params(BACKWARD_MIB),
-        cost_estimate=cost(1e10, 8e6, 2**21),
+        cost_estimate=cost(5e9 * len(plan), 8e6, 2**21),
         name="backward_attention",
-    )(place, cells, tokens_t, vec_sums, *saved, d_t, *before, *later)
+    )(place, cells, tokens_t, vec_sums, d_t, *flat, *before, *later)
 
 
 def input_grad_kernel(w_a, w_b, dh1_ref, trio_a, trio_b, *refs):
     out = refs[-1]
-    for part in range(TOK_DEV // QT):
-        here = slice(part * QT, (part + 1) * QT)
+    trios = [ref.at[number] for ref in (trio_a, trio_b) for number in range(ref.shape[0])]
+    for tile in range(TOK_DEV // QT):
+        here = slice(tile * QT, (tile + 1) * QT)
         total = None
-        for w_ref, trio in ((w_a, trio_a), (w_b, trio_b)):
-            term = dot(w_ref[...], jnp.concatenate([trio[0, :, here], trio[1, :, here]], 0), NN)
+        for w_ref, trio in ((w_a, trios[:GROUP]), (w_b, trios[GROUP:])):
+            term = dot(w_ref[...], jnp.concatenate([part[:, here] for part in trio], 0), NN)
             total = term if total is None else total + term
         out[here, :] = dh1_ref[here, :] + total.T
 
@@ -592,7 +598,7 @@
         in_specs=[VM] * 5 + [ANY] * len(later),
         out_specs=VM,
         out_shape=sds((TOK_DEV, D), F32),
-        compiler_params=params(24),
+        compiler_params=params(),
         cost_estimate=cost(1, 1),
         name="input_gradient",
     )(*weights, d_h1, *trios, *later)
@@ -606,14 +612,17 @@
     return weight - rate * (update + decay * weight), first, second
 
 
-def pair_parts(first, base):
+def pair_parts(first, pairs):
     return [
-        (slice(first + target, first + target + PAIR), 0, source) for target, source in trio_columns(base)
+        (slice(at, at + PAIR), 0, t * D + pair * PAIR)
+        for number, pair in enumerate(pairs)
+        for t in range(3)
+        for at in [first + number * TRIO + t * PAIR]
     ]
 
 
-EARLY_PARTS = [(slice(i * D, (i + 1) * D), i + 1, 0) for i in range(3)] + pair_parts(3 * D, 0)
-LATE_PARTS = pair_parts(0, GROUP)
+EARLY_PARTS = [(slice(i * D, (i + 1) * D), i + 1, 0) for i in range(3)] + pair_parts(3 * D, range(FIRST))
+LATE_PARTS = pair_parts(0, range(FIRST, PAIRS))
 
 
 def adam_kernel(quick, limit, place, square_ref, *refs):
@@ -707,26 +716,27 @@
     return add_low(keep[:rows], arrived[:rows]), send
 
 
-def finish_kernel(place, early_ref, keep, arrived, piece_out, vec_out, square_out):
-    late = add_low(keep[:, :HW], arrived[:, :HW])
-    vec = keep[:, HW:].astype(F32) + arrived[:, HW:].astype(F32)
-    piece_out[...] = late
-    vec_out[...] = vec
-    early, late = early_ref[...].astype(F32), late.astype(F32)
-    total = jnp.sum(early * early) + jnp.sum(late * late)
-    total = total + jnp.where(place[1] == 0, jnp.sum(vec * vec), 0.0)
-    square_out[...] = jnp.full(square_out.shape, total, F32)
-
-
-def finish(place, early, keep, arrived):
-    return pl.pallas_call(
-        finish_kernel,
+def squares_kernel(place, early, late, vec, out):
+    total = []
+    for piece in range(4):
+        rows = slice(16 * piece, 16 * (piece + 1))
+        first, second = early[rows, :].astype(F32), late[rows, :].astype(F32)
+        total.append(jnp.sum(first * first) + jnp.sum(second * second))
+    total = (total[0] + total[1]) + (total[2] + total[3])
+    total = total + jnp.where((place[1] & 1) == 0, jnp.sum(vec[...] * vec[...]), 0.0)
+    out[...] = jnp.full(out.shape, total, F32)
+
+
+def half_squares(place, early, late, vec):
+    return pl.pallas_call(
+        squares_kernel,
         in_specs=[SMEM] + [VM] * 3,
-        out_specs=[VM] * 3,
-        out_shape=[sds((16, HW), BF), sds((16, PAIR), F32), sds((8, PAIR), F32)],
+        out_specs=VM,
+        out_shape=sds((8, PAIR), F32),
         compiler_params=params(),
-        name="finish",
-    )(place, early, keep, arrived)
+        cost_estimate=cost(1, 1),
+        name="half_squares",
+    )(place, early, late, vec)
 
 
 def directly(value, axis, masks):
@@ -762,10 +772,8 @@
     shard = w_qkv.shape[0]
 
     low_a = pack_first(w_qkv, vectors)
-    keys = jnp.where((present == 1) & (generate == 0), cells, -1)
-    tokens, tokens_t, cells, start = turn_tokens(
-        tokens, after(jnp.concatenate([cells, keys], 0), low_a), []
-    )
+    coded = jnp.where((present == 1) & (generate == 0), cells, cells + HIDDEN)
+    tokens, tokens_t, cells, start = turn_tokens(tokens, after(coded, low_a))
     low_b, low_rest = pl.pallas_call(
         pack_second_kernel,
         in_specs=[VM] * 4 + [ANY],
@@ -802,8 +810,10 @@
     mixed, d_h1, d_t, vec_sums, *g_rest = middle(
         place, tokens, cotangent, (saved_a[0], saved_b[0]), vec_full, pieces_rest, order, stages
     )
+    sets = [saved_a, saved_b]
+    plan = [(pair // GROUP, pair % GROUP, pair) for pair in range(PAIRS)]
     trio_a, vec_sums, *early = backward_attention(
-        0, place, cells, tokens_t, vec_sums, saved_a, d_t, g_rest, narrow, stages, []
+        plan[:FIRST], False, place, cells, tokens_t, vec_sums, sets, d_t, g_rest, narrow, stages, []
     )
     later = []
     if quick:
@@ -812,44 +822,44 @@
         e_arrived = swap(e_send, "narrow", 2)
         later = [e_send]
     trio_b, vec_sums, *late = backward_attention(
-        GROUP, place, cells, tokens_t, vec_sums, saved_b, d_t, [], narrow, stages, later
+        plan[FIRST:], True, place, cells, tokens_t, vec_sums, sets, d_t, [], narrow, stages, later
     )
     weights, trios = (w_a, w_b), (trio_a, trio_b)
 
     if quick:
         b_keep, b_send = late
         b_arrived = swap(b_send, "narrow", 1)
-        e_keep, e_send = fold(e_keep, after(e_arrived, trio_b))
+        turned_grad = input_gradient(weights, d_h1, trios, [])
+        e_keep, e_send = fold(e_keep, after(e_arrived, turned_grad))
         e_arrived = swap(e_send, "wide", 1)
         b_keep, b_send = fold(b_keep, after(b_arrived, e_send))
         b_arrived = swap(b_send, "narrow", 2)
-        turned_grad = input_gradient(weights, d_h1, trios, [b_send])
-        input_grad, mixed = turn_back(start, turned_grad, mixed, [])
-        b_keep, b_send = fold(b_keep, after(b_arrived, input_grad))
-        b_arrived = swap(b_send, "wide", 1)
-        e_keep, e_send = fold(e_keep, after(e_arrived, b_send))
+        input_grad, mixed = turn_back(start, turned_grad, mixed, [b_send])
+        e_keep, e_send = fold(e_keep, after(e_arrived, input_grad))
         e_arrived = swap(e_send, "wide", 2)
         b_keep, b_send = fold(b_keep, after(b_arrived, e_send))
-        b_arrived = swap(b_send, "wide", 2)
+        b_arrived = swap(b_send, "wide", 1)
         e_keep, e_send = fold(e_keep, after(e_arrived, b_send))
         e_arrived = swap(e_send, "wide", 4)
         b_keep, b_send = fold(b_keep, after(b_arrived, e_send))
-        b_arrived = swap(b_send, "wide", 4)
+        b_arrived = swap(b_send, "wide", 2)
         e_low = add_low(e_keep, after(e_arrived, b_send))
         e_arrived = swap(e_low, "wide", 4)
-        b_low, vec_total, squares = finish(place, e_low, b_keep, b_arrived)
+        b_keep, b_send = fold(b_keep, after(b_arrived, e_low))
+        b_arrived = swap(b_send, "wide", 4)
+        e_low = join(e_low, after(e_arrived, b_send))
+        e_arrived = swap(e_low, "wide", 2)
+        b_arrived = after(b_arrived, e_low)
+        vec_total = b_keep[:, LATE:].astype(F32) + b_arrived[:, LATE:].astype(F32)
+        b_low = add_low(b_keep[:, :LATE], b_arrived[:, :LATE])
         b_arrived = swap(b_low, "wide", 4)
+        e_low = join(e_low, after(e_arrived, b_low))
+        b_low = join(b_low, after(b_arrived, e_low))
+        b_low = join(b_low, swap(b_low, "wide", 2))
+        e_arrived, b_arrived = swap(e_low, "wide", 1), swap(b_low, "wide", 1)
+        squares = half_squares(place, e_low, b_low, vec_total)
         squares = four(squares, directly(squares, "narrow", (1, 2, 3)))
-        e_low = join(e_low, after(e_arrived, squares))
-        e_arrived, square = swap(e_low, "wide", 2), swap(squares, "wide", 1)
-        b_low = join(b_low, after(b_arrived, e_low))
-        b_arrived = swap(b_low, "wide", 2)
-        squares = squares + after(square, b_low)
-        e_low = join(e_low, after(e_arrived, squares))
-        e_arrived, others = swap(e_low, "wide", 1), directly(squares, "wide", (2, 4, 6))
-        b_low = join(b_low, after(b_arrived, e_low))
-        b_arrived = swap(b_low, "wide", 1)
-        squares = four(squares, after(others, b_low))
+        squares = squares + swap(squares, "wide", 1)
         grads = [e_low, after(e_arrived, squares), b_low, after(b_arrived, squares)]
     else:
         turned_grad = input_gradient(weights, d_h1, trios, [])

time: 129 us -> 119 us (0.922)
  waiting for transfers between devices: 28.7 us -> 22 us
  starting transfers between devices: 36.8 us -> 34.7 us
    ppermute x32 -> x29, waiting for transfers between devices: 28.7 us -> 22 us  [swap(): return lax.ppermute(value, axis, [(i, i ^ mask) for i in range(size)])]
    ppermute x32 -> x29, starting transfers between devices: 36.8 us -> 34.7 us  [swap(): return lax.ppermute(value, axis, [(i, i ^ mask) for i in range(size)])]
    unnamed x44 -> x42, local copies, waits for them, and re-layouts: 3.49 us -> 3.5 us
  transfers between devices with their start and end apart: 32 -> 29, of which waited for: 14 -> 15; matrix products, arithmetic and copies ran while one was open for 2% -> 1% of each run, Pallas kernels for 23% -> 28%
where the time goes in v2:
time: 119 us
  Pallas kernels  55.8 us (47%)
  starting transfers between devices  34.7 us (29%)
  waiting for transfers between devices  22 us (18%)
  local copies, waits for them, and re-layouts  3.51 us (3%)
  other arithmetic  1.62 us (1%)
  between operations  1.28 us (1%)
    ppermute x29, starting transfers between devices, swap(): return lax.ppermute(value, axis, [(i, i ^ mask) for i in range(size)])  34.7 us
    ppermute x29, waiting for transfers between devices, swap(): return lax.ppermute(value, axis, [(i, i ^ mask) for i in range(size)])  22 us
    pallas_call x2, Pallas kernels, backward_attention(): pl.pallas_call(functools.partial(backward_kernel, n_shards, stages, plan,...  17.2 us
    pallas_call x2, Pallas kernels, forward_attention(): pl.pallas_call(functools.partial(forward_kernel, order, len(pieces), base...  12.3 us
    pallas_call x1, Pallas kernels, middle(): pl.pallas_call(functools.partial(middle_kernel, order, len(pieces), len(o...  11.2 us
    pallas_call x1, Pallas kernels, adam_step(): pl.pallas_call(functools.partial(adam_kernel, quick, limit), grid=(steps,...  4.19 us
    unnamed x42, local copies, waits for them, and re-layouts  3.5 us
    pallas_call x1, Pallas kernels, turn_back(): pl.pallas_call(turn_back_kernel, in_specs=[SMEM, VM, VM] + [ANY] * len(la...  3.23 us
  transfers between devices with their start and end apart: 29, of which 15 were waited for; matrix products, arithmetic and copies ran while one was open for 1% of the time, Pallas kernels for 28%

profile of v2, /device:TPU:0, one launch (start us, length us, event | category | flops | bytes accessed | tf_op | source)
XLA Modules:
  0.0 118.9 jit_solution(1583888600037204499)
XLA Ops:
  0.7 1.9 %pack_first.1.refs_4_ = bf16[144,768]{1,0:T(8,128)(2,1)} custom-call(f32[128,1536]{1,0:T(8,128)} %refs_5_.1, f32[9,128]{1,0:T(8,128)} %refs_9_.1), custom_call_target="tpu_custom_call" | custom-call | tf_op jit(solution)/shard_map/pack_first/pallas_call | solution.py:105
  2.6 3.0 %collective-permute-start.1 = (bf16[144,768]{1,0:T(8,128)(2,1)}, bf16[144,768]{1,0:T(8,128)(2,1)S(1)}, u32[]{:S(2)}, u32[]{:S(2)}) collective-permute-start(bf16[144,768]{1,0:T(8,128)(2,1)} %pack_first.1.refs_4_), channel_id=1, source_target_pairs={{0,2},{1,3},{2,0},{3,1},{4,6},{5,7},{6,4},{7,5},{8,10},{9,11},{10,... | collective-permute-start | bytes 663560 | tf_op jit(solution)/shard_map/ppermute | solution.py:702
  11.9 1.7 %collective-permute-start.4 = (bf16[128,768]{1,0:T(8,128)(2,1)}, bf16[128,768]{1,0:T(8,128)(2,1)S(1)}, u32[]{:S(2)}, u32[]{:S(2)}) collective-permute-start(bf16[128,768]{1,0:T(8,128)(2,1)} %get-tuple-element.118.refs_4_), channel_id=1, source_target_pairs={{0,2},{1,3},{2,0},{3,1},{4,6},{5,7},{6,4},{7,5},{8,10},{9,11},{10,... | collective-permute-start | bytes 589832 | tf_op jit(solution)/shard_map/ppermute | solution.py:702
  14.9 6.1 %forward_attention.2 = (bf16[256,1024]{1,0:T(8,128)(2,1)S(1)}, f32[2,8,1024]{2,1,0:T(8,128)S(1)}, bf16[2,1024,128]{2,1,0:T(8,128)(2,1)S(1)}, bf16[2,1024,128]{2,...) custom-call(s32[2]{0:T(128)S(1)} %pad_add_fusion.refs_0_.place, ...), custom_call_target="tpu_custom_call" | custom-call | flops 6000000000 | bytes 8000000 | tf_op jit(solution)/shard_map/forward_attention/pallas_call | solution.py:324
  22.9 6.1 %forward_attention.3 = (bf16[256,1024]{1,0:T(8,128)(2,1)S(1)}, f32[2,8,1024]{2,1,0:T(8,128)S(1)}, bf16[2,1024,128]{2,1,0:T(8,128)(2,1)S(1)}, bf16[2,1024,128]{2,...) custom-call(s32[2]{0:T(128)S(1)} %pad_add_fusion.refs_0_.place, ...), custom_call_target="tpu_custom_call" | custom-call | flops 6000000000 | bytes 8000000 | tf_op jit(solution)/shard_map/forward_attention/pallas_call | solution.py:324
  30.1 2.6 %collective-permute-done.7.refs_8_ = bf16[128,1536]{1,0:T(8,128)(2,1)S(1)} collective-permute-done((bf16[128,1536]{1,0:T(8,128)(2,1)S(1)}, bf16[128,1536]{1,0:T(8,128)(2,1)S(1)}, u32[]{:S(2)}, u32[]{:S(2)}) %collective-permute-start.7) | collective-permute-done | bytes 393248 | tf_op jit(solution)/shard_map/ppermute | solution.py:702
  32.7 1.7 %collective-permute-done.8.refs_9_ = bf16[128,1536]{1,0:T(8,128)(2,1)S(1)} collective-permute-done((bf16[128,1536]{1,0:T(8,128)(2,1)S(1)}, bf16[128,1536]{1,0:T(8,128)(2,1)S(1)}, u32[]{:S(2)}, u32[]{:S(2)}) %collective-permute-start.8) | collective-permute-done | bytes 393248 | tf_op jit(solution)/shard_map/ppermute | solution.py:702
  34.4 11.2 %middle.1 = (bf16[1024,512]{1,0:T(8,128)(2,1)S(1)}, f32[1024,512]{1,0:T(8,128)S(1)}, bf16[512,1024]{1,0:T(8,128)(2,1)S(1)}, f32[16,512]{1,0:T(8,128)S(1)}, bf16[...) custom-call(s32[2]{0:T(128)S(1)} %pad_add_fusion.refs_0_.place, bf16[1024,512]{1,0:T(8,128)(2,1)S(1)} %copy-done.20, ...), custom_call_target="tpu_custom_call" | custom-call | flops 10000000000 | bytes 12000000 | tf_op jit(solution)/shard_map/middle/pallas_call | solution.py:479
  45.6 4.6 %backward_attention.2 = (bf16[1,384,1024]{2,1,0:T(8,128)(2,1)S(1)}, f32[16,512]{1,0:T(8,128)S(1)}, bf16[256,1920]{1,0:T(8,128)(2,1)S(1)}, bf16[256,1920]{1,0:T(8,128)(2,1)S(1)}) custom-call(s32[2]{0:T(128)S(1)} %pad_add_fusion.refs_0_.place, s32[8,1024]{1,0:T(8,128)S(1)} %get-tuple-element.106.refs_0_.refs_2_.cells_ref, ...), custom_call_target="tpu_custom_call" | custom-call | flops 5000000000 | bytes 8000000 | tf_op jit(solution)/shard_map/backward_attention/pallas_call | solution.py:571
  50.4 2.4 %collective-permute-done.9 = bf16[256,1920]{1,0:T(8,128)(2,1)S(1)} collective-permute-done((bf16[256,1920]{1,0:T(8,128)(2,1)S(1)}, bf16[256,1920]{1,0:T(8,128)(2,1)S(1)}, u32[]{:S(2)}, u32[]{:S(2)}) %collective-permute-start.9) | collective-permute-done | bytes 983072 | tf_op jit(solution)/shard_map/ppermute | solution.py:702
  54.5 12.6 %backward_attention.3 = (bf16[3,384,1024]{2,1,0:T(8,128)(2,1)S(1)}, f32[16,512]{1,0:T(8,128)}, bf16[256,1280]{1,0:T(8,128)(2,1)S(1)}, bf16[256,1280]{1,0:T(8,128)(2,1)S(1)}) custom-call(s32[2]{0:T(128)S(1)} %pad_add_fusion.refs_0_.place, s32[8,1024]{1,0:T(8,128)S(1)} %get-tuple-element.106.refs_0_.refs_2_.cells_ref, ...), custom_call_target="tpu_custom_call" | custom-call | flops 15000000512 | bytes 8000000 | tf_op jit(solution)/shard_map/backward_attention/pallas_call | solution.py:571
  67.1 2.0 %input_gradient.1.grad_ref = f32[1024,512]{1,0:T(8,128)S(1)} custom-call(bf16[512,768]{1,0:T(8,128)(2,1)S(1)} %get-tuple-element.109.w_a, bf16[512,768]{1,0:T(8,128)(2,1)S(1)} %get-tuple-element.120.w_b, f32[1024,512]{1,0:T(8,128)S(1)} %get-tuple-element.132.dh1_ref, bf16[1,384,1024]{2,1,0:T(8,128)(2,1)S(1)} %get-tuple-element.138.trio_a, ...), custom_call_target="tpu_custom_call" | custom-call | flops 1 | bytes 1 | tf_op jit(solution)/shard_map/input_gradient/pallas_call | solution.py:596
  71.7 3.2 %turn_back.1 = (f32[1024,512]{1,0:T(8,128)}, bf16[1024,512]{1,0:T(8,128)(2,1)}) custom-call(s32[1]{0:T(128)} %get-tuple-element.104.start, f32[1024,512]{1,0:T(8,128)S(1)} %input_gradient.1.grad_ref, bf16[1024,512]{1,0:T(8,128)(2,1)S(1)} %get-tuple-element.143.mixed_ref, bf16[128,1280]{1,0:T(8,128)(2,1)S(1)} %get-tuple-element.186.refs_0_), custom_call_target="tpu_custom_call" | custom-call | flops 1 | bytes 1 | tf_op jit(solution)/shard_map/turn_back/pallas_call | solution.py:228
  74.9 2.7 %collective-permute-done.12 = bf16[64,1920]{1,0:T(8,128)(2,1)S(1)} collective-permute-done((bf16[64,1920]{1,0:T(8,128)(2,1)S(1)}, bf16[64,1920]{1,0:T(8,128)(2,1)S(1)}, u32[]{:S(2)}, u32[]{:S(2)}) %collective-permute-start.12) | collective-permute-done | bytes 245792 | tf_op jit(solution)/shard_map/ppermute | solution.py:702
  82.9 2.7 %collective-permute-start.15 = (bf16[16,1920]{1,0:T(8,128)(2,1)S(1)}, bf16[16,1920]{1,0:T(8,128)(2,1)S(1)}, u32[]{:S(2)}, u32[]{:S(2)}) collective-permute-start(bf16[16,1920]{1,0:T(8,128)(2,1)S(1)} %add_convert_fusion.13), channel_id=1, source_target_pairs={{0,16},{4,20},{8,24},{12,28},{16,0},{20,4},{24,8},{28,12},{1,17},{... | collective-permute-start | bytes 184328 | tf_op jit(solution)/shard_map/ppermute | solution.py:702
  86.6 1.6 %collective-permute-start.18 = (bf16[32,1280]{1,0:T(8,128)(2,1)S(1)}, bf16[32,1280]{1,0:T(8,128)(2,1)S(1)}, u32[]{:S(2)}, u32[]{:S(2)}) collective-permute-start(bf16[32,1280]{1,0:T(8,128)(2,1)S(1)} %get-tuple-element.194), channel_id=1, source_target_pairs={{0,8},{4,12},{8,0},{12,4},{16,24},{20,28},{24,16},{28,20},{1,9},{5... | collective-permute-start | bytes 245768 | tf_op jit(solution)/shard_map/ppermute | solution.py:702
  88.2 3.0 %collective-permute-start.17 = (bf16[16,1920]{1,0:T(8,128)(2,1)S(1)}, bf16[16,1920]{1,0:T(8,128)(2,1)S(1)}, u32[]{:S(2)}, u32[]{:S(2)}) collective-permute-start(bf16[16,1920]{1,0:T(8,128)(2,1)S(1)} %add_convert_fusion.12), channel_id=1, source_target_pairs={{0,16},{4,20},{8,24},{12,28},{16,0},{20,4},{24,8},{28,12},{1,17},{... | collective-permute-start | bytes 184328 | tf_op jit(solution)/shard_map/ppermute | solution.py:702
  91.6 2.2 %collective-permute-start.20 = (bf16[16,1280]{1,0:T(8,128)(2,1)S(1)}, bf16[16,1280]{1,0:T(8,128)(2,1)S(1)}, u32[]{:S(2)}, u32[]{:S(2)}) collective-permute-start(bf16[16,1280]{1,0:T(8,128)(2,1)S(1)} %get-tuple-element.196), channel_id=1, source_target_pairs={{0,16},{4,20},{8,24},{12,28},{16,0},{20,4},{24,8},{28,12},{1,17},{... | collective-permute-start | bytes 122888 | tf_op jit(solution)/shard_map/ppermute | solution.py:702
  93.8 2.2 %collective-permute-start.19 = (bf16[32,1920]{1,0:T(8,128)(2,1)S(1)}, bf16[32,1920]{1,0:T(8,128)(2,1)S(1)}, u32[]{:S(2)}, u32[]{:S(2)}) collective-permute-start(bf16[32,1920]{1,0:T(8,128)(2,1)S(1)} %pad_maximum_fusion.2), channel_id=1, source_target_pairs={{0,8},{4,12},{8,0},{12,4},{16,24},{20,28},{24,16},{28,20},{1,9},{5... | collective-permute-start | bytes 368648 | tf_op jit(solution)/shard_map/ppermute | solution.py:702
  96.5 2.2 %collective-permute-start.21 = (bf16[16,1152]{1,0:T(8,128)(2,1)S(1)}, bf16[16,1152]{1,0:T(8,128)(2,1)S(1)}, u32[]{:S(2)}, u32[]{:S(2)}) collective-permute-start(bf16[16,1152]{1,0:T(8,128)(2,1)S(1)} %add_convert_fusion.17), channel_id=1, source_target_pairs={{0,16},{4,20},{8,24},{12,28},{16,0},{20,4},{24,8},{28,12},{1,17},{... | collective-permute-start | bytes 110600 | tf_op jit(solution)/shard_map/ppermute | solution.py:702
  98.8 2.6 %collective-permute-done.21 = bf16[16,1152]{1,0:T(8,128)(2,1)S(1)} collective-permute-done((bf16[16,1152]{1,0:T(8,128)(2,1)S(1)}, bf16[16,1152]{1,0:T(8,128)(2,1)S(1)}, u32[]{:S(2)}, u32[]{:S(2)}) %collective-permute-start.21) | collective-permute-done | bytes 36896 | tf_op jit(solution)/shard_map/ppermute | solution.py:702
  101.5 2.1 %collective-permute-start.22 = (bf16[32,1152]{1,0:T(8,128)(2,1)S(1)}, bf16[32,1152]{1,0:T(8,128)(2,1)S(1)}, u32[]{:S(2)}, u32[]{:S(2)}) collective-permute-start(bf16[32,1152]{1,0:T(8,128)(2,1)S(1)} %pad_maximum_fusion.3), channel_id=1, source_target_pairs={{0,8},{4,12},{8,0},{12,4},{16,24},{20,28},{24,16},{28,20},{1,9},{5... | collective-permute-start | bytes 221192 | tf_op jit(solution)/shard_map/ppermute | solution.py:702
  111.8 2.7 %collective-permute-done.26 = f32[8,128]{1,0:T(8,128)S(1)} collective-permute-done((f32[8,128]{1,0:T(8,128)S(1)}, f32[8,128]{1,0:T(8,128)S(1)}, u32[]{:S(2)}, u32[]{:S(2)}) %collective-permute-start.26) | collective-permute-done | bytes 4128 | tf_op jit(solution)/shard_map/ppermute | solution.py:702
  114.6 4.2 %adam.1 = (f32[128,1536]{1,0:T(8,128)}, f32[128,512]{1,0:T(8,128)}, f32[128,512]{1,0:T(8,128)}, f32[128,512]{1,0:T(8,128)}, f32[9,128]{1,0:T(8,128)}, /*index=5*...) custom-call(s32[2]{0:T(128)S(1)} %pad_add_fusion.refs_0_.place, ...), custom_call_target="tpu_custom_call" | custom-call | tf_op jit(solution)/shard_map/adam/pallas_call | solution.py:689
  (109 shorter events, 30.1 us)
Async XLA Ops:
  2.6 8.7 %collective-permute-start.1 = (bf16[144,768]{1,0:T(8,128)(2,1)}, bf16[144,768]{1,0:T(8,128)(2,1)S(1)}, u32[]{:S(2)}, u32[]{:S(2)}) collective-permute-start(bf16[144,768]{1,0:T(8,128)(2,1)} %pack_first.1.refs_4_), channel_id=1, source_target_pairs={{0,2},{1,3},{2,0},{3,1},{4,6},{5,7},{6,4},{7,5},{8,10},{9,11},{10,... | collective-permute-start | bytes 663560 | tf_op jit(solution)/shard_map/ppermute | solution.py:702
  5.6 8.0 %collective-permute-start = (bf16[144,768]{1,0:T(8,128)(2,1)}, bf16[144,768]{1,0:T(8,128)(2,1)}, u32[]{:S(2)}, u32[]{:S(2)}) collective-permute-start(bf16[144,768]{1,0:T(8,128)(2,1)} %pack_first.1.refs_4_), channel_id=1, source_target_pairs={{0,1},{1,0},{2,3},{3,2},{4,5},{5,4},{6,7},{7,6},{8,9},{9,8},{10,11... | collective-permute-start | bytes 663560 | tf_op jit(solution)/shard_map/ppermute | solution.py:702
  11.3 10.3 %collective-permute-start.3 = (bf16[128,768]{1,0:T(8,128)(2,1)}, bf16[128,768]{1,0:T(8,128)(2,1)}, u32[]{:S(2)}, u32[]{:S(2)}) collective-permute-start(bf16[128,768]{1,0:T(8,128)(2,1)} %get-tuple-element.118.refs_4_), channel_id=1, source_target_pairs={{0,1},{1,0},{2,3},{3,2},{4,5},{5,4},{6,7},{7,6},{8,9},{9,8},{10,11... | collective-permute-start | bytes 589832 | tf_op jit(solution)/shard_map/ppermute | solution.py:702
  11.9 9.1 %collective-permute-start.4 = (bf16[128,768]{1,0:T(8,128)(2,1)}, bf16[128,768]{1,0:T(8,128)(2,1)S(1)}, u32[]{:S(2)}, u32[]{:S(2)}) collective-permute-start(bf16[128,768]{1,0:T(8,128)(2,1)} %get-tuple-element.118.refs_4_), channel_id=1, source_target_pairs={{0,2},{1,3},{2,0},{3,1},{4,6},{5,7},{6,4},{7,5},{8,10},{9,11},{10,... | collective-permute-start | bytes 589832 | tf_op jit(solution)/shard_map/ppermute | solution.py:702
  21.1 11.6 %collective-permute-start.6 = (bf16[128,1536]{1,0:T(8,128)(2,1)S(1)}, bf16[128,1536]{1,0:T(8,128)(2,1)S(1)}, u32[]{:S(2)}, u32[]{:S(2)}) collective-permute-start(bf16[128,1536]{1,0:T(8,128)(2,1)S(1)} %get-tuple-element.130.refs_6_), channel_id=1, source_target_pairs={{0,1},{1,0},{2,3},{3,2},{4,5},{5,4},{6,7},{7,6},{8,9},{9,8},{10,11... | collective-permute-start | bytes 1179656 | tf_op jit(solution)/shard_map/ppermute | solution.py:702
  21.6 11.1 %collective-permute-start.7 = (bf16[128,1536]{1,0:T(8,128)(2,1)S(1)}, bf16[128,1536]{1,0:T(8,128)(2,1)S(1)}, u32[]{:S(2)}, u32[]{:S(2)}) collective-permute-start(bf16[128,1536]{1,0:T(8,128)(2,1)S(1)} %get-tuple-element.130.refs_6_), channel_id=1, source_target_pairs={{0,2},{1,3},{2,0},{3,1},{4,6},{5,7},{6,4},{7,5},{8,10},{9,11},{10,... | collective-permute-start | bytes 1179656 | tf_op jit(solution)/shard_map/ppermute | solution.py:702
  53.1 16.0 %collective-permute-start.11 = (bf16[128,1920]{1,0:T(8,128)(2,1)S(1)}, bf16[128,1920]{1,0:T(8,128)(2,1)S(1)}, u32[]{:S(2)}, u32[]{:S(2)}) collective-permute-start(bf16[128,1920]{1,0:T(8,128)(2,1)S(1)} %get-tuple-element.184.refs_12_), channel_id=1, source_target_pairs={{0,2},{1,3},{2,0},{3,1},{4,6},{5,7},{6,4},{7,5},{8,10},{9,11},{10,... | collective-permute-start | bytes 1474568 | tf_op jit(solution)/shard_map/ppermute | solution.py:702
  67.1 3.7 %collective-permute-start.10 = (bf16[256,1280]{1,0:T(8,128)(2,1)S(1)}, bf16[256,1280]{1,0:T(8,128)(2,1)S(1)}, u32[]{:S(2)}, u32[]{:S(2)}) collective-permute-start(bf16[256,1280]{1,0:T(8,128)(2,1)S(1)} %get-tuple-element.145), channel_id=1, source_target_pairs={{0,1},{1,0},{2,3},{3,2},{4,5},{5,4},{6,7},{7,6},{8,9},{9,8},{10,11... | collective-permute-start | bytes 1966088 | tf_op jit(solution)/shard_map/ppermute | solution.py:702
  69.2 8.4 %collective-permute-start.12 = (bf16[64,1920]{1,0:T(8,128)(2,1)S(1)}, bf16[64,1920]{1,0:T(8,128)(2,1)S(1)}, u32[]{:S(2)}, u32[]{:S(2)}) collective-permute-start(bf16[64,1920]{1,0:T(8,128)(2,1)S(1)} %get-tuple-element.188), channel_id=1, source_target_pairs={{0,4},{4,0},{8,12},{12,8},{16,20},{20,16},{24,28},{28,24},{1,5},{5... | collective-permute-start | bytes 737288 | tf_op jit(solution)/shard_map/ppermute | solution.py:702
  71.0 9.9 %collective-permute-start.14 = (bf16[128,1280]{1,0:T(8,128)(2,1)S(1)}, bf16[128,1280]{1,0:T(8,128)(2,1)S(1)}, u32[]{:S(2)}, u32[]{:S(2)}) collective-permute-start(bf16[128,1280]{1,0:T(8,128)(2,1)S(1)} %get-tuple-element.186.refs_0_), channel_id=1, source_target_pairs={{0,2},{1,3},{2,0},{3,1},{4,6},{5,7},{6,4},{7,5},{8,10},{9,11},{10,... | collective-permute-start | bytes 983048 | tf_op jit(solution)/shard_map/ppermute | solution.py:702
  77.9 5.0 %collective-permute-start.13 = (bf16[32,1920]{1,0:T(8,128)(2,1)S(1)}, bf16[32,1920]{1,0:T(8,128)(2,1)S(1)}, u32[]{:S(2)}, u32[]{:S(2)}) collective-permute-start(bf16[32,1920]{1,0:T(8,128)(2,1)S(1)} %get-tuple-element.191), channel_id=1, source_target_pairs={{0,8},{4,12},{8,0},{12,4},{16,24},{20,28},{24,16},{28,20},{1,9},{5... | collective-permute-start | bytes 368648 | tf_op jit(solution)/shard_map/ppermute | solution.py:702
  80.9 5.6 %collective-permute-start.16 = (bf16[64,1280]{1,0:T(8,128)(2,1)S(1)}, bf16[64,1280]{1,0:T(8,128)(2,1)S(1)}, u32[]{:S(2)}, u32[]{:S(2)}) collective-permute-start(bf16[64,1280]{1,0:T(8,128)(2,1)S(1)} %get-tuple-element.190), channel_id=1, source_target_pairs={{0,4},{4,0},{8,12},{12,8},{16,20},{20,16},{24,28},{28,24},{1,5},{5... | collective-permute-start | bytes 491528 | tf_op jit(solution)/shard_map/ppermute | solution.py:702
  82.9 5.3 %collective-permute-start.15 = (bf16[16,1920]{1,0:T(8,128)(2,1)S(1)}, bf16[16,1920]{1,0:T(8,128)(2,1)S(1)}, u32[]{:S(2)}, u32[]{:S(2)}) collective-permute-start(bf16[16,1920]{1,0:T(8,128)(2,1)S(1)} %add_convert_fusion.13), channel_id=1, source_target_pairs={{0,16},{4,20},{8,24},{12,28},{16,0},{20,4},{24,8},{28,12},{1,17},{... | collective-permute-start | bytes 184328 | tf_op jit(solution)/shard_map/ppermute | solution.py:702
  86.6 5.0 %collective-permute-start.18 = (bf16[32,1280]{1,0:T(8,128)(2,1)S(1)}, bf16[32,1280]{1,0:T(8,128)(2,1)S(1)}, u32[]{:S(2)}, u32[]{:S(2)}) collective-permute-start(bf16[32,1280]{1,0:T(8,128)(2,1)S(1)} %get-tuple-element.194), channel_id=1, source_target_pairs={{0,8},{4,12},{8,0},{12,4},{16,24},{20,28},{24,16},{28,20},{1,9},{5... | collective-permute-start | bytes 245768 | tf_op jit(solution)/shard_map/ppermute | solution.py:702
  88.2 5.5 %collective-permute-start.17 = (bf16[16,1920]{1,0:T(8,128)(2,1)S(1)}, bf16[16,1920]{1,0:T(8,128)(2,1)S(1)}, u32[]{:S(2)}, u32[]{:S(2)}) collective-permute-start(bf16[16,1920]{1,0:T(8,128)(2,1)S(1)} %add_convert_fusion.12), channel_id=1, source_target_pairs={{0,16},{4,20},{8,24},{12,28},{16,0},{20,4},{24,8},{28,12},{1,17},{... | collective-permute-start | bytes 184328 | tf_op jit(solution)/shard_map/ppermute | solution.py:702
  91.6 5.0 %collective-permute-start.20 = (bf16[16,1280]{1,0:T(8,128)(2,1)S(1)}, bf16[16,1280]{1,0:T(8,128)(2,1)S(1)}, u32[]{:S(2)}, u32[]{:S(2)}) collective-permute-start(bf16[16,1280]{1,0:T(8,128)(2,1)S(1)} %get-tuple-element.196), channel_id=1, source_target_pairs={{0,16},{4,20},{8,24},{12,28},{16,0},{20,4},{24,8},{28,12},{1,17},{... | collective-permute-start | bytes 122888 | tf_op jit(solution)/shard_map/ppermute | solution.py:702
  93.8 5.0 %collective-permute-start.19 = (bf16[32,1920]{1,0:T(8,128)(2,1)S(1)}, bf16[32,1920]{1,0:T(8,128)(2,1)S(1)}, u32[]{:S(2)}, u32[]{:S(2)}) collective-permute-start(bf16[32,1920]{1,0:T(8,128)(2,1)S(1)} %pad_maximum_fusion.2), channel_id=1, source_target_pairs={{0,8},{4,12},{8,0},{12,4},{16,24},{20,28},{24,16},{28,20},{1,9},{5... | collective-permute-start | bytes 368648 | tf_op jit(solution)/shard_map/ppermute | solution.py:702
  96.5 4.9 %collective-permute-start.21 = (bf16[16,1152]{1,0:T(8,128)(2,1)S(1)}, bf16[16,1152]{1,0:T(8,128)(2,1)S(1)}, u32[]{:S(2)}, u32[]{:S(2)}) collective-permute-start(bf16[16,1152]{1,0:T(8,128)(2,1)S(1)} %add_convert_fusion.17), channel_id=1, source_target_pairs={{0,16},{4,20},{8,24},{12,28},{16,0},{20,4},{24,8},{28,12},{1,17},{... | collective-permute-start | bytes 110600 | tf_op jit(solution)/shard_map/ppermute | solution.py:702
  101.5 4.4 %collective-permute-start.22 = (bf16[32,1152]{1,0:T(8,128)(2,1)S(1)}, bf16[32,1152]{1,0:T(8,128)(2,1)S(1)}, u32[]{:S(2)}, u32[]{:S(2)}) collective-permute-start(bf16[32,1152]{1,0:T(8,128)(2,1)S(1)} %pad_maximum_fusion.3), channel_id=1, source_target_pairs={{0,8},{4,12},{8,0},{12,4},{16,24},{20,28},{24,16},{28,20},{1,9},{5... | collective-permute-start | bytes 221192 | tf_op jit(solution)/shard_map/ppermute | solution.py:702
  103.6 10.9 %collective-permute-start.27 = (bf16[64,1920]{1,0:T(8,128)(2,1)S(1)}, bf16[64,1920]{1,0:T(8,128)(2,1)S(1)}, u32[]{:S(2)}, u32[]{:S(2)}) collective-permute-start(bf16[64,1920]{1,0:T(8,128)(2,1)S(1)} %pad_maximum_fusion.early.refs_0_), channel_id=1, source_target_pairs={{0,4},{4,0},{8,12},{12,8},{16,20},{20,16},{24,28},{28,24},{1,5},{5... | collective-permute-start | bytes 737288 | tf_op jit(solution)/shard_map/ppermute | solution.py:702
  106.7 3.2 %collective-permute-start.25 = (f32[8,128]{1,0:T(8,128)S(1)}, f32[8,128]{1,0:T(8,128)S(1)}, u32[]{:S(2)}, u32[]{:S(2)}) collective-permute-start(f32[8,128]{1,0:T(8,128)S(1)} %half_squares.1), channel_id=1, source_target_pairs={{0,3},{1,2},{2,1},{3,0},{4,7},{5,6},{6,5},{7,4},{8,11},{9,10},{10,... | collective-permute-start | bytes 12296 | tf_op jit(solution)/shard_map/ppermute | solution.py:702
  106.8 3.7 %collective-permute-start.24 = (f32[8,128]{1,0:T(8,128)S(1)}, f32[8,128]{1,0:T(8,128)S(1)}, u32[]{:S(2)}, u32[]{:S(2)}) collective-permute-start(f32[8,128]{1,0:T(8,128)S(1)} %half_squares.1), channel_id=1, source_target_pairs={{0,2},{1,3},{2,0},{3,1},{4,6},{5,7},{6,4},{7,5},{8,10},{9,11},{10,... | collective-permute-start | bytes 12296 | tf_op jit(solution)/shard_map/ppermute | solution.py:702
  108.6 5.9 %collective-permute-start.28 = (bf16[64,1152]{1,0:T(8,128)(2,1)S(1)}, bf16[64,1152]{1,0:T(8,128)(2,1)S(1)}, u32[]{:S(2)}, u32[]{:S(2)}) collective-permute-start(bf16[64,1152]{1,0:T(8,128)(2,1)S(1)} %pad_maximum_fusion.1.late.refs_2_), channel_id=1, source_target_pairs={{0,4},{4,0},{8,12},{12,8},{16,20},{20,16},{24,28},{28,24},{1,5},{5... | collective-permute-start | bytes 442376 | tf_op jit(solution)/shard_map/ppermute | solution.py:702
  110.4 4.0 %collective-permute-start.26 = (f32[8,128]{1,0:T(8,128)S(1)}, f32[8,128]{1,0:T(8,128)S(1)}, u32[]{:S(2)}, u32[]{:S(2)}) collective-permute-start(f32[8,128]{1,0:T(8,128)S(1)} %add_add_fusion), channel_id=1, source_target_pairs={{0,4},{4,0},{8,12},{12,8},{16,20},{20,16},{24,28},{28,24},{1,5},{5... | collective-permute-start | bytes 12296 | tf_op jit(solution)/shard_map/ppermute | solution.py:702
  (26 other events, 475.4 us)

commit v3 on v2

--- a/solution.py
+++ b/solution.py
@@ -36,7 +36,6 @@
 NN = (((1,), (0,)), ((), ()))
 NT = (((1,), (1,)), ((), ()))
 TN = (((0,), (0,)), ((), ()))
-TT = (((0,), (1,)), ((), ()))
 
 
 def dot(a, b, dims):
@@ -216,25 +215,28 @@
     )(start, cot, *later)
 
 
-def turn_back_kernel(start, grad_ref, mixed_ref, *refs):
-    grad_out, mixed_out, wide_mixed = refs[-3:]
+def turn_back_kernel(start, source, *refs):
+    turned, wide_source = refs[-2:]
     back = (TOK_DEV - start[0]) & (TOK_DEV - 1)
-    wide_mixed[...] = mixed_ref[...].astype(F32)
-    turn_rows(wide_mixed, back, write_into(mixed_out))
-    turn_rows(grad_ref, back, write_into(grad_out))
-
-
-def turn_back(start, grad, mixed, later):
+    if source.dtype == F32:
+        turn_rows(source, back, write_into(turned))
+    else:
+        wide_source[...] = source[...].astype(F32)
+        turn_rows(wide_source, back, write_into(turned))
+
+
+def turn_back(start, value, later):
+    scratch = (8, PAIR) if value.dtype == F32 else value.shape
     return pl.pallas_call(
         turn_back_kernel,
-        in_specs=[SMEM, VM, VM] + [ANY] * len(later),
-        out_specs=[VM, VM],
-        out_shape=[sds(grad.shape, F32), sds(mixed.shape, BF)],
-        scratch_shapes=[pltpu.VMEM(mixed.shape, F32)],
+        in_specs=[SMEM, VM] + [ANY] * len(later),
+        out_specs=VM,
+        out_shape=sds(value.shape, value.dtype),
+        scratch_shapes=[pltpu.VMEM(scratch, F32)],
         compiler_params=params(),
         cost_estimate=cost(1, 1),
         name="turn_back",
-    )(start, grad, mixed, *later)
+    )(start, value, *later)
 
 
 def make_bias(cells_ref, bias):
@@ -268,9 +270,11 @@
 
 
 def forward_kernel(order, n_pieces, base, *refs):
-    place, tokens, cells_ref, vec_in = refs[:4]
-    pieces = refs[4 : 4 + n_pieces]
-    att_out, lse_out, krow_out, vrow_out, qt_out, kt_out, w_full, vec_full, bias = refs[4 + n_pieces :]
+    place, tokens, tokens_t, cells_ref, vec_in = refs[:5]
+    pieces = refs[5 : 5 + n_pieces]
+    att_out, lse_out, krow_out, vrow_out, qt_out, kt_out, w_full, vec_full, tokens_out, bias = refs[
+        5 + n_pieces :
+    ]
     assemble(order, pieces, place, w_full)
     if vec_in.shape[1] == D:
         vec_full[...] = vec_in[...].astype(F32)
@@ -283,6 +287,7 @@
             ].astype(F32)
     make_bias(cells_ref, bias)
     x = tokens[...]
+    tokens_out[...] = x
     halves = [slice(0, HALF), slice(HALF, TOK_DEV)]
     chains = []
     for local in range(GROUP):
@@ -290,7 +295,7 @@
         w = w_full[:, local * TRIO : (local + 1) * TRIO]
         b_q = vec_full[0:1, lane]
         b_v = vec_full[1:2, lane]
-        trio = dot(w, x, TT)
+        trio = dot(w, tokens_t[...], TN)
         rows = dot(x, w[:, PAIR:], NN)
         here = slice(local * PAIR, (local + 1) * PAIR)
         q_t = ((trio[:PAIR] + column_of(b_q)) * (HEAD_DIM**-0.5)).astype(BF)
@@ -319,20 +324,21 @@
             lse_out[local, h : h + 1, mine] = lse[:, cols]
 
 
-def forward_attention(base, place, tokens, cells, vec, pieces, order):
+def forward_attention(base, place, tokens, tokens_t, cells, vec, pieces, order):
     wide_t, tall = sds((GROUP * PAIR, TOK_DEV), BF), sds((GROUP, TOK_DEV, PAIR), BF)
     return pl.pallas_call(
         functools.partial(forward_kernel, order, len(pieces), base),
-        in_specs=[SMEM] + [VM] * (3 + len(pieces)),
-        out_specs=[VM] * 8,
+        in_specs=[SMEM] + [VM] * (4 + len(pieces)),
+        out_specs=[VM] * 9,
         out_shape=[
-            wide_t, sds((GROUP, 8, TOK_DEV), F32), tall, tall, wide_t, wide_t, sds((D, HW), BF), sds((16, D), F32)
+            wide_t, sds((GROUP, 8, TOK_DEV), F32), tall, tall, wide_t, wide_t, sds((D, HW), BF), sds((16, D), F32),
+            sds((TOK_DEV, D), BF),
         ],
         scratch_shapes=[pltpu.VMEM((TOK_DEV, HALF), F32)],
         compiler_params=params(FORWARD_MIB),
         cost_estimate=cost(6e9, 8e6, 2**21),
         name="forward_attention",
-    )(place, tokens, cells, vec, *pieces)
+    )(place, tokens, tokens_t, cells, vec, *pieces)
 
 
 def normalize(value):
@@ -787,6 +793,8 @@
         pieces_a = [low_a, swap(low_a, "narrow", 1), y_a, swap(y_a, "narrow", 1)]
         y_b = swap(after(low_b, y_a), "narrow", 2)
         c_b = swap(low_b, "narrow", 1)
+        y_rest = swap(after(low_rest, y_a), "narrow", 2)
+        c_rest = swap(low_rest, "narrow", 1)
         order = [(j, None, j) for j in range(4)]
         vec = jnp.zeros((8, PAIR), BF)
     else:
@@ -796,17 +804,20 @@
         vec = lax.all_gather(vectors.astype(BF), "narrow", axis=1, tiled=True)
         vec = jnp.pad(vec, ((0, 7), (0, 0)))
 
-    *saved_a, w_a, vec_full = forward_attention(0, place, tokens, cells, vec, pieces_a, order)
+    *saved_a, w_a, vec_full, tokens = forward_attention(
+        0, place, tokens, tokens_t, cells, vec, pieces_a, order
+    )
     if quick:
         y_b, c_b = after(y_b, saved_a), after(c_b, saved_a)
-        pieces_b = [low_b, c_b, y_b, swap(y_b, "narrow", 1)]
-        y_rest = swap(after(low_rest, y_b), "narrow", 2)
-        c_rest = swap(low_rest, "narrow", 1)
-    *saved_b, w_b, vec_full = forward_attention(GROUP, place, tokens, cells, vec_full, pieces_b, order)
+        y_rest = after(y_rest, y_b)
+        d_rest = swap(y_rest, "narrow", 1)
+        pieces_b = [low_b, c_b, y_b, after(swap(y_b, "narrow", 1), y_rest)]
+    *saved_b, w_b, vec_full, tokens = forward_attention(
+        GROUP, place, tokens, tokens_t, cells, vec_full, pieces_b, order
+    )
     cotangent = turn_cotangent(start, cotangent, [saved_b[0]])
     if quick:
-        y_rest, c_rest = after(y_rest, (saved_b, cotangent)), after(c_rest, saved_b)
-        pieces_rest = [low_rest, c_rest, y_rest, swap(y_rest, "narrow", 1)]
+        pieces_rest = [low_rest, *after((c_rest, y_rest, d_rest), cotangent)]
     mixed, d_h1, d_t, vec_sums, *g_rest = middle(
         place, tokens, cotangent, (saved_a[0], saved_b[0]), vec_full, pieces_rest, order, stages
     )
@@ -818,7 +829,8 @@
     later = []
     if quick:
         e_keep, e_send = early
-        e_keep, e_send = fold(e_keep, swap(e_send, "narrow", 1))
+        mixed = turn_back(start, mixed, [trio_a])
+        e_keep, e_send = fold(e_keep, after(swap(e_send, "narrow", 1), mixed))
         e_arrived = swap(e_send, "narrow", 2)
         later = [e_send]
     trio_b, vec_sums, *late = backward_attention(
@@ -829,33 +841,33 @@
     if quick:
         b_keep, b_send = late
         b_arrived = swap(b_send, "narrow", 1)
-        turned_grad = input_gradient(weights, d_h1, trios, [])
-        e_keep, e_send = fold(e_keep, after(e_arrived, turned_grad))
+        e_keep, e_send = fold(e_keep, after(e_arrived, trio_b))
         e_arrived = swap(e_send, "wide", 1)
         b_keep, b_send = fold(b_keep, after(b_arrived, e_send))
         b_arrived = swap(b_send, "narrow", 2)
-        input_grad, mixed = turn_back(start, turned_grad, mixed, [b_send])
-        e_keep, e_send = fold(e_keep, after(e_arrived, input_grad))
+        turned_grad = input_gradient(weights, d_h1, trios, [b_send])
+        input_grad = turn_back(start, turned_grad, [])
+        b_keep, b_send = fold(b_keep, after(b_arrived, input_grad))
+        b_arrived = swap(b_send, "wide", 1)
+        e_keep, e_send = fold(e_keep, after(e_arrived, b_send))
         e_arrived = swap(e_send, "wide", 2)
         b_keep, b_send = fold(b_keep, after(b_arrived, e_send))
-        b_arrived = swap(b_send, "wide", 1)
+        b_arrived = swap(b_send, "wide", 2)
         e_keep, e_send = fold(e_keep, after(e_arrived, b_send))
         e_arrived = swap(e_send, "wide", 4)
         b_keep, b_send = fold(b_keep, after(b_arrived, e_send))
-        b_arrived = swap(b_send, "wide", 2)
+        b_arrived = swap(b_send, "wide", 4)
         e_low = add_low(e_keep, after(e_arrived, b_send))
         e_arrived = swap(e_low, "wide", 4)
-        b_keep, b_send = fold(b_keep, after(b_arrived, e_low))
-        b_arrived = swap(b_send, "wide", 4)
-        e_low = join(e_low, after(e_arrived, b_send))
-        e_arrived = swap(e_low, "wide", 2)
-        b_arrived = after(b_arrived, e_low)
         vec_total = b_keep[:, LATE:].astype(F32) + b_arrived[:, LATE:].astype(F32)
         b_low = add_low(b_keep[:, :LATE], b_arrived[:, :LATE])
         b_arrived = swap(b_low, "wide", 4)
         e_low = join(e_low, after(e_arrived, b_low))
+        e_arrived = swap(e_low, "wide", 2)
         b_low = join(b_low, after(b_arrived, e_low))
-        b_low = join(b_low, swap(b_low, "wide", 2))
+        b_arrived = swap(b_low, "wide", 2)
+        e_low = join(e_low, after(e_arrived, b_low))
+        b_low = join(b_low, after(b_arrived, e_low))
         e_arrived, b_arrived = swap(e_low, "wide", 1), swap(b_low, "wide", 1)
         squares = half_squares(place, e_low, b_low, vec_total)
         squares = four(squares, directly(squares, "narrow", (1, 2, 3)))
@@ -863,7 +875,7 @@
         grads = [e_low, after(e_arrived, squares), b_low, after(b_arrived, squares)]
     else:
         turned_grad = input_gradient(weights, d_h1, trios, [])
-        input_grad, mixed = turn_back(start, turned_grad, mixed, [])
+        input_grad, mixed = turn_back(start, turned_grad, []), turn_back(start, mixed, [])
         vec_total = lax.psum_scatter(vec_sums, "narrow", scatter_dimension=1, tiled=True)
         vec_total = lax.psum(vec_total, "wide")
         grads = []

time: 119 us -> 120 us (level)
  Pallas kernels: 55.8 us -> 57.5 us
  starting transfers between devices: 34.7 us -> 33.1 us
    ppermute x29, starting transfers between devices: 34.7 us -> 33.1 us  [swap(): return lax.ppermute(value, axis, [(i, i ^ mask) for i in range(size)])]
    pallas_call x1 -> x2, Pallas kernels: 3.23 us -> 4.73 us  [turn_back(): pl.pallas_call(turn_back_kernel, in_specs=[SMEM, VM] + [ANY] * len(later)...]
    unnamed x42 -> x40, local copies, waits for them, and re-layouts: 3.5 us -> 3.49 us
  transfers between devices with their start and end apart: 29 -> 29, of which waited for: 15 -> 14; matrix products, arithmetic and copies ran while one was open for 1% -> 1% of each run, Pallas kernels for 28% -> 30%
where the time goes in v3:
time: 120 us; the launch traced here: 119 us
  Pallas kernels  57.5 us (48%)
  starting transfers between devices  33.1 us (28%)
  waiting for transfers between devices  22.2 us (18%)
  local copies, waits for them, and re-layouts  3.49 us (3%)
  other arithmetic  1.62 us (1%)
  between operations  1.28 us (1%)
    ppermute x29, starting transfers between devices, swap(): return lax.ppermute(value, axis, [(i, i ^ mask) for i in range(size)])  33.1 us
    ppermute x29, waiting for transfers between devices, swap(): return lax.ppermute(value, axis, [(i, i ^ mask) for i in range(size)])  22.2 us
    pallas_call x2, Pallas kernels, backward_attention(): pl.pallas_call(functools.partial(backward_kernel, n_shards, stages, plan,...  17 us
    pallas_call x2, Pallas kernels, forward_attention(): pl.pallas_call(functools.partial(forward_kernel, order, len(pieces), base...  12.3 us
    pallas_call x1, Pallas kernels, middle(): pl.pallas_call(functools.partial(middle_kernel, order, len(pieces), len(o...  11.5 us
    pallas_call x2, Pallas kernels, turn_back(): pl.pallas_call(turn_back_kernel, in_specs=[SMEM, VM] + [ANY] * len(later)...  4.73 us
    pallas_call x1, Pallas kernels, adam_step(): pl.pallas_call(functools.partial(adam_kernel, quick, limit), grid=(steps,...  4.19 us
    unnamed x40, local copies, waits for them, and re-layouts  3.49 us
  transfers between devices with their start and end apart: 29, of which 14 were waited for; matrix products, arithmetic and copies ran while one was open for 1% of the time, Pallas kernels for 30%

profile of v3, /device:TPU:0, one launch (start us, length us, event | category | flops | bytes accessed | tf_op | source)
XLA Modules:
  0.0 119.3 jit_solution(10608173392833910738)
XLA Ops:
  0.7 1.9 %pack_first.1.refs_5_ = bf16[144,768]{1,0:T(8,128)(2,1)} custom-call(f32[128,1536]{1,0:T(8,128)} %refs_5_.1, f32[9,128]{1,0:T(8,128)} %refs_9_.1), custom_call_target="tpu_custom_call" | custom-call | tf_op jit(solution)/shard_map/pack_first/pallas_call | solution.py:104
  2.6 3.0 %collective-permute-start.1 = (bf16[144,768]{1,0:T(8,128)(2,1)}, bf16[144,768]{1,0:T(8,128)(2,1)S(1)}, u32[]{:S(2)}, u32[]{:S(2)}) collective-permute-start(bf16[144,768]{1,0:T(8,128)(2,1)} %pack_first.1.refs_5_), channel_id=1, source_target_pairs={{0,2},{1,3},{2,0},{3,1},{4,6},{5,7},{6,4},{7,5},{8,10},{9,11},{10,... | collective-permute-start | bytes 663560 | tf_op jit(solution)/shard_map/ppermute | solution.py:708
  11.9 1.7 %collective-permute-start.4 = (bf16[128,768]{1,0:T(8,128)(2,1)}, bf16[128,768]{1,0:T(8,128)(2,1)S(1)}, u32[]{:S(2)}, u32[]{:S(2)}) collective-permute-start(bf16[128,768]{1,0:T(8,128)(2,1)} %get-tuple-element.123.refs_5_), channel_id=1, source_target_pairs={{0,2},{1,3},{2,0},{3,1},{4,6},{5,7},{6,4},{7,5},{8,10},{9,11},{10,... | collective-permute-start | bytes 589832 | tf_op jit(solution)/shard_map/ppermute | solution.py:708
  15.1 6.1 %forward_attention.2 = (bf16[256,1024]{1,0:T(8,128)(2,1)S(1)}, f32[2,8,1024]{2,1,0:T(8,128)S(1)}, bf16[2,1024,128]{2,1,0:T(8,128)(2,1)S(1)}, bf16[2,1024,128]{2,...) custom-call(s32[2]{0:T(128)S(1)} %pad_add_fusion.refs_0_.place, ...), custom_call_target="tpu_custom_call" | custom-call | flops 6000000000 | bytes 8000000 | tf_op jit(solution)/shard_map/forward_attention/pallas_call | solution.py:329
  21.8 5.5 %collective-permute-done.6.refs_8_ = bf16[128,1536]{1,0:T(8,128)(2,1)S(1)} collective-permute-done((bf16[128,1536]{1,0:T(8,128)(2,1)S(1)}, bf16[128,1536]{1,0:T(8,128)(2,1)S(1)}, u32[]{:S(2)}, u32[]{:S(2)}) %collective-permute-start.6) | collective-permute-done | bytes 393248 | tf_op jit(solution)/shard_map/ppermute | solution.py:708
  27.3 6.2 %forward_attention.3 = (bf16[256,1024]{1,0:T(8,128)(2,1)S(1)}, f32[2,8,1024]{2,1,0:T(8,128)S(1)}, bf16[2,1024,128]{2,1,0:T(8,128)(2,1)S(1)}, bf16[2,1024,128]{2,...) custom-call(s32[2]{0:T(128)S(1)} %pad_add_fusion.refs_0_.place, ...), custom_call_target="tpu_custom_call" | custom-call | flops 6000000000 | bytes 8000000 | tf_op jit(solution)/shard_map/forward_attention/pallas_call | solution.py:329
  34.6 11.5 %middle.1 = (bf16[1024,512]{1,0:T(8,128)(2,1)S(1)}, f32[1024,512]{1,0:T(8,128)S(1)}, bf16[512,1024]{1,0:T(8,128)(2,1)S(1)}, f32[16,512]{1,0:T(8,128)S(1)}, bf16[...) custom-call(s32[2]{0:T(128)S(1)} %pad_add_fusion.refs_0_.place, ...), custom_call_target="tpu_custom_call" | custom-call | flops 10000000000 | bytes 12000000 | tf_op jit(solution)/shard_map/middle/pallas_call | solution.py:485
  46.1 4.6 %backward_attention.2 = (bf16[1,384,1024]{2,1,0:T(8,128)(2,1)S(1)}, f32[16,512]{1,0:T(8,128)S(1)}, bf16[256,1920]{1,0:T(8,128)(2,1)S(1)}, bf16[256,1920]{1,0:T(8,128)(2,1)S(1)}) custom-call(s32[2]{0:T(128)S(1)} %pad_add_fusion.refs_0_.place, s32[8,1024]{1,0:T(8,128)S(1)} %get-tuple-element.111.refs_0_.refs_3_.cells_ref, ...), custom_call_target="tpu_custom_call" | custom-call | flops 5000000000 | bytes 8000000 | tf_op jit(solution)/shard_map/backward_attention/pallas_call | solution.py:577
  51.2 2.3 %turn_back.2 = bf16[1024,512]{1,0:T(8,128)(2,1)} custom-call(s32[1]{0:T(128)} %get-tuple-element.108.start, bf16[1024,512]{1,0:T(8,128)(2,1)S(1)} %get-tuple-element.135.source, bf16[1,384,1024]{2,1,0:T(8,128)(2,1)S(1)} %get-tuple-element.145.refs_0_.trio_a), custom_call_target="tpu_custom_call" | custom-call | flops 1 | bytes 1 | tf_op jit(solution)/shard_map/turn_back/pallas_call | solution.py:230
  53.8 1.8 %collective-permute-start.11 = (bf16[128,1920]{1,0:T(8,128)(2,1)S(1)}, bf16[128,1920]{1,0:T(8,128)(2,1)S(1)}, u32[]{:S(2)}, u32[]{:S(2)}) collective-permute-start(bf16[128,1920]{1,0:T(8,128)(2,1)S(1)} %get-tuple-element.192.refs_12_), channel_id=1, source_target_pairs={{0,2},{1,3},{2,0},{3,1},{4,6},{5,7},{6,4},{7,5},{8,10},{9,11},{10,... | collective-permute-start | bytes 1474568 | tf_op jit(solution)/shard_map/ppermute | solution.py:708
  55.6 12.4 %backward_attention.3 = (bf16[3,384,1024]{2,1,0:T(8,128)(2,1)S(1)}, f32[16,512]{1,0:T(8,128)}, bf16[256,1280]{1,0:T(8,128)(2,1)S(1)}, bf16[256,1280]{1,0:T(8,128)(2,1)S(1)}) custom-call(s32[2]{0:T(128)S(1)} %pad_add_fusion.refs_0_.place, s32[8,1024]{1,0:T(8,128)S(1)} %get-tuple-element.111.refs_0_.refs_3_.cells_ref, ...), custom_call_target="tpu_custom_call" | custom-call | flops 15000000512 | bytes 8000000 | tf_op jit(solution)/shard_map/backward_attention/pallas_call | solution.py:577
  68.1 2.0 %collective-permute-done.10 = bf16[256,1280]{1,0:T(8,128)(2,1)S(1)} collective-permute-done((bf16[256,1280]{1,0:T(8,128)(2,1)S(1)}, bf16[256,1280]{1,0:T(8,128)(2,1)S(1)}, u32[]{:S(2)}, u32[]{:S(2)}) %collective-permute-start.10) | collective-permute-done | bytes 655392 | tf_op jit(solution)/shard_map/ppermute | solution.py:708
  70.6 2.3 %input_gradient.1.source = f32[1024,512]{1,0:T(8,128)S(1)} custom-call(bf16[512,768]{1,0:T(8,128)(2,1)S(1)} %get-tuple-element.146.w_a, bf16[512,768]{1,0:T(8,128)(2,1)S(1)} %get-tuple-element.147.w_b, f32[1024,512]{1,0:T(8,128)S(1)} %get-tuple-element.148.dh1_ref, bf16[1,384,1024]{2,1,0:T(8,128)(2,1)S(1)} %get-tuple-element.145.refs_0_.trio_a, ...), custom_call_target="tpu_custom_call" | custom-call | flops 1 | bytes 1 | tf_op jit(solution)/shard_map/input_gradient/pallas_call | solution.py:602
  72.9 1.8 %collective-permute-start.12 = (bf16[64,1920]{1,0:T(8,128)(2,1)S(1)}, bf16[64,1920]{1,0:T(8,128)(2,1)S(1)}, u32[]{:S(2)}, u32[]{:S(2)}) collective-permute-start(bf16[64,1920]{1,0:T(8,128)(2,1)S(1)} %get-tuple-element.196), channel_id=1, source_target_pairs={{0,4},{4,0},{8,12},{12,8},{16,20},{20,16},{24,28},{28,24},{1,5},{5... | collective-permute-start | bytes 737288 | tf_op jit(solution)/shard_map/ppermute | solution.py:708
  74.6 2.4 %turn_back.3 = f32[1024,512]{1,0:T(8,128)} custom-call(s32[1]{0:T(128)} %get-tuple-element.108.start, f32[1024,512]{1,0:T(8,128)S(1)} %input_gradient.1.source), custom_call_target="tpu_custom_call" | custom-call | flops 1 | bytes 1 | tf_op jit(solution)/shard_map/turn_back/pallas_call | solution.py:230
  77.0 3.0 %collective-permute-done.13 = bf16[128,1280]{1,0:T(8,128)(2,1)S(1)} collective-permute-done((bf16[128,1280]{1,0:T(8,128)(2,1)S(1)}, bf16[128,1280]{1,0:T(8,128)(2,1)S(1)}, u32[]{:S(2)}, u32[]{:S(2)}) %collective-permute-start.13) | collective-permute-done | bytes 327712 | tf_op jit(solution)/shard_map/ppermute | solution.py:708
  83.5 2.2 %collective-permute-done.15 = bf16[64,1280]{1,0:T(8,128)(2,1)S(1)} collective-permute-done((bf16[64,1280]{1,0:T(8,128)(2,1)S(1)}, bf16[64,1280]{1,0:T(8,128)(2,1)S(1)}, u32[]{:S(2)}, u32[]{:S(2)}) %collective-permute-start.15) | collective-permute-done | bytes 163872 | tf_op jit(solution)/shard_map/ppermute | solution.py:708
  87.4 2.7 %collective-permute-start.16 = (bf16[16,1920]{1,0:T(8,128)(2,1)S(1)}, bf16[16,1920]{1,0:T(8,128)(2,1)S(1)}, u32[]{:S(2)}, u32[]{:S(2)}) collective-permute-start(bf16[16,1920]{1,0:T(8,128)(2,1)S(1)} %add_convert_fusion.13), channel_id=1, source_target_pairs={{0,16},{4,20},{8,24},{12,28},{16,0},{20,4},{24,8},{28,12},{1,17},{... | collective-permute-start | bytes 184328 | tf_op jit(solution)/shard_map/ppermute | solution.py:708
  90.7 2.5 %collective-permute-start.19 = (bf16[16,1280]{1,0:T(8,128)(2,1)S(1)}, bf16[16,1280]{1,0:T(8,128)(2,1)S(1)}, u32[]{:S(2)}, u32[]{:S(2)}) collective-permute-start(bf16[16,1280]{1,0:T(8,128)(2,1)S(1)} %get-tuple-element.204), channel_id=1, source_target_pairs={{0,16},{4,20},{8,24},{12,28},{16,0},{20,4},{24,8},{28,12},{1,17},{... | collective-permute-start | bytes 122888 | tf_op jit(solution)/shard_map/ppermute | solution.py:708
  95.6 2.9 %collective-permute-start.21 = (bf16[16,1152]{1,0:T(8,128)(2,1)S(1)}, bf16[16,1152]{1,0:T(8,128)(2,1)S(1)}, u32[]{:S(2)}, u32[]{:S(2)}) collective-permute-start(bf16[16,1152]{1,0:T(8,128)(2,1)S(1)} %add_convert_fusion.17), channel_id=1, source_target_pairs={{0,16},{4,20},{8,24},{12,28},{16,0},{20,4},{24,8},{28,12},{1,17},{... | collective-permute-start | bytes 110600 | tf_op jit(solution)/shard_map/ppermute | solution.py:708
  100.7 2.1 %collective-permute-start.22 = (bf16[32,1152]{1,0:T(8,128)(2,1)S(1)}, bf16[32,1152]{1,0:T(8,128)(2,1)S(1)}, u32[]{:S(2)}, u32[]{:S(2)}) collective-permute-start(bf16[32,1152]{1,0:T(8,128)(2,1)S(1)} %pad_maximum_fusion.3), channel_id=1, source_target_pairs={{0,8},{4,12},{8,0},{12,4},{16,24},{20,28},{24,16},{28,20},{1,9},{5... | collective-permute-start | bytes 221192 | tf_op jit(solution)/shard_map/ppermute | solution.py:708
  102.8 1.7 %collective-permute-done.20 = bf16[32,1920]{1,0:T(8,128)(2,1)S(1)} collective-permute-done((bf16[32,1920]{1,0:T(8,128)(2,1)S(1)}, bf16[32,1920]{1,0:T(8,128)(2,1)S(1)}, u32[]{:S(2)}, u32[]{:S(2)}) %collective-permute-start.20) | collective-permute-done | bytes 122912 | tf_op jit(solution)/shard_map/ppermute | solution.py:708
  111.5 3.2 %collective-permute-done.26 = f32[8,128]{1,0:T(8,128)S(1)} collective-permute-done((f32[8,128]{1,0:T(8,128)S(1)}, f32[8,128]{1,0:T(8,128)S(1)}, u32[]{:S(2)}, u32[]{:S(2)}) %collective-permute-start.26) | collective-permute-done | bytes 4128 | tf_op jit(solution)/shard_map/ppermute | solution.py:708
  114.9 4.2 %adam.1 = (f32[128,1536]{1,0:T(8,128)}, f32[128,512]{1,0:T(8,128)}, f32[128,512]{1,0:T(8,128)}, f32[128,512]{1,0:T(8,128)}, f32[9,128]{1,0:T(8,128)}, /*index=5*...) custom-call(s32[2]{0:T(128)S(1)} %pad_add_fusion.refs_0_.place, ...), custom_call_target="tpu_custom_call" | custom-call | tf_op jit(solution)/shard_map/adam/pallas_call | solution.py:695
  (108 shorter events, 28.0 us)
Async XLA Ops:
  2.6 8.7 %collective-permute-start.1 = (bf16[144,768]{1,0:T(8,128)(2,1)}, bf16[144,768]{1,0:T(8,128)(2,1)S(1)}, u32[]{:S(2)}, u32[]{:S(2)}) collective-permute-start(bf16[144,768]{1,0:T(8,128)(2,1)} %pack_first.1.refs_5_), channel_id=1, source_target_pairs={{0,2},{1,3},{2,0},{3,1},{4,6},{5,7},{6,4},{7,5},{8,10},{9,11},{10,... | collective-permute-start | bytes 663560 | tf_op jit(solution)/shard_map/ppermute | solution.py:708
  5.6 8.3 %collective-permute-start = (bf16[144,768]{1,0:T(8,128)(2,1)}, bf16[144,768]{1,0:T(8,128)(2,1)}, u32[]{:S(2)}, u32[]{:S(2)}) collective-permute-start(bf16[144,768]{1,0:T(8,128)(2,1)} %pack_first.1.refs_5_), channel_id=1, source_target_pairs={{0,1},{1,0},{2,3},{3,2},{4,5},{5,4},{6,7},{7,6},{8,9},{9,8},{10,11... | collective-permute-start | bytes 663560 | tf_op jit(solution)/shard_map/ppermute | solution.py:708
  11.3 10.5 %collective-permute-start.3 = (bf16[128,768]{1,0:T(8,128)(2,1)}, bf16[128,768]{1,0:T(8,128)(2,1)}, u32[]{:S(2)}, u32[]{:S(2)}) collective-permute-start(bf16[128,768]{1,0:T(8,128)(2,1)} %get-tuple-element.123.refs_5_), channel_id=1, source_target_pairs={{0,1},{1,0},{2,3},{3,2},{4,5},{5,4},{6,7},{7,6},{8,9},{9,8},{10,11... | collective-permute-start | bytes 589832 | tf_op jit(solution)/shard_map/ppermute | solution.py:708
  11.9 9.4 %collective-permute-start.4 = (bf16[128,768]{1,0:T(8,128)(2,1)}, bf16[128,768]{1,0:T(8,128)(2,1)S(1)}, u32[]{:S(2)}, u32[]{:S(2)}) collective-permute-start(bf16[128,768]{1,0:T(8,128)(2,1)} %get-tuple-element.123.refs_5_), channel_id=1, source_target_pairs={{0,2},{1,3},{2,0},{3,1},{4,6},{5,7},{6,4},{7,5},{8,10},{9,11},{10,... | collective-permute-start | bytes 589832 | tf_op jit(solution)/shard_map/ppermute | solution.py:708
  13.6 13.7 %collective-permute-start.6 = (bf16[128,1536]{1,0:T(8,128)(2,1)S(1)}, bf16[128,1536]{1,0:T(8,128)(2,1)S(1)}, u32[]{:S(2)}, u32[]{:S(2)}) collective-permute-start(bf16[128,1536]{1,0:T(8,128)(2,1)S(1)} %get-tuple-element.126.refs_6_), channel_id=1, source_target_pairs={{0,2},{1,3},{2,0},{3,1},{4,6},{5,7},{6,4},{7,5},{8,10},{9,11},{10,... | collective-permute-start | bytes 1179656 | tf_op jit(solution)/shard_map/ppermute | solution.py:708
  21.2 6.1 %collective-permute-start.5 = (bf16[128,768]{1,0:T(8,128)(2,1)S(1)}, bf16[128,768]{1,0:T(8,128)(2,1)S(1)}, u32[]{:S(2)}, u32[]{:S(2)}) collective-permute-start(bf16[128,768]{1,0:T(8,128)(2,1)S(1)} %collective-permute-done.4.refs_7_), channel_id=1, source_target_pairs={{0,1},{1,0},{2,3},{3,2},{4,5},{5,4},{6,7},{7,6},{8,9},{9,8},{10,11... | collective-permute-start | bytes 589832 | tf_op jit(solution)/shard_map/ppermute | solution.py:708
  21.3 13.3 %collective-permute-start.7 = (bf16[128,1536]{1,0:T(8,128)(2,1)S(1)}, bf16[128,1536]{1,0:T(8,128)(2,1)S(1)}, u32[]{:S(2)}, u32[]{:S(2)}) collective-permute-start(bf16[128,1536]{1,0:T(8,128)(2,1)S(1)} %get-tuple-element.126.refs_6_), channel_id=1, source_target_pairs={{0,1},{1,0},{2,3},{3,2},{4,5},{5,4},{6,7},{7,6},{8,9},{9,8},{10,11... | collective-permute-start | bytes 1179656 | tf_op jit(solution)/shard_map/ppermute | solution.py:708
  27.3 7.3 %collective-permute-start.8 = (bf16[128,1536]{1,0:T(8,128)(2,1)S(1)}, bf16[128,1536]{1,0:T(8,128)(2,1)S(1)}, u32[]{:S(2)}, u32[]{:S(2)}) collective-permute-start(bf16[128,1536]{1,0:T(8,128)(2,1)S(1)} %collective-permute-done.6.refs_8_), channel_id=1, source_target_pairs={{0,1},{1,0},{2,3},{3,2},{4,5},{5,4},{6,7},{7,6},{8,9},{9,8},{10,11... | collective-permute-start | bytes 1179656 | tf_op jit(solution)/shard_map/ppermute | solution.py:708
  53.8 14.2 %collective-permute-start.11 = (bf16[128,1920]{1,0:T(8,128)(2,1)S(1)}, bf16[128,1920]{1,0:T(8,128)(2,1)S(1)}, u32[]{:S(2)}, u32[]{:S(2)}) collective-permute-start(bf16[128,1920]{1,0:T(8,128)(2,1)S(1)} %get-tuple-element.192.refs_12_), channel_id=1, source_target_pairs={{0,2},{1,3},{2,0},{3,1},{4,6},{5,7},{6,4},{7,5},{8,10},{9,11},{10,... | collective-permute-start | bytes 1474568 | tf_op jit(solution)/shard_map/ppermute | solution.py:708
  70.2 9.8 %collective-permute-start.13 = (bf16[128,1280]{1,0:T(8,128)(2,1)S(1)}, bf16[128,1280]{1,0:T(8,128)(2,1)S(1)}, u32[]{:S(2)}, u32[]{:S(2)}) collective-permute-start(bf16[128,1280]{1,0:T(8,128)(2,1)S(1)} %get-tuple-element.194.refs_0_), channel_id=1, source_target_pairs={{0,2},{1,3},{2,0},{3,1},{4,6},{5,7},{6,4},{7,5},{8,10},{9,11},{10,... | collective-permute-start | bytes 983048 | tf_op jit(solution)/shard_map/ppermute | solution.py:708
  72.9 9.0 %collective-permute-start.12 = (bf16[64,1920]{1,0:T(8,128)(2,1)S(1)}, bf16[64,1920]{1,0:T(8,128)(2,1)S(1)}, u32[]{:S(2)}, u32[]{:S(2)}) collective-permute-start(bf16[64,1920]{1,0:T(8,128)(2,1)S(1)} %get-tuple-element.196), channel_id=1, source_target_pairs={{0,4},{4,0},{8,12},{12,8},{16,20},{20,16},{24,28},{28,24},{1,5},{5... | collective-permute-start | bytes 737288 | tf_op jit(solution)/shard_map/ppermute | solution.py:708
  80.2 5.5 %collective-permute-start.15 = (bf16[64,1280]{1,0:T(8,128)(2,1)S(1)}, bf16[64,1280]{1,0:T(8,128)(2,1)S(1)}, u32[]{:S(2)}, u32[]{:S(2)}) collective-permute-start(bf16[64,1280]{1,0:T(8,128)(2,1)S(1)} %get-tuple-element.198), channel_id=1, source_target_pairs={{0,4},{4,0},{8,12},{12,8},{16,20},{20,16},{24,28},{28,24},{1,5},{5... | collective-permute-start | bytes 491528 | tf_op jit(solution)/shard_map/ppermute | solution.py:708
  81.9 5.5 %collective-permute-start.14 = (bf16[32,1920]{1,0:T(8,128)(2,1)S(1)}, bf16[32,1920]{1,0:T(8,128)(2,1)S(1)}, u32[]{:S(2)}, u32[]{:S(2)}) collective-permute-start(bf16[32,1920]{1,0:T(8,128)(2,1)S(1)} %get-tuple-element.199), channel_id=1, source_target_pairs={{0,8},{4,12},{8,0},{12,4},{16,24},{20,28},{24,16},{28,20},{1,9},{5... | collective-permute-start | bytes 368648 | tf_op jit(solution)/shard_map/ppermute | solution.py:708
  85.8 4.9 %collective-permute-start.17 = (bf16[32,1280]{1,0:T(8,128)(2,1)S(1)}, bf16[32,1280]{1,0:T(8,128)(2,1)S(1)}, u32[]{:S(2)}, u32[]{:S(2)}) collective-permute-start(bf16[32,1280]{1,0:T(8,128)(2,1)S(1)} %get-tuple-element.202), channel_id=1, source_target_pairs={{0,8},{4,12},{8,0},{12,4},{16,24},{20,28},{24,16},{28,20},{1,9},{5... | collective-permute-start | bytes 245768 | tf_op jit(solution)/shard_map/ppermute | solution.py:708
  87.4 6.3 %collective-permute-start.16 = (bf16[16,1920]{1,0:T(8,128)(2,1)S(1)}, bf16[16,1920]{1,0:T(8,128)(2,1)S(1)}, u32[]{:S(2)}, u32[]{:S(2)}) collective-permute-start(bf16[16,1920]{1,0:T(8,128)(2,1)S(1)} %add_convert_fusion.13), channel_id=1, source_target_pairs={{0,16},{4,20},{8,24},{12,28},{16,0},{20,4},{24,8},{28,12},{1,17},{... | collective-permute-start | bytes 184328 | tf_op jit(solution)/shard_map/ppermute | solution.py:708
  90.7 5.0 %collective-permute-start.19 = (bf16[16,1280]{1,0:T(8,128)(2,1)S(1)}, bf16[16,1280]{1,0:T(8,128)(2,1)S(1)}, u32[]{:S(2)}, u32[]{:S(2)}) collective-permute-start(bf16[16,1280]{1,0:T(8,128)(2,1)S(1)} %get-tuple-element.204), channel_id=1, source_target_pairs={{0,16},{4,20},{8,24},{12,28},{16,0},{20,4},{24,8},{28,12},{1,17},{... | collective-permute-start | bytes 122888 | tf_op jit(solution)/shard_map/ppermute | solution.py:708
  93.8 5.8 %collective-permute-start.18 = (bf16[16,1920]{1,0:T(8,128)(2,1)S(1)}, bf16[16,1920]{1,0:T(8,128)(2,1)S(1)}, u32[]{:S(2)}, u32[]{:S(2)}) collective-permute-start(bf16[16,1920]{1,0:T(8,128)(2,1)S(1)} %add_convert_fusion.12), channel_id=1, source_target_pairs={{0,16},{4,20},{8,24},{12,28},{16,0},{20,4},{24,8},{28,12},{1,17},{... | collective-permute-start | bytes 184328 | tf_op jit(solution)/shard_map/ppermute | solution.py:708
  95.6 5.0 %collective-permute-start.21 = (bf16[16,1152]{1,0:T(8,128)(2,1)S(1)}, bf16[16,1152]{1,0:T(8,128)(2,1)S(1)}, u32[]{:S(2)}, u32[]{:S(2)}) collective-permute-start(bf16[16,1152]{1,0:T(8,128)(2,1)S(1)} %add_convert_fusion.17), channel_id=1, source_target_pairs={{0,16},{4,20},{8,24},{12,28},{16,0},{20,4},{24,8},{28,12},{1,17},{... | collective-permute-start | bytes 110600 | tf_op jit(solution)/shard_map/ppermute | solution.py:708
  99.6 4.9 %collective-permute-start.20 = (bf16[32,1920]{1,0:T(8,128)(2,1)S(1)}, bf16[32,1920]{1,0:T(8,128)(2,1)S(1)}, u32[]{:S(2)}, u32[]{:S(2)}) collective-permute-start(bf16[32,1920]{1,0:T(8,128)(2,1)S(1)} %pad_maximum_fusion.2), channel_id=1, source_target_pairs={{0,8},{4,12},{8,0},{12,4},{16,24},{20,28},{24,16},{28,20},{1,9},{5... | collective-permute-start | bytes 368648 | tf_op jit(solution)/shard_map/ppermute | solution.py:708
  100.7 5.5 %collective-permute-start.22 = (bf16[32,1152]{1,0:T(8,128)(2,1)S(1)}, bf16[32,1152]{1,0:T(8,128)(2,1)S(1)}, u32[]{:S(2)}, u32[]{:S(2)}) collective-permute-start(bf16[32,1152]{1,0:T(8,128)(2,1)S(1)} %pad_maximum_fusion.3), channel_id=1, source_target_pairs={{0,8},{4,12},{8,0},{12,4},{16,24},{20,28},{24,16},{28,20},{1,9},{5... | collective-permute-start | bytes 221192 | tf_op jit(solution)/shard_map/ppermute | solution.py:708
  104.6 10.2 %collective-permute-start.27 = (bf16[64,1920]{1,0:T(8,128)(2,1)S(1)}, bf16[64,1920]{1,0:T(8,128)(2,1)S(1)}, u32[]{:S(2)}, u32[]{:S(2)}) collective-permute-start(bf16[64,1920]{1,0:T(8,128)(2,1)S(1)} %pad_maximum_fusion.early.refs_0_), channel_id=1, source_target_pairs={{0,4},{4,0},{8,12},{12,8},{16,20},{20,16},{24,28},{28,24},{1,5},{5... | collective-permute-start | bytes 737288 | tf_op jit(solution)/shard_map/ppermute | solution.py:708
  107.1 3.7 %collective-permute-start.24 = (f32[8,128]{1,0:T(8,128)S(1)}, f32[8,128]{1,0:T(8,128)S(1)}, u32[]{:S(2)}, u32[]{:S(2)}) collective-permute-start(f32[8,128]{1,0:T(8,128)S(1)} %half_squares.1), channel_id=1, source_target_pairs={{0,2},{1,3},{2,0},{3,1},{4,6},{5,7},{6,4},{7,5},{8,10},{9,11},{10,... | collective-permute-start | bytes 12296 | tf_op jit(solution)/shard_map/ppermute | solution.py:708
  108.9 5.9 %collective-permute-start.28 = (bf16[64,1152]{1,0:T(8,128)(2,1)S(1)}, bf16[64,1152]{1,0:T(8,128)(2,1)S(1)}, u32[]{:S(2)}, u32[]{:S(2)}) collective-permute-start(bf16[64,1152]{1,0:T(8,128)(2,1)S(1)} %pad_maximum_fusion.1.late.refs_2_), channel_id=1, source_target_pairs={{0,4},{4,0},{8,12},{12,8},{16,20},{20,16},{24,28},{28,24},{1,5},{5... | collective-permute-start | bytes 442376 | tf_op jit(solution)/shard_map/ppermute | solution.py:708
  110.8 4.0 %collective-permute-start.26 = (f32[8,128]{1,0:T(8,128)S(1)}, f32[8,128]{1,0:T(8,128)S(1)}, u32[]{:S(2)}, u32[]{:S(2)}) collective-permute-start(f32[8,128]{1,0:T(8,128)S(1)} %add_add_fusion), channel_id=1, source_target_pairs={{0,4},{4,0},{8,12},{12,8},{16,20},{20,16},{24,28},{28,24},{1,5},{5... | collective-permute-start | bytes 12296 | tf_op jit(solution)/shard_map/ppermute | solution.py:708
  (25 other events, 448.3 us)

commit v4 on v3

--- a/solution.py
+++ b/solution.py
@@ -17,8 +17,8 @@
 TOK_DEV = 1024
 QT = 256
 HALF = TOK_DEV // 2
-TILES = 1
-MT = 512
+TILES = 2
+MT = 256
 STEP = 10
 NORM_EPS = 1e-05
 ADAM_EPS = 1e-08
@@ -31,7 +31,7 @@
 HW = GROUP * TRIO
 FIRST = 1
 LATE = (PAIRS - FIRST) * TRIO
-FORWARD_MIB, MIDDLE_MIB, BACKWARD_MIB = 12, 20, 22
+FORWARD_MIB, MIDDLE_MIB, BACKWARD_MIB = 12, 13, 20
 
 NN = (((1,), (0,)), ((), ()))
 NT = (((1,), (1,)), ((), ()))
@@ -305,9 +305,17 @@
         vrow_out[local] = (rows[:, PAIR:] + b_v).astype(BF)
         qt_out[here, :] = q_t
         kt_out[here, :] = trio[PAIR : 2 * PAIR].astype(BF)
-        for mine in halves:
-            chains.append((local, mine, v_t, dot(k_row[mine], both_heads(q_t[:, mine]), NN)))
-    for local, mine, v_t, s in chains:
+        chains += [(local, mine, q_t, v_t, k_row) for mine in halves]
+
+    def scores(chain):
+        local, mine, q_t, v_t, k_row = chain
+        return dot(k_row[mine], both_heads(q_t[:, mine]), NN)
+
+    ahead = scores(chains[0])
+    for number, (local, mine, q_t, v_t, k_row) in enumerate(chains):
+        s = ahead
+        if number + 1 < len(chains):
+            ahead = scores(chains[number + 1])
         mask = bias[mine, :]
         s = s + jnp.concatenate([mask, mask], 1)
         top = jnp.max(s, 0, keepdims=True)
@@ -336,7 +344,7 @@
         ],
         scratch_shapes=[pltpu.VMEM((TOK_DEV, HALF), F32)],
         compiler_params=params(FORWARD_MIB),
-        cost_estimate=cost(6e9, 8e6, 2**21),
+        cost_estimate=cost(1, 1),
         name="forward_attention",
     )(place, tokens, tokens_t, cells, vec, *pieces)
 
@@ -395,15 +403,12 @@
     return jnp.where(value >= 0.0, 1.0 - tail, tail), value * density * (1.0 / math.sqrt(2.0 * math.pi))
 
 
-def middle_kernel(order, n_pieces, n_shards, stages, *refs):
-    n_g = 2 if stages else 1
+def middle_kernel(order, n_pieces, *refs):
     place, tokens, cot_ref, att_a, att_b, vec_ref = refs[:6]
     pieces = refs[6 : 6 + n_pieces]
     mixed_out, dh1_out, datt_out, vec_out = refs[6 + n_pieces : 10 + n_pieces]
-    g_outs = refs[10 + n_pieces : 10 + n_pieces + n_g]
-    w_full, att_all, first_all, hidden_all, branch_all, pre_all, down_all, dw, sums = refs[
-        10 + n_pieces + n_g :
-    ]
+    first_all, hidden_all, branch_all, pre_all, down_all = refs[10 + n_pieces : 15 + n_pieces]
+    w_full, sums = refs[15 + n_pieces :]
     step = pl.program_id(0)
 
     @pl.when(step == 0)
@@ -419,7 +424,6 @@
     def tile(number):
         at = pl.ds(pl.multiple_of(step * (TILES * MT) + number * MT, MT), MT)
         att_t = jnp.concatenate([att_a[:, at], att_b[:, at]], 0)
-        att_all[:, at] = att_t
         branch = dot(att_t, w_out, TN)
         yield
         normal_1, inverse_1 = normalize(tokens[at, :].astype(F32) + (branch + vec(2)))
@@ -470,43 +474,33 @@
         sums[3:4, :] = dot(ones, pre_all[...], NN)[:1]
         sums[4:5, :] = dot(ones, down_all[...], NN)[:1]
         vec_out[...] = sums[...]
-        dw[0] = dot(att_all[...], branch_all[...], NN)
-        dw[1] = dot(first_all[...], pre_all[...], TN)
-        dw[2] = dot(hidden_all[...], down_all[...], TN)
-        for number in range(3):
-            store_rows(
-                g_outs, place, n_shards, stages, dw.at[number], slice(number * D, (number + 1) * D)
-            )
-
-
-def middle(place, tokens, cot, atts, vec, pieces, order, stages):
+
+
+def middle(place, tokens, cot, atts, vec, pieces, order):
     height = TILES * MT
-    g_shapes = [(D // 2, 3 * D)] * 2 if stages else [(D, 3 * D)]
     return pl.pallas_call(
-        functools.partial(middle_kernel, order, len(pieces), len(order), stages),
+        functools.partial(middle_kernel, order, len(pieces)),
         grid=(TOK_DEV // height,),
         in_specs=[SMEM] + [VM] * (5 + len(pieces)),
-        out_specs=[VM] * (4 + len(g_shapes)),
+        out_specs=[VM] * 9,
         out_shape=[
             sds((TOK_DEV, D), BF),
             sds((TOK_DEV, D), F32),
             sds((D, TOK_DEV), BF),
             sds((16, D), F32),
         ]
-        + [sds(shape, BF) for shape in g_shapes],
-        scratch_shapes=[pltpu.VMEM((D, 3 * D), BF), pltpu.VMEM((D, TOK_DEV), BF)]
-        + [pltpu.VMEM((TOK_DEV, D), BF)] * 5
-        + [pltpu.VMEM((3, D, D), F32), pltpu.VMEM((16, D), F32)],
+        + [sds((TOK_DEV, D), BF)] * 5,
+        scratch_shapes=[pltpu.VMEM((D, 3 * D), BF), pltpu.VMEM((16, D), F32)],
         compiler_params=params(MIDDLE_MIB),
         cost_estimate=cost(1e10, 1.2e7, 2**20),
         name="middle",
     )(place, tokens, cot, *atts, vec, *pieces)
 
 
-def backward_kernel(n_shards, stages, plan, n_sets, n_before, last, place, cells_ref, tokens_t, vec_ref,
+def backward_kernel(n_shards, stages, plan, n_sets, n_inner, last, place, cells_ref, tokens_t, vec_ref,
                     datt_ref, *refs):
     sets = [refs[6 * number : 6 * (number + 1)] for number in range(n_sets)]
-    before = refs[6 * n_sets : 6 * n_sets + n_before]
+    inner = refs[6 * n_sets : 6 * n_sets + n_inner]
     bias, dw = refs[-2:]
     n_g = 2 if stages else 1
     d_out, vec = refs[-4 - n_g : -2 - n_g]
@@ -514,46 +508,63 @@
     make_bias(cells_ref, bias)
     vec[...] = vec_ref[...]
     halves = [slice(0, HALF), slice(HALF, TOK_DEV)]
-    chains = []
-    for place_out, (number, local, pair) in enumerate(plan):
+    chains = [(place_out, *entry, mine) for place_out, entry in enumerate(plan) for mine in halves]
+
+    def scores(chain):
+        _, number, local, pair, mine = chain
         att_ref, lse_ref, krow_ref, vrow_ref, qt_ref, kt_ref = sets[number]
         here = slice(local * PAIR, (local + 1) * PAIR)
-        q_t, k_t = qt_ref[here, :], kt_ref[here, :]
-        d_t = datt_ref[pair * PAIR : (pair + 1) * PAIR, :]
-        k_row, v_row = krow_ref[local], vrow_ref[local]
-        product = d_t.astype(F32) * att_ref[here, :].astype(F32)
-        for mine in halves:
-            s = dot(k_row[mine], both_heads(q_t[:, mine]), NN)
-            d_prob = dot(v_row[mine], both_heads(d_t[:, mine]), NN)
-            lse = jnp.concatenate([lse_ref[local, 0:1, mine], lse_ref[local, 1:2, mine]], 1)
-            chains.append((place_out, mine, q_t, k_t, d_t, product, s, d_prob, lse))
-    for place_out, mine, q_t, k_t, d_t, product, s, d_prob, lse in chains:
+        q_t, d_t = qt_ref[here, mine], datt_ref[pair * PAIR : (pair + 1) * PAIR, mine]
+        s = dot(krow_ref[local, mine, :], both_heads(q_t), NN)
+        return q_t, d_t, s, dot(vrow_ref[local, mine, :], both_heads(d_t), NN)
+
+    first = 0
+    if inner:
+        first = 3 * D
+        first_all, hidden_all, branch_all, pre_all, down_all = inner
+        attended = jnp.concatenate([sets[0][0][...], sets[1][0][...]], 0)
+        products = [
+            dot(attended, branch_all[...], NN),
+            dot(first_all[...], pre_all[...], TN),
+            dot(hidden_all[...], down_all[...], TN),
+        ]
+        for number, product in enumerate(products):
+            dw[number % 2] = product
+            cols = slice(number * D, (number + 1) * D)
+            store_rows(g_outs, place, n_shards, stages, dw.at[number % 2], cols)
+    ahead = scores(chains[0])
+    for step, (place_out, number, local, pair, mine) in enumerate(chains):
+        q_t, d_t, s, d_prob = ahead
+        if step + 1 < len(chains):
+            ahead = scores(chains[step + 1])
+        att_ref, lse_ref, krow_ref, vrow_ref, qt_ref, kt_ref = sets[number]
         mask = bias[mine, :]
-        delta = jnp.concatenate(
-            [column_sum(product[:HEAD_DIM, mine]), column_sum(product[HEAD_DIM:, mine])], 1
-        )
+        lse = jnp.concatenate([lse_ref[local, 0:1, mine], lse_ref[local, 1:2, mine]], 1)
+        here = slice(local * PAIR, (local + 1) * PAIR)
+        product = d_t.astype(F32) * att_ref[here, mine].astype(F32)
+        delta = jnp.concatenate([column_sum(product[:HEAD_DIM]), column_sum(product[HEAD_DIM:])], 1)
         prob = jnp.exp(s + jnp.concatenate([mask, mask], 1) - lse)
         d_s = (prob * (d_prob - delta)).astype(BF)
         prob_low = prob.astype(BF)
         for h in range(2):
             cols = slice(h * HALF, (h + 1) * HALF)
             head = slice(h * HEAD_DIM, (h + 1) * HEAD_DIM)
-            d_q = dot(k_t[head, mine], d_s[:, cols], NN) * (HEAD_DIM**-0.5)
-            d_k = dot(q_t[head, mine], d_s[:, cols], NT)
-            d_v = dot(d_t[head, mine], prob_low[:, cols], NT)
+            k_t = kt_ref[local * PAIR + h * HEAD_DIM : local * PAIR + (h + 1) * HEAD_DIM, mine]
+            d_q = dot(k_t, d_s[:, cols], NN) * (HEAD_DIM**-0.5)
+            d_k = dot(q_t[head], d_s[:, cols], NT)
+            d_v = dot(d_t[head], prob_low[:, cols], NT)
             for t, value in enumerate((d_q, d_k, d_v)):
                 at = t * PAIR + h * HEAD_DIM
                 d_out[place_out, at : at + HEAD_DIM, mine] = value.astype(BF)
-    ones = jnp.ones((16, TOK_DEV), BF)
-    for out, ref in zip(g_outs, before):
-        out[:, : ref.shape[1]] = ref[...]
-    first = before[0].shape[1] if before else 0
-    for place_out, (number, local, pair) in enumerate(plan):
+        if mine.start == 0:
+            continue
         trio = d_out[place_out]
-        dw[place_out] = dot(tokens_t[...], trio, NT)
+        dw[place_out % 2, :, :TRIO] = dot(tokens_t[...], trio, NT)
         at = first + place_out * TRIO
-        store_rows(g_outs, place, n_shards, stages, dw.at[place_out], slice(at, at + TRIO))
-        total = dot(ones, trio, NT)
+        store_rows(
+            g_outs, place, n_shards, stages, dw.at[place_out % 2, :, :TRIO], slice(at, at + TRIO)
+        )
+        total = dot(jnp.ones((16, TOK_DEV), BF), trio, NT)
         lanes = slice(pair * PAIR, (pair + 1) * PAIR)
         vec[0:1, lanes] = total[:1, :PAIR]
         vec[1:2, lanes] = total[:1, 2 * PAIR :]
@@ -567,23 +578,23 @@
             ].astype(BF)
 
 
-def backward_attention(plan, last, place, cells, tokens_t, vec_sums, sets, d_t, before, n_shards, stages, later):
-    width = len(plan) * TRIO + (before[0].shape[1] if before else 0)
+def backward_attention(plan, last, place, cells, tokens_t, vec_sums, sets, d_t, inner, n_shards, stages, later):
+    width = len(plan) * TRIO + (3 * D if inner else 0)
     if stages:
         shapes = [sds((D // 2, width + (PAIR if last else 0)), BF)] * 2
     else:
         shapes = [sds((D, width), BF)]
     flat = [value for saved in sets for value in saved]
     return pl.pallas_call(
-        functools.partial(backward_kernel, n_shards, stages, plan, len(sets), len(before), last),
-        in_specs=[SMEM] + [VM] * (4 + len(flat) + len(before)) + [ANY] * len(later),
+        functools.partial(backward_kernel, n_shards, stages, plan, len(sets), len(inner), last),
+        in_specs=[SMEM] + [VM] * (4 + len(flat) + len(inner)) + [ANY] * len(later),
         out_specs=[VM] * (2 + len(shapes)),
         out_shape=[sds((len(plan), TRIO, TOK_DEV), BF), sds((16, D), F32)] + shapes,
-        scratch_shapes=[pltpu.VMEM((TOK_DEV, HALF), F32), pltpu.VMEM((len(plan), D, TRIO), F32)],
+        scratch_shapes=[pltpu.VMEM((TOK_DEV, HALF), F32), pltpu.VMEM((2, D, D), F32)],
         compiler_params=params(BACKWARD_MIB),
         cost_estimate=cost(5e9 * len(plan), 8e6, 2**21),
         name="backward_attention",
-    )(place, cells, tokens_t, vec_sums, d_t, *flat, *before, *later)
+    )(place, cells, tokens_t, vec_sums, d_t, *flat, *inner, *later)
 
 
 def input_grad_kernel(w_a, w_b, dh1_ref, trio_a, trio_b, *refs):
@@ -809,22 +820,21 @@
     )
     if quick:
         y_b, c_b = after(y_b, saved_a), after(c_b, saved_a)
-        y_rest = after(y_rest, y_b)
-        d_rest = swap(y_rest, "narrow", 1)
-        pieces_b = [low_b, c_b, y_b, after(swap(y_b, "narrow", 1), y_rest)]
+        pieces_b = [low_b, c_b, y_b, swap(y_b, "narrow", 1)]
     *saved_b, w_b, vec_full, tokens = forward_attention(
         GROUP, place, tokens, tokens_t, cells, vec_full, pieces_b, order
     )
     cotangent = turn_cotangent(start, cotangent, [saved_b[0]])
     if quick:
-        pieces_rest = [low_rest, *after((c_rest, y_rest, d_rest), cotangent)]
-    mixed, d_h1, d_t, vec_sums, *g_rest = middle(
-        place, tokens, cotangent, (saved_a[0], saved_b[0]), vec_full, pieces_rest, order, stages
+        y_rest, c_rest = after(y_rest, (saved_b, cotangent)), after(c_rest, saved_b)
+        pieces_rest = [low_rest, c_rest, y_rest, swap(y_rest, "narrow", 1)]
+    mixed, d_h1, d_t, vec_sums, *inner = middle(
+        place, tokens, cotangent, (saved_a[0], saved_b[0]), vec_full, pieces_rest, order
     )
     sets = [saved_a, saved_b]
     plan = [(pair // GROUP, pair % GROUP, pair) for pair in range(PAIRS)]
     trio_a, vec_sums, *early = backward_attention(
-        plan[:FIRST], False, place, cells, tokens_t, vec_sums, sets, d_t, g_rest, narrow, stages, []
+        plan[:FIRST], False, place, cells, tokens_t, vec_sums, sets, d_t, inner, narrow, stages, []
     )
     later = []
     if quick:

time: 120 us -> 117 us (0.975)
  waiting for transfers between devices: 22.2 us -> 19.2 us
    ppermute x29, waiting for transfers between devices: 22.2 us -> 19.2 us  [swap(): return lax.ppermute(value, axis, [(i, i ^ mask) for i in range(size)])]
    pallas_call x2, Pallas kernels: 17 us -> 18.8 us  [backward_attention(): pl.pallas_call(functools.partial(backward_kernel, n_shards, stages, plan,...]
    pallas_call x1, Pallas kernels: 11.5 us -> 10 us  [middle(): pl.pallas_call(functools.partial(middle_kernel, order, len(pieces)), grid...]
  transfers between devices with their start and end apart: 29 -> 29, of which waited for: 14 -> 15; matrix products, arithmetic and copies ran while one was open for 1% -> 1% of each run, Pallas kernels for 30% -> 30%
where the time goes in v4:
time: 117 us; the launch traced here: 116 us
  Pallas kernels  57.6 us (49%)
  starting transfers between devices  33.1 us (28%)
  waiting for transfers between devices  19.2 us (16%)
  local copies, waits for them, and re-layouts  3.49 us (3%)
  other arithmetic  1.68 us (1%)
  between operations  1.26 us (1%)
    ppermute x29, starting transfers between devices, swap(): return lax.ppermute(value, axis, [(i, i ^ mask) for i in range(size)])  33.1 us
    ppermute x29, waiting for transfers between devices, swap(): return lax.ppermute(value, axis, [(i, i ^ mask) for i in range(size)])  19.2 us
    pallas_call x2, Pallas kernels, backward_attention(): pl.pallas_call(functools.partial(backward_kernel, n_shards, stages, plan,...  18.8 us
    pallas_call x2, Pallas kernels, forward_attention(): pl.pallas_call(functools.partial(forward_kernel, order, len(pieces), base...  11.7 us
    pallas_call x1, Pallas kernels, middle(): pl.pallas_call(functools.partial(middle_kernel, order, len(pieces)), grid...  10 us
    pallas_call x2, Pallas kernels, turn_back(): pl.pallas_call(turn_back_kernel, in_specs=[SMEM, VM] + [ANY] * len(later)...  4.73 us
    pallas_call x1, Pallas kernels, adam_step(): pl.pallas_call(functools.partial(adam_kernel, quick, limit), grid=(steps,...  4.19 us
    unnamed x40, local copies, waits for them, and re-layouts  3.49 us
  transfers between devices with their start and end apart: 29, of which 15 were waited for; matrix products, arithmetic and copies ran while one was open for 1% of the time, Pallas kernels for 30%

profile of v4, /device:TPU:0, one launch (start us, length us, event | category | flops | bytes accessed | tf_op | source)
XLA Modules:
  0.0 116.3 jit_solution(2373659321077968027)
XLA Ops:
  0.7 1.9 %pack_first.1.refs_5_ = bf16[144,768]{1,0:T(8,128)(2,1)} custom-call(f32[128,1536]{1,0:T(8,128)} %refs_5_.1, f32[9,128]{1,0:T(8,128)} %refs_9_.1), custom_call_target="tpu_custom_call" | custom-call | tf_op jit(solution)/shard_map/pack_first/pallas_call | solution.py:104
  2.6 3.0 %collective-permute-start.1 = (bf16[144,768]{1,0:T(8,128)(2,1)}, bf16[144,768]{1,0:T(8,128)(2,1)S(1)}, u32[]{:S(2)}, u32[]{:S(2)}) collective-permute-start(bf16[144,768]{1,0:T(8,128)(2,1)} %pack_first.1.refs_5_), channel_id=1, source_target_pairs={{0,2},{1,3},{2,0},{3,1},{4,6},{5,7},{6,4},{7,5},{8,10},{9,11},{10,... | collective-permute-start | bytes 663560 | tf_op jit(solution)/shard_map/ppermute | solution.py:719
  11.3 1.7 %collective-permute-start.4 = (bf16[128,768]{1,0:T(8,128)(2,1)}, bf16[128,768]{1,0:T(8,128)(2,1)}, u32[]{:S(2)}, u32[]{:S(2)}) collective-permute-start(bf16[128,768]{1,0:T(8,128)(2,1)} %get-tuple-element.123.refs_5_), channel_id=1, source_target_pairs={{0,2},{1,3},{2,0},{3,1},{4,6},{5,7},{6,4},{7,5},{8,10},{9,11},{10,... | collective-permute-start | bytes 589832 | tf_op jit(solution)/shard_map/ppermute | solution.py:719
  14.6 5.6 %forward_attention.2 = (bf16[256,1024]{1,0:T(8,128)(2,1)S(1)}, f32[2,8,1024]{2,1,0:T(8,128)S(1)}, bf16[2,1024,128]{2,1,0:T(8,128)(2,1)S(1)}, bf16[2,1024,128]{2,...) custom-call(s32[2]{0:T(128)S(1)} %pad_add_fusion.refs_0_.place, ...), custom_call_target="tpu_custom_call" | custom-call | flops 1 | bytes 1 | tf_op jit(solution)/shard_map/forward_attention/pallas_call | solution.py:337
  22.1 6.2 %forward_attention.3 = (bf16[256,1024]{1,0:T(8,128)(2,1)S(1)}, f32[2,8,1024]{2,1,0:T(8,128)S(1)}, bf16[2,1024,128]{2,1,0:T(8,128)(2,1)S(1)}, bf16[2,1024,128]{2,...) custom-call(s32[2]{0:T(128)S(1)} %pad_add_fusion.refs_0_.place, ...), custom_call_target="tpu_custom_call" | custom-call | flops 1 | bytes 1 | tf_op jit(solution)/shard_map/forward_attention/pallas_call | solution.py:337
  31.3 10.0 %middle.1 = (bf16[1024,512]{1,0:T(8,128)(2,1)S(1)}, f32[1024,512]{1,0:T(8,128)S(1)}, bf16[512,1024]{1,0:T(8,128)(2,1)S(1)}, f32[16,512]{1,0:T(8,128)S(1)}, bf16[...) custom-call(s32[2]{0:T(128)S(1)} %pad_add_fusion.refs_0_.place, ...), custom_call_target="tpu_custom_call" | custom-call | flops 10000000000 | bytes 12000000 | tf_op jit(solution)/shard_map/middle/pallas_call | solution.py:481
  41.4 6.3 %backward_attention.2 = (bf16[1,384,1024]{2,1,0:T(8,128)(2,1)S(1)}, f32[16,512]{1,0:T(8,128)S(1)}, bf16[256,1920]{1,0:T(8,128)(2,1)S(1)}, bf16[256,1920]{1,0:T(8,128)(2,1)S(1)}) custom-call(s32[2]{0:T(128)S(1)} %pad_add_fusion.refs_0_.place, s32[8,1024]{1,0:T(8,128)S(1)} %get-tuple-element.111.refs_0_.refs_3_.cells_ref, ...), custom_call_target="tpu_custom_call" | custom-call | flops 5000000000 | bytes 8000000 | tf_op jit(solution)/shard_map/backward_attention/pallas_call | solution.py:588
  48.1 2.3 %turn_back.2 = bf16[1024,512]{1,0:T(8,128)(2,1)} custom-call(s32[1]{0:T(128)} %get-tuple-element.108.start, bf16[1024,512]{1,0:T(8,128)(2,1)S(1)} %get-tuple-element.137.source, bf16[1,384,1024]{2,1,0:T(8,128)(2,1)S(1)} %get-tuple-element.145.refs_0_.trio_a), custom_call_target="tpu_custom_call" | custom-call | flops 1 | bytes 1 | tf_op jit(solution)/shard_map/turn_back/pallas_call | solution.py:230
  50.7 1.8 %collective-permute-start.11 = (bf16[128,1920]{1,0:T(8,128)(2,1)S(1)}, bf16[128,1920]{1,0:T(8,128)(2,1)S(1)}, u32[]{:S(2)}, u32[]{:S(2)}) collective-permute-start(bf16[128,1920]{1,0:T(8,128)(2,1)S(1)} %get-tuple-element.192.refs_12_), channel_id=1, source_target_pairs={{0,2},{1,3},{2,0},{3,1},{4,6},{5,7},{6,4},{7,5},{8,10},{9,11},{10,... | collective-permute-start | bytes 1474568 | tf_op jit(solution)/shard_map/ppermute | solution.py:719
  52.5 12.5 %backward_attention.3 = (bf16[3,384,1024]{2,1,0:T(8,128)(2,1)S(1)}, f32[16,512]{1,0:T(8,128)}, bf16[256,1280]{1,0:T(8,128)(2,1)S(1)}, bf16[256,1280]{1,0:T(8,128)(2,1)S(1)}) custom-call(s32[2]{0:T(128)S(1)} %pad_add_fusion.refs_0_.place, s32[8,1024]{1,0:T(8,128)S(1)} %get-tuple-element.111.refs_0_.refs_3_.cells_ref, ...), custom_call_target="tpu_custom_call" | custom-call | flops 15000000512 | bytes 8000000 | tf_op jit(solution)/shard_map/backward_attention/pallas_call | solution.py:588
  65.1 2.0 %collective-permute-done.10 = bf16[256,1280]{1,0:T(8,128)(2,1)S(1)} collective-permute-done((bf16[256,1280]{1,0:T(8,128)(2,1)S(1)}, bf16[256,1280]{1,0:T(8,128)(2,1)S(1)}, u32[]{:S(2)}, u32[]{:S(2)}) %collective-permute-start.10) | collective-permute-done | bytes 655392 | tf_op jit(solution)/shard_map/ppermute | solution.py:719
  67.6 2.3 %input_gradient.1.source = f32[1024,512]{1,0:T(8,128)S(1)} custom-call(bf16[512,768]{1,0:T(8,128)(2,1)S(1)} %get-tuple-element.146.w_a, bf16[512,768]{1,0:T(8,128)(2,1)S(1)} %get-tuple-element.147.w_b, f32[1024,512]{1,0:T(8,128)S(1)} %get-tuple-element.148.dh1_ref, bf16[1,384,1024]{2,1,0:T(8,128)(2,1)S(1)} %get-tuple-element.145.refs_0_.trio_a, ...), custom_call_target="tpu_custom_call" | custom-call | flops 1 | bytes 1 | tf_op jit(solution)/shard_map/input_gradient/pallas_call | solution.py:613
  69.9 1.8 %collective-permute-start.12 = (bf16[64,1920]{1,0:T(8,128)(2,1)S(1)}, bf16[64,1920]{1,0:T(8,128)(2,1)S(1)}, u32[]{:S(2)}, u32[]{:S(2)}) collective-permute-start(bf16[64,1920]{1,0:T(8,128)(2,1)S(1)} %get-tuple-element.196), channel_id=1, source_target_pairs={{0,4},{4,0},{8,12},{12,8},{16,20},{20,16},{24,28},{28,24},{1,5},{5... | collective-permute-start | bytes 737288 | tf_op jit(solution)/shard_map/ppermute | solution.py:719
  71.7 2.4 %turn_back.3 = f32[1024,512]{1,0:T(8,128)} custom-call(s32[1]{0:T(128)} %get-tuple-element.108.start, f32[1024,512]{1,0:T(8,128)S(1)} %input_gradient.1.source), custom_call_target="tpu_custom_call" | custom-call | flops 1 | bytes 1 | tf_op jit(solution)/shard_map/turn_back/pallas_call | solution.py:230
  74.1 3.0 %collective-permute-done.13 = bf16[128,1280]{1,0:T(8,128)(2,1)S(1)} collective-permute-done((bf16[128,1280]{1,0:T(8,128)(2,1)S(1)}, bf16[128,1280]{1,0:T(8,128)(2,1)S(1)}, u32[]{:S(2)}, u32[]{:S(2)}) %collective-permute-start.13) | collective-permute-done | bytes 327712 | tf_op jit(solution)/shard_map/ppermute | solution.py:719
  80.5 2.2 %collective-permute-done.15 = bf16[64,1280]{1,0:T(8,128)(2,1)S(1)} collective-permute-done((bf16[64,1280]{1,0:T(8,128)(2,1)S(1)}, bf16[64,1280]{1,0:T(8,128)(2,1)S(1)}, u32[]{:S(2)}, u32[]{:S(2)}) %collective-permute-start.15) | collective-permute-done | bytes 163872 | tf_op jit(solution)/shard_map/ppermute | solution.py:719
  84.4 2.7 %collective-permute-start.16 = (bf16[16,1920]{1,0:T(8,128)(2,1)S(1)}, bf16[16,1920]{1,0:T(8,128)(2,1)S(1)}, u32[]{:S(2)}, u32[]{:S(2)}) collective-permute-start(bf16[16,1920]{1,0:T(8,128)(2,1)S(1)} %add_convert_fusion.13), channel_id=1, source_target_pairs={{0,16},{4,20},{8,24},{12,28},{16,0},{20,4},{24,8},{28,12},{1,17},{... | collective-permute-start | bytes 184328 | tf_op jit(solution)/shard_map/ppermute | solution.py:719
  87.7 2.5 %collective-permute-start.19 = (bf16[16,1280]{1,0:T(8,128)(2,1)S(1)}, bf16[16,1280]{1,0:T(8,128)(2,1)S(1)}, u32[]{:S(2)}, u32[]{:S(2)}) collective-permute-start(bf16[16,1280]{1,0:T(8,128)(2,1)S(1)} %get-tuple-element.204), channel_id=1, source_target_pairs={{0,16},{4,20},{8,24},{12,28},{16,0},{20,4},{24,8},{28,12},{1,17},{... | collective-permute-start | bytes 122888 | tf_op jit(solution)/shard_map/ppermute | solution.py:719
  92.7 2.9 %collective-permute-start.21 = (bf16[16,1152]{1,0:T(8,128)(2,1)S(1)}, bf16[16,1152]{1,0:T(8,128)(2,1)S(1)}, u32[]{:S(2)}, u32[]{:S(2)}) collective-permute-start(bf16[16,1152]{1,0:T(8,128)(2,1)S(1)} %add_convert_fusion.17), channel_id=1, source_target_pairs={{0,16},{4,20},{8,24},{12,28},{16,0},{20,4},{24,8},{28,12},{1,17},{... | collective-permute-start | bytes 110600 | tf_op jit(solution)/shard_map/ppermute | solution.py:719
  97.7 2.2 %collective-permute-start.22 = (bf16[32,1152]{1,0:T(8,128)(2,1)S(1)}, bf16[32,1152]{1,0:T(8,128)(2,1)S(1)}, u32[]{:S(2)}, u32[]{:S(2)}) collective-permute-start(bf16[32,1152]{1,0:T(8,128)(2,1)S(1)} %pad_maximum_fusion.3), channel_id=1, source_target_pairs={{0,8},{4,12},{8,0},{12,4},{16,24},{20,28},{24,16},{28,20},{1,9},{5... | collective-permute-start | bytes 221192 | tf_op jit(solution)/shard_map/ppermute | solution.py:719
  99.9 1.7 %collective-permute-done.20 = bf16[32,1920]{1,0:T(8,128)(2,1)S(1)} collective-permute-done((bf16[32,1920]{1,0:T(8,128)(2,1)S(1)}, bf16[32,1920]{1,0:T(8,128)(2,1)S(1)}, u32[]{:S(2)}, u32[]{:S(2)}) %collective-permute-start.20) | collective-permute-done | bytes 122912 | tf_op jit(solution)/shard_map/ppermute | solution.py:719
  101.6 1.7 %collective-permute-start.27 = (bf16[64,1920]{1,0:T(8,128)(2,1)S(1)}, bf16[64,1920]{1,0:T(8,128)(2,1)S(1)}, u32[]{:S(2)}, u32[]{:S(2)}) collective-permute-start(bf16[64,1920]{1,0:T(8,128)(2,1)S(1)} %pad_maximum_fusion.early.refs_0_), channel_id=1, source_target_pairs={{0,4},{4,0},{8,12},{12,8},{16,20},{20,16},{24,28},{28,24},{1,5},{5... | collective-permute-start | bytes 737288 | tf_op jit(solution)/shard_map/ppermute | solution.py:719
  108.6 3.2 %collective-permute-done.26 = f32[8,128]{1,0:T(8,128)S(1)} collective-permute-done((f32[8,128]{1,0:T(8,128)S(1)}, f32[8,128]{1,0:T(8,128)S(1)}, u32[]{:S(2)}, u32[]{:S(2)}) %collective-permute-start.26) | collective-permute-done | bytes 4128 | tf_op jit(solution)/shard_map/ppermute | solution.py:719
  111.9 4.2 %adam.1 = (f32[128,1536]{1,0:T(8,128)}, f32[128,512]{1,0:T(8,128)}, f32[128,512]{1,0:T(8,128)}, f32[128,512]{1,0:T(8,128)}, f32[9,128]{1,0:T(8,128)}, /*index=5*...) custom-call(s32[2]{0:T(128)S(1)} %pad_add_fusion.refs_0_.place, ...), custom_call_target="tpu_custom_call" | custom-call | tf_op jit(solution)/shard_map/adam/pallas_call | solution.py:706
  (108 shorter events, 29.0 us)
Async XLA Ops:
  2.6 8.7 %collective-permute-start.1 = (bf16[144,768]{1,0:T(8,128)(2,1)}, bf16[144,768]{1,0:T(8,128)(2,1)S(1)}, u32[]{:S(2)}, u32[]{:S(2)}) collective-permute-start(bf16[144,768]{1,0:T(8,128)(2,1)} %pack_first.1.refs_5_), channel_id=1, source_target_pairs={{0,2},{1,3},{2,0},{3,1},{4,6},{5,7},{6,4},{7,5},{8,10},{9,11},{10,... | collective-permute-start | bytes 663560 | tf_op jit(solution)/shard_map/ppermute | solution.py:719
  5.6 7.7 %collective-permute-start = (bf16[144,768]{1,0:T(8,128)(2,1)}, bf16[144,768]{1,0:T(8,128)(2,1)S(1)}, u32[]{:S(2)}, u32[]{:S(2)}) collective-permute-start(bf16[144,768]{1,0:T(8,128)(2,1)} %pack_first.1.refs_5_), channel_id=1, source_target_pairs={{0,1},{1,0},{2,3},{3,2},{4,5},{5,4},{6,7},{7,6},{8,9},{9,8},{10,11... | collective-permute-start | bytes 663560 | tf_op jit(solution)/shard_map/ppermute | solution.py:719
  11.3 8.9 %collective-permute-start.4 = (bf16[128,768]{1,0:T(8,128)(2,1)}, bf16[128,768]{1,0:T(8,128)(2,1)}, u32[]{:S(2)}, u32[]{:S(2)}) collective-permute-start(bf16[128,768]{1,0:T(8,128)(2,1)} %get-tuple-element.123.refs_5_), channel_id=1, source_target_pairs={{0,2},{1,3},{2,0},{3,1},{4,6},{5,7},{6,4},{7,5},{8,10},{9,11},{10,... | collective-permute-start | bytes 589832 | tf_op jit(solution)/shard_map/ppermute | solution.py:719
  13.0 16.3 %collective-permute-start.7 = (bf16[128,1536]{1,0:T(8,128)(2,1)}, bf16[128,1536]{1,0:T(8,128)(2,1)}, u32[]{:S(2)}, u32[]{:S(2)}) collective-permute-start(bf16[128,1536]{1,0:T(8,128)(2,1)} %get-tuple-element.135.refs_6_), channel_id=1, source_target_pairs={{0,2},{1,3},{2,0},{3,1},{4,6},{5,7},{6,4},{7,5},{8,10},{9,11},{10,... | collective-permute-start | bytes 1179656 | tf_op jit(solution)/shard_map/ppermute | solution.py:719
  13.3 7.6 %collective-permute-start.3 = (bf16[128,768]{1,0:T(8,128)(2,1)}, bf16[128,768]{1,0:T(8,128)(2,1)}, u32[]{:S(2)}, u32[]{:S(2)}) collective-permute-start(bf16[128,768]{1,0:T(8,128)(2,1)} %get-tuple-element.123.refs_5_), channel_id=1, source_target_pairs={{0,1},{1,0},{2,3},{3,2},{4,5},{5,4},{6,7},{7,6},{8,9},{9,8},{10,11... | collective-permute-start | bytes 589832 | tf_op jit(solution)/shard_map/ppermute | solution.py:719
  20.8 9.0 %collective-permute-start.6 = (bf16[128,1536]{1,0:T(8,128)(2,1)}, bf16[128,1536]{1,0:T(8,128)(2,1)S(1)}, u32[]{:S(2)}, u32[]{:S(2)}) collective-permute-start(bf16[128,1536]{1,0:T(8,128)(2,1)} %get-tuple-element.135.refs_6_), channel_id=1, source_target_pairs={{0,1},{1,0},{2,3},{3,2},{4,5},{5,4},{6,7},{7,6},{8,9},{9,8},{10,11... | collective-permute-start | bytes 1179656 | tf_op jit(solution)/shard_map/ppermute | solution.py:719
  50.7 14.3 %collective-permute-start.11 = (bf16[128,1920]{1,0:T(8,128)(2,1)S(1)}, bf16[128,1920]{1,0:T(8,128)(2,1)S(1)}, u32[]{:S(2)}, u32[]{:S(2)}) collective-permute-start(bf16[128,1920]{1,0:T(8,128)(2,1)S(1)} %get-tuple-element.192.refs_12_), channel_id=1, source_target_pairs={{0,2},{1,3},{2,0},{3,1},{4,6},{5,7},{6,4},{7,5},{8,10},{9,11},{10,... | collective-permute-start | bytes 1474568 | tf_op jit(solution)/shard_map/ppermute | solution.py:719
  67.2 9.8 %collective-permute-start.13 = (bf16[128,1280]{1,0:T(8,128)(2,1)S(1)}, bf16[128,1280]{1,0:T(8,128)(2,1)S(1)}, u32[]{:S(2)}, u32[]{:S(2)}) collective-permute-start(bf16[128,1280]{1,0:T(8,128)(2,1)S(1)} %get-tuple-element.194.refs_0_), channel_id=1, source_target_pairs={{0,2},{1,3},{2,0},{3,1},{4,6},{5,7},{6,4},{7,5},{8,10},{9,11},{10,... | collective-permute-start | bytes 983048 | tf_op jit(solution)/shard_map/ppermute | solution.py:719
  69.9 8.9 %collective-permute-start.12 = (bf16[64,1920]{1,0:T(8,128)(2,1)S(1)}, bf16[64,1920]{1,0:T(8,128)(2,1)S(1)}, u32[]{:S(2)}, u32[]{:S(2)}) collective-permute-start(bf16[64,1920]{1,0:T(8,128)(2,1)S(1)} %get-tuple-element.196), channel_id=1, source_target_pairs={{0,4},{4,0},{8,12},{12,8},{16,20},{20,16},{24,28},{28,24},{1,5},{5... | collective-permute-start | bytes 737288 | tf_op jit(solution)/shard_map/ppermute | solution.py:719
  77.2 5.5 %collective-permute-start.15 = (bf16[64,1280]{1,0:T(8,128)(2,1)S(1)}, bf16[64,1280]{1,0:T(8,128)(2,1)S(1)}, u32[]{:S(2)}, u32[]{:S(2)}) collective-permute-start(bf16[64,1280]{1,0:T(8,128)(2,1)S(1)} %get-tuple-element.198), channel_id=1, source_target_pairs={{0,4},{4,0},{8,12},{12,8},{16,20},{20,16},{24,28},{28,24},{1,5},{5... | collective-permute-start | bytes 491528 | tf_op jit(solution)/shard_map/ppermute | solution.py:719
  78.9 5.5 %collective-permute-start.14 = (bf16[32,1920]{1,0:T(8,128)(2,1)S(1)}, bf16[32,1920]{1,0:T(8,128)(2,1)S(1)}, u32[]{:S(2)}, u32[]{:S(2)}) collective-permute-start(bf16[32,1920]{1,0:T(8,128)(2,1)S(1)} %get-tuple-element.199), channel_id=1, source_target_pairs={{0,8},{4,12},{8,0},{12,4},{16,24},{20,28},{24,16},{28,20},{1,9},{5... | collective-permute-start | bytes 368648 | tf_op jit(solution)/shard_map/ppermute | solution.py:719
  82.8 4.9 %collective-permute-start.17 = (bf16[32,1280]{1,0:T(8,128)(2,1)S(1)}, bf16[32,1280]{1,0:T(8,128)(2,1)S(1)}, u32[]{:S(2)}, u32[]{:S(2)}) collective-permute-start(bf16[32,1280]{1,0:T(8,128)(2,1)S(1)} %get-tuple-element.202), channel_id=1, source_target_pairs={{0,8},{4,12},{8,0},{12,4},{16,24},{20,28},{24,16},{28,20},{1,9},{5... | collective-permute-start | bytes 245768 | tf_op jit(solution)/shard_map/ppermute | solution.py:719
  84.4 6.3 %collective-permute-start.16 = (bf16[16,1920]{1,0:T(8,128)(2,1)S(1)}, bf16[16,1920]{1,0:T(8,128)(2,1)S(1)}, u32[]{:S(2)}, u32[]{:S(2)}) collective-permute-start(bf16[16,1920]{1,0:T(8,128)(2,1)S(1)} %add_convert_fusion.13), channel_id=1, source_target_pairs={{0,16},{4,20},{8,24},{12,28},{16,0},{20,4},{24,8},{28,12},{1,17},{... | collective-permute-start | bytes 184328 | tf_op jit(solution)/shard_map/ppermute | solution.py:719
  87.7 5.0 %collective-permute-start.19 = (bf16[16,1280]{1,0:T(8,128)(2,1)S(1)}, bf16[16,1280]{1,0:T(8,128)(2,1)S(1)}, u32[]{:S(2)}, u32[]{:S(2)}) collective-permute-start(bf16[16,1280]{1,0:T(8,128)(2,1)S(1)} %get-tuple-element.204), channel_id=1, source_target_pairs={{0,16},{4,20},{8,24},{12,28},{16,0},{20,4},{24,8},{28,12},{1,17},{... | collective-permute-start | bytes 122888 | tf_op jit(solution)/shard_map/ppermute | solution.py:719
  90.8 5.8 %collective-permute-start.18 = (bf16[16,1920]{1,0:T(8,128)(2,1)S(1)}, bf16[16,1920]{1,0:T(8,128)(2,1)S(1)}, u32[]{:S(2)}, u32[]{:S(2)}) collective-permute-start(bf16[16,1920]{1,0:T(8,128)(2,1)S(1)} %add_convert_fusion.12), channel_id=1, source_target_pairs={{0,16},{4,20},{8,24},{12,28},{16,0},{20,4},{24,8},{28,12},{1,17},{... | collective-permute-start | bytes 184328 | tf_op jit(solution)/shard_map/ppermute | solution.py:719
  92.7 5.0 %collective-permute-start.21 = (bf16[16,1152]{1,0:T(8,128)(2,1)S(1)}, bf16[16,1152]{1,0:T(8,128)(2,1)S(1)}, u32[]{:S(2)}, u32[]{:S(2)}) collective-permute-start(bf16[16,1152]{1,0:T(8,128)(2,1)S(1)} %add_convert_fusion.17), channel_id=1, source_target_pairs={{0,16},{4,20},{8,24},{12,28},{16,0},{20,4},{24,8},{28,12},{1,17},{... | collective-permute-start | bytes 110600 | tf_op jit(solution)/shard_map/ppermute | solution.py:719
  96.6 4.9 %collective-permute-start.20 = (bf16[32,1920]{1,0:T(8,128)(2,1)S(1)}, bf16[32,1920]{1,0:T(8,128)(2,1)S(1)}, u32[]{:S(2)}, u32[]{:S(2)}) collective-permute-start(bf16[32,1920]{1,0:T(8,128)(2,1)S(1)} %pad_maximum_fusion.2), channel_id=1, source_target_pairs={{0,8},{4,12},{8,0},{12,4},{16,24},{20,28},{24,16},{28,20},{1,9},{5... | collective-permute-start | bytes 368648 | tf_op jit(solution)/shard_map/ppermute | solution.py:719
  97.7 5.6 %collective-permute-start.22 = (bf16[32,1152]{1,0:T(8,128)(2,1)S(1)}, bf16[32,1152]{1,0:T(8,128)(2,1)S(1)}, u32[]{:S(2)}, u32[]{:S(2)}) collective-permute-start(bf16[32,1152]{1,0:T(8,128)(2,1)S(1)} %pad_maximum_fusion.3), channel_id=1, source_target_pairs={{0,8},{4,12},{8,0},{12,4},{16,24},{20,28},{24,16},{28,20},{1,9},{5... | collective-permute-start | bytes 221192 | tf_op jit(solution)/shard_map/ppermute | solution.py:719
  101.6 10.2 %collective-permute-start.27 = (bf16[64,1920]{1,0:T(8,128)(2,1)S(1)}, bf16[64,1920]{1,0:T(8,128)(2,1)S(1)}, u32[]{:S(2)}, u32[]{:S(2)}) collective-permute-start(bf16[64,1920]{1,0:T(8,128)(2,1)S(1)} %pad_maximum_fusion.early.refs_0_), channel_id=1, source_target_pairs={{0,4},{4,0},{8,12},{12,8},{16,20},{20,16},{24,28},{28,24},{1,5},{5... | collective-permute-start | bytes 737288 | tf_op jit(solution)/shard_map/ppermute | solution.py:719
  104.0 3.1 %collective-permute-start.25 = (f32[8,128]{1,0:T(8,128)S(1)}, f32[8,128]{1,0:T(8,128)S(1)}, u32[]{:S(2)}, u32[]{:S(2)}) collective-permute-start(f32[8,128]{1,0:T(8,128)S(1)} %half_squares.1), channel_id=1, source_target_pairs={{0,3},{1,2},{2,1},{3,0},{4,7},{5,6},{6,5},{7,4},{8,11},{9,10},{10,... | collective-permute-start | bytes 12296 | tf_op jit(solution)/shard_map/ppermute | solution.py:719
  104.1 3.7 %collective-permute-start.24 = (f32[8,128]{1,0:T(8,128)S(1)}, f32[8,128]{1,0:T(8,128)S(1)}, u32[]{:S(2)}, u32[]{:S(2)}) collective-permute-start(f32[8,128]{1,0:T(8,128)S(1)} %half_squares.1), channel_id=1, source_target_pairs={{0,2},{1,3},{2,0},{3,1},{4,6},{5,7},{6,4},{7,5},{8,10},{9,11},{10,... | collective-permute-start | bytes 12296 | tf_op jit(solution)/shard_map/ppermute | solution.py:719
  104.5 3.3 %collective-permute-start.23 = (f32[8,128]{1,0:T(8,128)S(1)}, f32[8,128]{1,0:T(8,128)S(1)}, u32[]{:S(2)}, u32[]{:S(2)}) collective-permute-start(f32[8,128]{1,0:T(8,128)S(1)} %half_squares.1), channel_id=1, source_target_pairs={{0,1},{1,0},{2,3},{3,2},{4,5},{5,4},{6,7},{7,6},{8,9},{9,8},{10,11... | collective-permute-start | bytes 12296 | tf_op jit(solution)/shard_map/ppermute | solution.py:719
  106.0 5.9 %collective-permute-start.28 = (bf16[64,1152]{1,0:T(8,128)(2,1)S(1)}, bf16[64,1152]{1,0:T(8,128)(2,1)S(1)}, u32[]{:S(2)}, u32[]{:S(2)}) collective-permute-start(bf16[64,1152]{1,0:T(8,128)(2,1)S(1)} %pad_maximum_fusion.1.late.refs_2_), channel_id=1, source_target_pairs={{0,4},{4,0},{8,12},{12,8},{16,20},{20,16},{24,28},{28,24},{1,5},{5... | collective-permute-start | bytes 442376 | tf_op jit(solution)/shard_map/ppermute | solution.py:719
  107.8 4.0 %collective-permute-start.26 = (f32[8,128]{1,0:T(8,128)S(1)}, f32[8,128]{1,0:T(8,128)S(1)}, u32[]{:S(2)}, u32[]{:S(2)}) collective-permute-start(f32[8,128]{1,0:T(8,128)S(1)} %add_add_fusion), channel_id=1, source_target_pairs={{0,4},{4,0},{8,12},{12,8},{16,20},{20,16},{24,28},{28,24},{1,5},{5... | collective-permute-start | bytes 12296 | tf_op jit(solution)/shard_map/ppermute | solution.py:719
  (25 other events, 446.9 us)

commit v5 on v4

--- a/solution.py
+++ b/solution.py
@@ -17,8 +17,8 @@
 TOK_DEV = 1024
 QT = 256
 HALF = TOK_DEV // 2
-TILES = 2
-MT = 256
+TILES = 1
+MT = 512
 STEP = 10
 NORM_EPS = 1e-05
 ADAM_EPS = 1e-08
@@ -597,28 +597,30 @@
     )(place, cells, tokens_t, vec_sums, d_t, *flat, *inner, *later)
 
 
-def input_grad_kernel(w_a, w_b, dh1_ref, trio_a, trio_b, *refs):
-    out = refs[-1]
+def input_grad_kernel(start, w_a, w_b, dh1_ref, trio_a, trio_b, *refs):
+    out, turned = refs[-2:]
     trios = [ref.at[number] for ref in (trio_a, trio_b) for number in range(ref.shape[0])]
     for tile in range(TOK_DEV // QT):
         here = slice(tile * QT, (tile + 1) * QT)
         total = None
-        for w_ref, trio in ((w_a, trios[:GROUP]), (w_b, trios[GROUP:])):
-            term = dot(w_ref[...], jnp.concatenate([part[:, here] for part in trio], 0), NN)
+        for w_ref, parts in ((w_a, trios[:GROUP]), (w_b, trios[GROUP:])):
+            term = dot(w_ref[...], jnp.concatenate([part[:, here] for part in parts], 0), NN)
             total = term if total is None else total + term
-        out[here, :] = dh1_ref[here, :] + total.T
-
-
-def input_gradient(weights, d_h1, trios, later):
+        turned[here, :] = dh1_ref[here, :] + total.T
+    turn_rows(turned, (TOK_DEV - start[0]) & (TOK_DEV - 1), write_into(out))
+
+
+def input_gradient(start, weights, d_h1, trios, later):
     return pl.pallas_call(
         input_grad_kernel,
-        in_specs=[VM] * 5 + [ANY] * len(later),
+        in_specs=[SMEM] + [VM] * 5 + [ANY] * len(later),
         out_specs=VM,
         out_shape=sds((TOK_DEV, D), F32),
+        scratch_shapes=[pltpu.VMEM((TOK_DEV, D), F32)],
         compiler_params=params(),
         cost_estimate=cost(1, 1),
         name="input_gradient",
-    )(*weights, d_h1, *trios, *later)
+    )(start, *weights, d_h1, *trios, *later)
 
 
 def adam(weight, grad, first, second, rate, decay):
@@ -855,37 +857,35 @@
         e_arrived = swap(e_send, "wide", 1)
         b_keep, b_send = fold(b_keep, after(b_arrived, e_send))
         b_arrived = swap(b_send, "narrow", 2)
-        turned_grad = input_gradient(weights, d_h1, trios, [b_send])
-        input_grad = turn_back(start, turned_grad, [])
-        b_keep, b_send = fold(b_keep, after(b_arrived, input_grad))
-        b_arrived = swap(b_send, "wide", 1)
-        e_keep, e_send = fold(e_keep, after(e_arrived, b_send))
+        input_grad = input_gradient(start, weights, d_h1, trios, [b_send, e_send])
+        e_keep, e_send = fold(e_keep, after(e_arrived, input_grad))
         e_arrived = swap(e_send, "wide", 2)
         b_keep, b_send = fold(b_keep, after(b_arrived, e_send))
-        b_arrived = swap(b_send, "wide", 2)
+        b_arrived = swap(b_send, "wide", 1)
         e_keep, e_send = fold(e_keep, after(e_arrived, b_send))
         e_arrived = swap(e_send, "wide", 4)
         b_keep, b_send = fold(b_keep, after(b_arrived, e_send))
-        b_arrived = swap(b_send, "wide", 4)
+        b_arrived = swap(b_send, "wide", 2)
         e_low = add_low(e_keep, after(e_arrived, b_send))
         e_arrived = swap(e_low, "wide", 4)
+        b_keep, b_send = fold(b_keep, after(b_arrived, e_low))
+        b_arrived = swap(b_send, "wide", 4)
+        e_low = join(e_low, after(e_arrived, b_send))
+        e_arrived = swap(e_low, "wide", 2)
+        b_arrived = after(b_arrived, e_low)
         vec_total = b_keep[:, LATE:].astype(F32) + b_arrived[:, LATE:].astype(F32)
         b_low = add_low(b_keep[:, :LATE], b_arrived[:, :LATE])
         b_arrived = swap(b_low, "wide", 4)
         e_low = join(e_low, after(e_arrived, b_low))
-        e_arrived = swap(e_low, "wide", 2)
         b_low = join(b_low, after(b_arrived, e_low))
-        b_arrived = swap(b_low, "wide", 2)
-        e_low = join(e_low, after(e_arrived, b_low))
-        b_low = join(b_low, after(b_arrived, e_low))
+        b_low = join(b_low, swap(b_low, "wide", 2))
         e_arrived, b_arrived = swap(e_low, "wide", 1), swap(b_low, "wide", 1)
         squares = half_squares(place, e_low, b_low, vec_total)
         squares = four(squares, directly(squares, "narrow", (1, 2, 3)))
         squares = squares + swap(squares, "wide", 1)
         grads = [e_low, after(e_arrived, squares), b_low, after(b_arrived, squares)]
     else:
-        turned_grad = input_gradient(weights, d_h1, trios, [])
-        input_grad, mixed = turn_back(start, turned_grad, []), turn_back(start, mixed, [])
+        input_grad, mixed = input_gradient(start, weights, d_h1, trios, []), turn_back(start, mixed, [])
         vec_total = lax.psum_scatter(vec_sums, "narrow", scatter_dimension=1, tiled=True)
         vec_total = lax.psum(vec_total, "wide")
         grads = []

time: 117 us -> 115 us (0.983)
  waiting for transfers between devices: 19.2 us -> 15.4 us
  starting transfers between devices: 33.1 us -> 35.7 us
    ppermute x29, waiting for transfers between devices: 19.2 us -> 15.4 us  [swap(): return lax.ppermute(value, axis, [(i, i ^ mask) for i in range(size)])]
    ppermute x29, starting transfers between devices: 33.1 us -> 35.7 us  [swap(): return lax.ppermute(value, axis, [(i, i ^ mask) for i in range(size)])]
    pallas_call x1, Pallas kernels: 2.27 us -> 4.66 us  [input_gradient(): pl.pallas_call(input_grad_kernel, in_specs=[SMEM] + [VM] * 5 + [ANY] * le...]
    pallas_call x2 -> x1, Pallas kernels: 4.73 us -> 2.34 us  [turn_back(): pl.pallas_call(turn_back_kernel, in_specs=[SMEM, VM] + [ANY] * len(later)...]
  transfers between devices with their start and end apart: 29 -> 29, of which waited for: 15 -> 13; matrix products, arithmetic and copies ran while one was open for 1% -> 1% of each run, Pallas kernels for 30% -> 30%
where the time goes in v5:
time: 115 us
  Pallas kernels  57.4 us (50%)
  starting transfers between devices  35.7 us (31%)
  waiting for transfers between devices  15.4 us (13%)
  local copies, waits for them, and re-layouts  3.5 us (3%)
  other arithmetic  1.66 us (1%)
  between operations  1.28 us (1%)
    ppermute x29, starting transfers between devices, swap(): return lax.ppermute(value, axis, [(i, i ^ mask) for i in range(size)])  35.7 us
    pallas_call x2, Pallas kernels, backward_attention(): pl.pallas_call(functools.partial(backward_kernel, n_shards, stages, plan,...  18.7 us
    ppermute x29, waiting for transfers between devices, swap(): return lax.ppermute(value, axis, [(i, i ^ mask) for i in range(size)])  15.4 us
    pallas_call x2, Pallas kernels, forward_attention(): pl.pallas_call(functools.partial(forward_kernel, order, len(pieces), base...  11.7 us
    pallas_call x1, Pallas kernels, middle(): pl.pallas_call(functools.partial(middle_kernel, order, len(pieces)), grid...  9.98 us
    pallas_call x1, Pallas kernels, input_gradient(): pl.pallas_call(input_grad_kernel, in_specs=[SMEM] + [VM] * 5 + [ANY] * le...  4.66 us
    pallas_call x1, Pallas kernels, adam_step(): pl.pallas_call(functools.partial(adam_kernel, quick, limit), grid=(steps,...  4.19 us
    unnamed x40, local copies, waits for them, and re-layouts  3.5 us
  transfers between devices with their start and end apart: 29, of which 13 were waited for; matrix products, arithmetic and copies ran while one was open for 1% of the time, Pallas kernels for 30%

profile of v5, /device:TPU:0, one launch (start us, length us, event | category | flops | bytes accessed | tf_op | source)
XLA Modules:
  0.0 114.9 jit_solution(14589204637096274211)
XLA Ops:
  0.7 1.9 %pack_first.1.refs_5_ = bf16[144,768]{1,0:T(8,128)(2,1)} custom-call(f32[128,1536]{1,0:T(8,128)} %refs_5_.1, f32[9,128]{1,0:T(8,128)} %refs_9_.1), custom_call_target="tpu_custom_call" | custom-call | tf_op jit(solution)/shard_map/pack_first/pallas_call | solution.py:104
  2.6 3.0 %collective-permute-start.1 = (bf16[144,768]{1,0:T(8,128)(2,1)}, bf16[144,768]{1,0:T(8,128)(2,1)S(1)}, u32[]{:S(2)}, u32[]{:S(2)}) collective-permute-start(bf16[144,768]{1,0:T(8,128)(2,1)} %pack_first.1.refs_5_), channel_id=1, source_target_pairs={{0,2},{1,3},{2,0},{3,1},{4,6},{5,7},{6,4},{7,5},{8,10},{9,11},{10,... | collective-permute-start | bytes 663560 | tf_op jit(solution)/shard_map/ppermute | solution.py:721
  11.3 1.7 %collective-permute-start.4 = (bf16[128,768]{1,0:T(8,128)(2,1)}, bf16[128,768]{1,0:T(8,128)(2,1)}, u32[]{:S(2)}, u32[]{:S(2)}) collective-permute-start(bf16[128,768]{1,0:T(8,128)(2,1)} %get-tuple-element.123.refs_5_), channel_id=1, source_target_pairs={{0,2},{1,3},{2,0},{3,1},{4,6},{5,7},{6,4},{7,5},{8,10},{9,11},{10,... | collective-permute-start | bytes 589832 | tf_op jit(solution)/shard_map/ppermute | solution.py:721
  14.6 5.6 %forward_attention.2 = (bf16[256,1024]{1,0:T(8,128)(2,1)S(1)}, f32[2,8,1024]{2,1,0:T(8,128)S(1)}, bf16[2,1024,128]{2,1,0:T(8,128)(2,1)S(1)}, bf16[2,1024,128]{2,...) custom-call(s32[2]{0:T(128)S(1)} %pad_add_fusion.refs_0_.place, ...), custom_call_target="tpu_custom_call" | custom-call | flops 1 | bytes 1 | tf_op jit(solution)/shard_map/forward_attention/pallas_call | solution.py:337
  22.1 6.1 %forward_attention.3 = (bf16[256,1024]{1,0:T(8,128)(2,1)S(1)}, f32[2,8,1024]{2,1,0:T(8,128)S(1)}, bf16[2,1024,128]{2,1,0:T(8,128)(2,1)S(1)}, bf16[2,1024,128]{2,...) custom-call(s32[2]{0:T(128)S(1)} %pad_add_fusion.refs_0_.place, ...), custom_call_target="tpu_custom_call" | custom-call | flops 1 | bytes 1 | tf_op jit(solution)/shard_map/forward_attention/pallas_call | solution.py:337
  31.3 10.0 %middle.1 = (bf16[1024,512]{1,0:T(8,128)(2,1)S(1)}, f32[1024,512]{1,0:T(8,128)S(1)}, bf16[512,1024]{1,0:T(8,128)(2,1)S(1)}, f32[16,512]{1,0:T(8,128)S(1)}, bf16[...) custom-call(s32[2]{0:T(128)S(1)} %pad_add_fusion.refs_0_.place, ...), custom_call_target="tpu_custom_call" | custom-call | flops 10000000000 | bytes 12000000 | tf_op jit(solution)/shard_map/middle/pallas_call | solution.py:481
  41.3 6.3 %backward_attention.2 = (bf16[1,384,1024]{2,1,0:T(8,128)(2,1)S(1)}, f32[16,512]{1,0:T(8,128)S(1)}, bf16[256,1920]{1,0:T(8,128)(2,1)S(1)}, bf16[256,1920]{1,0:T(8,128)(2,1)S(1)}) custom-call(s32[2]{0:T(128)S(1)} %pad_add_fusion.refs_0_.place, s32[8,1024]{1,0:T(8,128)S(1)} %get-tuple-element.111.refs_0_.refs_3_.cells_ref, ...), custom_call_target="tpu_custom_call" | custom-call | flops 5000000000 | bytes 8000000 | tf_op jit(solution)/shard_map/backward_attention/pallas_call | solution.py:588
  48.0 2.3 %turn_back.1 = bf16[1024,512]{1,0:T(8,128)(2,1)} custom-call(s32[1]{0:T(128)} %get-tuple-element.108.start, bf16[1024,512]{1,0:T(8,128)(2,1)S(1)} %get-tuple-element.137.source, bf16[1,384,1024]{2,1,0:T(8,128)(2,1)S(1)} %get-tuple-element.145.refs_0_.trio_a), custom_call_target="tpu_custom_call" | custom-call | flops 1 | bytes 1 | tf_op jit(solution)/shard_map/turn_back/pallas_call | solution.py:230
  50.6 1.8 %collective-permute-start.11 = (bf16[128,1920]{1,0:T(8,128)(2,1)S(1)}, bf16[128,1920]{1,0:T(8,128)(2,1)S(1)}, u32[]{:S(2)}, u32[]{:S(2)}) collective-permute-start(bf16[128,1920]{1,0:T(8,128)(2,1)S(1)} %get-tuple-element.192.refs_12_), channel_id=1, source_target_pairs={{0,2},{1,3},{2,0},{3,1},{4,6},{5,7},{6,4},{7,5},{8,10},{9,11},{10,... | collective-permute-start | bytes 1474568 | tf_op jit(solution)/shard_map/ppermute | solution.py:721
  52.4 12.4 %backward_attention.3 = (bf16[3,384,1024]{2,1,0:T(8,128)(2,1)S(1)}, f32[16,512]{1,0:T(8,128)}, bf16[256,1280]{1,0:T(8,128)(2,1)S(1)}, bf16[256,1280]{1,0:T(8,128)(2,1)S(1)}) custom-call(s32[2]{0:T(128)S(1)} %pad_add_fusion.refs_0_.place, s32[8,1024]{1,0:T(8,128)S(1)} %get-tuple-element.111.refs_0_.refs_3_.cells_ref, ...), custom_call_target="tpu_custom_call" | custom-call | flops 15000000512 | bytes 8000000 | tf_op jit(solution)/shard_map/backward_attention/pallas_call | solution.py:588
  64.9 1.6 %collective-permute-start.12 = (bf16[64,1920]{1,0:T(8,128)(2,1)S(1)}, bf16[64,1920]{1,0:T(8,128)(2,1)S(1)}, u32[]{:S(2)}, u32[]{:S(2)}) collective-permute-start(bf16[64,1920]{1,0:T(8,128)(2,1)S(1)} %get-tuple-element.196.refs_1_), channel_id=1, source_target_pairs={{0,4},{4,0},{8,12},{12,8},{16,20},{20,16},{24,28},{28,24},{1,5},{5... | collective-permute-start | bytes 737288 | tf_op jit(solution)/shard_map/ppermute | solution.py:721
  67.6 4.7 %input_gradient.1 = f32[1024,512]{1,0:T(8,128)} custom-call(s32[1]{0:T(128)} %get-tuple-element.108.start, bf16[512,768]{1,0:T(8,128)(2,1)S(1)} %get-tuple-element.146.w_a, bf16[512,768]{1,0:T(8,128)(2,1)S(1)} %get-tuple-element.147.w_b, f32[1024,512]{1,0:T(8,128)S(1)} %get-tuple-element.148.dh1_ref, ...), custom_call_target="tpu_custom_call" | custom-call | flops 1 | bytes 1 | tf_op jit(solution)/shard_map/input_gradient/pallas_call | solution.py:614
  73.6 1.6 %collective-permute-start.13 = (bf16[32,1920]{1,0:T(8,128)(2,1)S(1)}, bf16[32,1920]{1,0:T(8,128)(2,1)S(1)}, u32[]{:S(2)}, u32[]{:S(2)}) collective-permute-start(bf16[32,1920]{1,0:T(8,128)(2,1)S(1)} %get-tuple-element.199), channel_id=1, source_target_pairs={{0,8},{4,12},{8,0},{12,4},{16,24},{20,28},{24,16},{28,20},{1,9},{5... | collective-permute-start | bytes 368648 | tf_op jit(solution)/shard_map/ppermute | solution.py:721
  75.2 1.7 %collective-permute-done.14 = bf16[128,1280]{1,0:T(8,128)(2,1)S(1)} collective-permute-done((bf16[128,1280]{1,0:T(8,128)(2,1)S(1)}, bf16[128,1280]{1,0:T(8,128)(2,1)S(1)}, u32[]{:S(2)}, u32[]{:S(2)}) %collective-permute-start.14) | collective-permute-done | bytes 327712 | tf_op jit(solution)/shard_map/ppermute | solution.py:721
  78.6 2.7 %collective-permute-start.15 = (bf16[16,1920]{1,0:T(8,128)(2,1)S(1)}, bf16[16,1920]{1,0:T(8,128)(2,1)S(1)}, u32[]{:S(2)}, u32[]{:S(2)}) collective-permute-start(bf16[16,1920]{1,0:T(8,128)(2,1)S(1)} %add_convert_fusion.13), channel_id=1, source_target_pairs={{0,16},{4,20},{8,24},{12,28},{16,0},{20,4},{24,8},{28,12},{1,17},{... | collective-permute-start | bytes 184328 | tf_op jit(solution)/shard_map/ppermute | solution.py:721
  82.5 1.6 %collective-permute-start.18 = (bf16[32,1280]{1,0:T(8,128)(2,1)S(1)}, bf16[32,1280]{1,0:T(8,128)(2,1)S(1)}, u32[]{:S(2)}, u32[]{:S(2)}) collective-permute-start(bf16[32,1280]{1,0:T(8,128)(2,1)S(1)} %get-tuple-element.202), channel_id=1, source_target_pairs={{0,8},{4,12},{8,0},{12,4},{16,24},{20,28},{24,16},{28,20},{1,9},{5... | collective-permute-start | bytes 245768 | tf_op jit(solution)/shard_map/ppermute | solution.py:721
  84.2 2.7 %collective-permute-start.17 = (bf16[16,1920]{1,0:T(8,128)(2,1)S(1)}, bf16[16,1920]{1,0:T(8,128)(2,1)S(1)}, u32[]{:S(2)}, u32[]{:S(2)}) collective-permute-start(bf16[16,1920]{1,0:T(8,128)(2,1)S(1)} %add_convert_fusion.12), channel_id=1, source_target_pairs={{0,16},{4,20},{8,24},{12,28},{16,0},{20,4},{24,8},{28,12},{1,17},{... | collective-permute-start | bytes 184328 | tf_op jit(solution)/shard_map/ppermute | solution.py:721
  87.4 2.3 %collective-permute-start.20 = (bf16[16,1280]{1,0:T(8,128)(2,1)S(1)}, bf16[16,1280]{1,0:T(8,128)(2,1)S(1)}, u32[]{:S(2)}, u32[]{:S(2)}) collective-permute-start(bf16[16,1280]{1,0:T(8,128)(2,1)S(1)} %get-tuple-element.204), channel_id=1, source_target_pairs={{0,16},{4,20},{8,24},{12,28},{16,0},{20,4},{24,8},{28,12},{1,17},{... | collective-permute-start | bytes 122888 | tf_op jit(solution)/shard_map/ppermute | solution.py:721
  89.7 2.2 %collective-permute-start.19 = (bf16[32,1920]{1,0:T(8,128)(2,1)S(1)}, bf16[32,1920]{1,0:T(8,128)(2,1)S(1)}, u32[]{:S(2)}, u32[]{:S(2)}) collective-permute-start(bf16[32,1920]{1,0:T(8,128)(2,1)S(1)} %pad_maximum_fusion.2), channel_id=1, source_target_pairs={{0,8},{4,12},{8,0},{12,4},{16,24},{20,28},{24,16},{28,20},{1,9},{5... | collective-permute-start | bytes 368648 | tf_op jit(solution)/shard_map/ppermute | solution.py:721
  92.6 2.2 %collective-permute-start.21 = (bf16[16,1152]{1,0:T(8,128)(2,1)S(1)}, bf16[16,1152]{1,0:T(8,128)(2,1)S(1)}, u32[]{:S(2)}, u32[]{:S(2)}) collective-permute-start(bf16[16,1152]{1,0:T(8,128)(2,1)S(1)} %add_convert_fusion.17), channel_id=1, source_target_pairs={{0,16},{4,20},{8,24},{12,28},{16,0},{20,4},{24,8},{28,12},{1,17},{... | collective-permute-start | bytes 110600 | tf_op jit(solution)/shard_map/ppermute | solution.py:721
  94.8 2.7 %collective-permute-done.21 = bf16[16,1152]{1,0:T(8,128)(2,1)S(1)} collective-permute-done((bf16[16,1152]{1,0:T(8,128)(2,1)S(1)}, bf16[16,1152]{1,0:T(8,128)(2,1)S(1)}, u32[]{:S(2)}, u32[]{:S(2)}) %collective-permute-start.21) | collective-permute-done | bytes 36896 | tf_op jit(solution)/shard_map/ppermute | solution.py:721
  97.5 1.9 %collective-permute-start.22 = (bf16[32,1152]{1,0:T(8,128)(2,1)S(1)}, bf16[32,1152]{1,0:T(8,128)(2,1)S(1)}, u32[]{:S(2)}, u32[]{:S(2)}) collective-permute-start(bf16[32,1152]{1,0:T(8,128)(2,1)S(1)} %pad_maximum_fusion.3), channel_id=1, source_target_pairs={{0,8},{4,12},{8,0},{12,4},{16,24},{20,28},{24,16},{28,20},{1,9},{5... | collective-permute-start | bytes 221192 | tf_op jit(solution)/shard_map/ppermute | solution.py:721
  108.0 2.4 %collective-permute-done.26 = f32[8,128]{1,0:T(8,128)S(1)} collective-permute-done((f32[8,128]{1,0:T(8,128)S(1)}, f32[8,128]{1,0:T(8,128)S(1)}, u32[]{:S(2)}, u32[]{:S(2)}) %collective-permute-start.26) | collective-permute-done | bytes 4128 | tf_op jit(solution)/shard_map/ppermute | solution.py:721
  110.5 4.2 %adam.1 = (f32[128,1536]{1,0:T(8,128)}, f32[128,512]{1,0:T(8,128)}, f32[128,512]{1,0:T(8,128)}, f32[128,512]{1,0:T(8,128)}, f32[9,128]{1,0:T(8,128)}, /*index=5*...) custom-call(s32[2]{0:T(128)S(1)} %pad_add_fusion.refs_0_.place, ...), custom_call_target="tpu_custom_call" | custom-call | tf_op jit(solution)/shard_map/adam/pallas_call | solution.py:708
  (107 shorter events, 28.1 us)
Async XLA Ops:
  2.6 8.7 %collective-permute-start.1 = (bf16[144,768]{1,0:T(8,128)(2,1)}, bf16[144,768]{1,0:T(8,128)(2,1)S(1)}, u32[]{:S(2)}, u32[]{:S(2)}) collective-permute-start(bf16[144,768]{1,0:T(8,128)(2,1)} %pack_first.1.refs_5_), channel_id=1, source_target_pairs={{0,2},{1,3},{2,0},{3,1},{4,6},{5,7},{6,4},{7,5},{8,10},{9,11},{10,... | collective-permute-start | bytes 663560 | tf_op jit(solution)/shard_map/ppermute | solution.py:721
  5.6 7.7 %collective-permute-start = (bf16[144,768]{1,0:T(8,128)(2,1)}, bf16[144,768]{1,0:T(8,128)(2,1)S(1)}, u32[]{:S(2)}, u32[]{:S(2)}) collective-permute-start(bf16[144,768]{1,0:T(8,128)(2,1)} %pack_first.1.refs_5_), channel_id=1, source_target_pairs={{0,1},{1,0},{2,3},{3,2},{4,5},{5,4},{6,7},{7,6},{8,9},{9,8},{10,11... | collective-permute-start | bytes 663560 | tf_op jit(solution)/shard_map/ppermute | solution.py:721
  11.3 8.9 %collective-permute-start.4 = (bf16[128,768]{1,0:T(8,128)(2,1)}, bf16[128,768]{1,0:T(8,128)(2,1)}, u32[]{:S(2)}, u32[]{:S(2)}) collective-permute-start(bf16[128,768]{1,0:T(8,128)(2,1)} %get-tuple-element.123.refs_5_), channel_id=1, source_target_pairs={{0,2},{1,3},{2,0},{3,1},{4,6},{5,7},{6,4},{7,5},{8,10},{9,11},{10,... | collective-permute-start | bytes 589832 | tf_op jit(solution)/shard_map/ppermute | solution.py:721
  13.0 16.3 %collective-permute-start.7 = (bf16[128,1536]{1,0:T(8,128)(2,1)}, bf16[128,1536]{1,0:T(8,128)(2,1)}, u32[]{:S(2)}, u32[]{:S(2)}) collective-permute-start(bf16[128,1536]{1,0:T(8,128)(2,1)} %get-tuple-element.135.refs_6_), channel_id=1, source_target_pairs={{0,2},{1,3},{2,0},{3,1},{4,6},{5,7},{6,4},{7,5},{8,10},{9,11},{10,... | collective-permute-start | bytes 1179656 | tf_op jit(solution)/shard_map/ppermute | solution.py:721
  13.3 7.6 %collective-permute-start.3 = (bf16[128,768]{1,0:T(8,128)(2,1)}, bf16[128,768]{1,0:T(8,128)(2,1)}, u32[]{:S(2)}, u32[]{:S(2)}) collective-permute-start(bf16[128,768]{1,0:T(8,128)(2,1)} %get-tuple-element.123.refs_5_), channel_id=1, source_target_pairs={{0,1},{1,0},{2,3},{3,2},{4,5},{5,4},{6,7},{7,6},{8,9},{9,8},{10,11... | collective-permute-start | bytes 589832 | tf_op jit(solution)/shard_map/ppermute | solution.py:721
  20.8 9.0 %collective-permute-start.6 = (bf16[128,1536]{1,0:T(8,128)(2,1)}, bf16[128,1536]{1,0:T(8,128)(2,1)S(1)}, u32[]{:S(2)}, u32[]{:S(2)}) collective-permute-start(bf16[128,1536]{1,0:T(8,128)(2,1)} %get-tuple-element.135.refs_6_), channel_id=1, source_target_pairs={{0,1},{1,0},{2,3},{3,2},{4,5},{5,4},{6,7},{7,6},{8,9},{9,8},{10,11... | collective-permute-start | bytes 1179656 | tf_op jit(solution)/shard_map/ppermute | solution.py:721
  50.6 14.2 %collective-permute-start.11 = (bf16[128,1920]{1,0:T(8,128)(2,1)S(1)}, bf16[128,1920]{1,0:T(8,128)(2,1)S(1)}, u32[]{:S(2)}, u32[]{:S(2)}) collective-permute-start(bf16[128,1920]{1,0:T(8,128)(2,1)S(1)} %get-tuple-element.192.refs_12_), channel_id=1, source_target_pairs={{0,2},{1,3},{2,0},{3,1},{4,6},{5,7},{6,4},{7,5},{8,10},{9,11},{10,... | collective-permute-start | bytes 1474568 | tf_op jit(solution)/shard_map/ppermute | solution.py:721
  64.9 8.4 %collective-permute-start.12 = (bf16[64,1920]{1,0:T(8,128)(2,1)S(1)}, bf16[64,1920]{1,0:T(8,128)(2,1)S(1)}, u32[]{:S(2)}, u32[]{:S(2)}) collective-permute-start(bf16[64,1920]{1,0:T(8,128)(2,1)S(1)} %get-tuple-element.196.refs_1_), channel_id=1, source_target_pairs={{0,4},{4,0},{8,12},{12,8},{16,20},{20,16},{24,28},{28,24},{1,5},{5... | collective-permute-start | bytes 737288 | tf_op jit(solution)/shard_map/ppermute | solution.py:721
  67.1 9.8 %collective-permute-start.14 = (bf16[128,1280]{1,0:T(8,128)(2,1)S(1)}, bf16[128,1280]{1,0:T(8,128)(2,1)S(1)}, u32[]{:S(2)}, u32[]{:S(2)}) collective-permute-start(bf16[128,1280]{1,0:T(8,128)(2,1)S(1)} %get-tuple-element.194.refs_0_), channel_id=1, source_target_pairs={{0,2},{1,3},{2,0},{3,1},{4,6},{5,7},{6,4},{7,5},{8,10},{9,11},{10,... | collective-permute-start | bytes 983048 | tf_op jit(solution)/shard_map/ppermute | solution.py:721
  73.6 5.0 %collective-permute-start.13 = (bf16[32,1920]{1,0:T(8,128)(2,1)S(1)}, bf16[32,1920]{1,0:T(8,128)(2,1)S(1)}, u32[]{:S(2)}, u32[]{:S(2)}) collective-permute-start(bf16[32,1920]{1,0:T(8,128)(2,1)S(1)} %get-tuple-element.199), channel_id=1, source_target_pairs={{0,8},{4,12},{8,0},{12,4},{16,24},{20,28},{24,16},{28,20},{1,9},{5... | collective-permute-start | bytes 368648 | tf_op jit(solution)/shard_map/ppermute | solution.py:721
  77.0 5.5 %collective-permute-start.16 = (bf16[64,1280]{1,0:T(8,128)(2,1)S(1)}, bf16[64,1280]{1,0:T(8,128)(2,1)S(1)}, u32[]{:S(2)}, u32[]{:S(2)}) collective-permute-start(bf16[64,1280]{1,0:T(8,128)(2,1)S(1)} %get-tuple-element.198), channel_id=1, source_target_pairs={{0,4},{4,0},{8,12},{12,8},{16,20},{20,16},{24,28},{28,24},{1,5},{5... | collective-permute-start | bytes 491528 | tf_op jit(solution)/shard_map/ppermute | solution.py:721
  78.6 5.5 %collective-permute-start.15 = (bf16[16,1920]{1,0:T(8,128)(2,1)S(1)}, bf16[16,1920]{1,0:T(8,128)(2,1)S(1)}, u32[]{:S(2)}, u32[]{:S(2)}) collective-permute-start(bf16[16,1920]{1,0:T(8,128)(2,1)S(1)} %add_convert_fusion.13), channel_id=1, source_target_pairs={{0,16},{4,20},{8,24},{12,28},{16,0},{20,4},{24,8},{28,12},{1,17},{... | collective-permute-start | bytes 184328 | tf_op jit(solution)/shard_map/ppermute | solution.py:721
  82.5 4.9 %collective-permute-start.18 = (bf16[32,1280]{1,0:T(8,128)(2,1)S(1)}, bf16[32,1280]{1,0:T(8,128)(2,1)S(1)}, u32[]{:S(2)}, u32[]{:S(2)}) collective-permute-start(bf16[32,1280]{1,0:T(8,128)(2,1)S(1)} %get-tuple-element.202), channel_id=1, source_target_pairs={{0,8},{4,12},{8,0},{12,4},{16,24},{20,28},{24,16},{28,20},{1,9},{5... | collective-permute-start | bytes 245768 | tf_op jit(solution)/shard_map/ppermute | solution.py:721
  84.2 5.5 %collective-permute-start.17 = (bf16[16,1920]{1,0:T(8,128)(2,1)S(1)}, bf16[16,1920]{1,0:T(8,128)(2,1)S(1)}, u32[]{:S(2)}, u32[]{:S(2)}) collective-permute-start(bf16[16,1920]{1,0:T(8,128)(2,1)S(1)} %add_convert_fusion.12), channel_id=1, source_target_pairs={{0,16},{4,20},{8,24},{12,28},{16,0},{20,4},{24,8},{28,12},{1,17},{... | collective-permute-start | bytes 184328 | tf_op jit(solution)/shard_map/ppermute | solution.py:721
  87.4 5.2 %collective-permute-start.20 = (bf16[16,1280]{1,0:T(8,128)(2,1)S(1)}, bf16[16,1280]{1,0:T(8,128)(2,1)S(1)}, u32[]{:S(2)}, u32[]{:S(2)}) collective-permute-start(bf16[16,1280]{1,0:T(8,128)(2,1)S(1)} %get-tuple-element.204), channel_id=1, source_target_pairs={{0,16},{4,20},{8,24},{12,28},{16,0},{20,4},{24,8},{28,12},{1,17},{... | collective-permute-start | bytes 122888 | tf_op jit(solution)/shard_map/ppermute | solution.py:721
  89.7 5.1 %collective-permute-start.19 = (bf16[32,1920]{1,0:T(8,128)(2,1)S(1)}, bf16[32,1920]{1,0:T(8,128)(2,1)S(1)}, u32[]{:S(2)}, u32[]{:S(2)}) collective-permute-start(bf16[32,1920]{1,0:T(8,128)(2,1)S(1)} %pad_maximum_fusion.2), channel_id=1, source_target_pairs={{0,8},{4,12},{8,0},{12,4},{16,24},{20,28},{24,16},{28,20},{1,9},{5... | collective-permute-start | bytes 368648 | tf_op jit(solution)/shard_map/ppermute | solution.py:721
  92.6 4.9 %collective-permute-start.21 = (bf16[16,1152]{1,0:T(8,128)(2,1)S(1)}, bf16[16,1152]{1,0:T(8,128)(2,1)S(1)}, u32[]{:S(2)}, u32[]{:S(2)}) collective-permute-start(bf16[16,1152]{1,0:T(8,128)(2,1)S(1)} %add_convert_fusion.17), channel_id=1, source_target_pairs={{0,16},{4,20},{8,24},{12,28},{16,0},{20,4},{24,8},{28,12},{1,17},{... | collective-permute-start | bytes 110600 | tf_op jit(solution)/shard_map/ppermute | solution.py:721
  97.5 4.4 %collective-permute-start.22 = (bf16[32,1152]{1,0:T(8,128)(2,1)S(1)}, bf16[32,1152]{1,0:T(8,128)(2,1)S(1)}, u32[]{:S(2)}, u32[]{:S(2)}) collective-permute-start(bf16[32,1152]{1,0:T(8,128)(2,1)S(1)} %pad_maximum_fusion.3), channel_id=1, source_target_pairs={{0,8},{4,12},{8,0},{12,4},{16,24},{20,28},{24,16},{28,20},{1,9},{5... | collective-permute-start | bytes 221192 | tf_op jit(solution)/shard_map/ppermute | solution.py:721
  99.4 11.0 %collective-permute-start.27 = (bf16[64,1920]{1,0:T(8,128)(2,1)S(1)}, bf16[64,1920]{1,0:T(8,128)(2,1)S(1)}, u32[]{:S(2)}, u32[]{:S(2)}) collective-permute-start(bf16[64,1920]{1,0:T(8,128)(2,1)S(1)} %pad_maximum_fusion.early.refs_0_), channel_id=1, source_target_pairs={{0,4},{4,0},{8,12},{12,8},{16,20},{20,16},{24,28},{28,24},{1,5},{5... | collective-permute-start | bytes 737288 | tf_op jit(solution)/shard_map/ppermute | solution.py:721
  102.7 3.4 %collective-permute-start.25 = (f32[8,128]{1,0:T(8,128)S(1)}, f32[8,128]{1,0:T(8,128)S(1)}, u32[]{:S(2)}, u32[]{:S(2)}) collective-permute-start(f32[8,128]{1,0:T(8,128)S(1)} %half_squares.1), channel_id=1, source_target_pairs={{0,3},{1,2},{2,1},{3,0},{4,7},{5,6},{6,5},{7,4},{8,11},{9,10},{10,... | collective-permute-start | bytes 12296 | tf_op jit(solution)/shard_map/ppermute | solution.py:721
  102.7 3.7 %collective-permute-start.24 = (f32[8,128]{1,0:T(8,128)S(1)}, f32[8,128]{1,0:T(8,128)S(1)}, u32[]{:S(2)}, u32[]{:S(2)}) collective-permute-start(f32[8,128]{1,0:T(8,128)S(1)} %half_squares.1), channel_id=1, source_target_pairs={{0,2},{1,3},{2,0},{3,1},{4,6},{5,7},{6,4},{7,5},{8,10},{9,11},{10,... | collective-permute-start | bytes 12296 | tf_op jit(solution)/shard_map/ppermute | solution.py:721
  103.3 3.1 %collective-permute-start.23 = (f32[8,128]{1,0:T(8,128)S(1)}, f32[8,128]{1,0:T(8,128)S(1)}, u32[]{:S(2)}, u32[]{:S(2)}) collective-permute-start(f32[8,128]{1,0:T(8,128)S(1)} %half_squares.1), channel_id=1, source_target_pairs={{0,1},{1,0},{2,3},{3,2},{4,5},{5,4},{6,7},{7,6},{8,9},{9,8},{10,11... | collective-permute-start | bytes 12296 | tf_op jit(solution)/shard_map/ppermute | solution.py:721
  104.6 5.9 %collective-permute-start.28 = (bf16[64,1152]{1,0:T(8,128)(2,1)S(1)}, bf16[64,1152]{1,0:T(8,128)(2,1)S(1)}, u32[]{:S(2)}, u32[]{:S(2)}) collective-permute-start(bf16[64,1152]{1,0:T(8,128)(2,1)S(1)} %pad_maximum_fusion.1.late.refs_2_), channel_id=1, source_target_pairs={{0,4},{4,0},{8,12},{12,8},{16,20},{20,16},{24,28},{28,24},{1,5},{5... | collective-permute-start | bytes 442376 | tf_op jit(solution)/shard_map/ppermute | solution.py:721
  106.4 4.0 %collective-permute-start.26 = (f32[8,128]{1,0:T(8,128)S(1)}, f32[8,128]{1,0:T(8,128)S(1)}, u32[]{:S(2)}, u32[]{:S(2)}) collective-permute-start(f32[8,128]{1,0:T(8,128)S(1)} %add_add_fusion), channel_id=1, source_target_pairs={{0,4},{4,0},{8,12},{12,8},{16,20},{20,16},{24,28},{28,24},{1,5},{5... | collective-permute-start | bytes 12296 | tf_op jit(solution)/shard_map/ppermute | solution.py:721
  (25 other events, 471.5 us)

commit v6 on v5

--- a/solution.py
+++ b/solution.py
@@ -655,44 +655,46 @@
     norm = jnp.sqrt(square_ref[0:1, 0:1])
     factor = limit / jnp.maximum(norm, limit)
 
-    def write(number, where, grad, rate, decay):
+    def write(number, where, target, grad, rate, decay):
         new, first, second = adam(
             states[number][where], grad * factor, states[5 + number][where],
             states[10 + number][where], rate, decay,
         )
-        outs[number][where] = new
-        outs[5 + number][where] = first
-        outs[10 + number][where] = second
-        outs[15 + number][where] = new.astype(BF)
-
-    height = states[0].shape[0]
+        outs[number][target] = new
+        outs[5 + number][target] = first
+        outs[10 + number][target] = second
+        outs[15 + number][target] = new.astype(BF)
+
+    height = outs[0].shape[0]
     pieces = height // 16 if quick else 1
     rows = height // pieces
     for piece in range(pieces):
+        here = pl.multiple_of(step * height + piece * rows, rows)
         if quick:
             mask = jnp.bitwise_xor(place[1], step * pieces + piece)
             at = pl.multiple_of(((mask >> 2) & 1) * 16 + ((mask >> 1) & 1) * 32, 16)
             odd = (mask & 1) == 1
         else:
-            at = pl.multiple_of(step * rows, rows)
+            at = here
         for group, parts in enumerate((EARLY_PARTS, LATE_PARTS)):
-            for cols, number, target in parts:
+            for cols, number, first in parts:
                 if quick:
                     low, high = grads[2 * group], grads[2 * group + 1]
                     grad = jnp.where(odd, high[pl.ds(at, rows), cols], low[pl.ds(at, rows), cols])
                 else:
                     grad = grads[group][pl.ds(at, rows), cols]
-                where = (
-                    slice(piece * rows, (piece + 1) * rows),
-                    slice(target, target + cols.stop - cols.start),
+                there = slice(first, first + cols.stop - cols.start)
+                write(
+                    number, (pl.ds(here, rows), there), (slice(piece * rows, (piece + 1) * rows), there),
+                    grad.astype(F32), 0.1, 0.01,
                 )
-                write(number, where, grad.astype(F32), 0.1, 0.01)
 
     @pl.when(step == 0)
     def _():
         norm_out[0, 0] = norm[0, 0]
         vec_cols = states[4].shape[1]
-        write(4, (slice(0, 9), slice(0, vec_cols)), vec_ref[0:9, :vec_cols].astype(F32), 0.5, 0.0)
+        where = (slice(0, 9), slice(0, vec_cols))
+        write(4, where, where, vec_ref[0:9, :vec_cols].astype(F32), 0.5, 0.0)
 
 
 def adam_step(place, squares, limit, grads, vec_grad, weights, firsts, seconds, quick):
@@ -708,7 +710,7 @@
     return pl.pallas_call(
         functools.partial(adam_kernel, quick, limit),
         grid=(steps,),
-        in_specs=[SMEM] + [VM] * (2 + len(grads)) + state * 3,
+        in_specs=[SMEM] + [VM] * (17 + len(grads)),
         out_specs=state * 4 + [SMEM],
         out_shape=shapes * 3 + [sds(w.shape, BF) for w in weights] + [sds((1, 1), F32)],
         compiler_params=params(),
@@ -826,10 +828,13 @@
     *saved_b, w_b, vec_full, tokens = forward_attention(
         GROUP, place, tokens, tokens_t, cells, vec_full, pieces_b, order
     )
-    cotangent = turn_cotangent(start, cotangent, [saved_b[0]])
     if quick:
-        y_rest, c_rest = after(y_rest, (saved_b, cotangent)), after(c_rest, saved_b)
-        pieces_rest = [low_rest, c_rest, y_rest, swap(y_rest, "narrow", 1)]
+        y_rest, c_rest = after(y_rest, saved_b), after(c_rest, saved_b)
+        d_rest = swap(y_rest, "narrow", 1)
+        cotangent = turn_cotangent(start, cotangent, [y_rest])
+        pieces_rest = [low_rest, c_rest, y_rest, after(d_rest, cotangent)]
+    else:
+        cotangent = turn_cotangent(start, cotangent, [])
     mixed, d_h1, d_t, vec_sums, *inner = middle(
         place, tokens, cotangent, (saved_a[0], saved_b[0]), vec_full, pieces_rest, order
     )

time: 115 us -> 115 us (level)
  transfers between devices with their start and end apart: 29 -> 29, of which waited for: 13 -> 13; matrix products, arithmetic and copies ran while one was open for 1% -> 1% of each run, Pallas kernels for 30% -> 31%
where the time goes in v6:
time: 115 us; the launch traced here: 114 us
  Pallas kernels  57.9 us (50%)
  starting transfers between devices  35.5 us (31%)
  waiting for transfers between devices  14.3 us (12%)
  local copies, waits for them, and re-layouts  3.5 us (3%)
  other arithmetic  1.69 us (1%)
  between operations  1.27 us (1%)
    ppermute x29, starting transfers between devices, swap(): return lax.ppermute(value, axis, [(i, i ^ mask) for i in range(size)])  35.5 us
    pallas_call x2, Pallas kernels, backward_attention(): pl.pallas_call(functools.partial(backward_kernel, n_shards, stages, plan,...  18.8 us
    ppermute x29, waiting for transfers between devices, swap(): return lax.ppermute(value, axis, [(i, i ^ mask) for i in range(size)])  14.3 us
    pallas_call x2, Pallas kernels, forward_attention(): pl.pallas_call(functools.partial(forward_kernel, order, len(pieces), base...  12.2 us
    pallas_call x1, Pallas kernels, middle(): pl.pallas_call(functools.partial(middle_kernel, order, len(pieces)), grid...  9.9 us
    pallas_call x1, Pallas kernels, input_gradient(): pl.pallas_call(input_grad_kernel, in_specs=[SMEM] + [VM] * 5 + [ANY] * le...  4.66 us
    pallas_call x1, Pallas kernels, adam_step(): pl.pallas_call(functools.partial(adam_kernel, quick, limit), grid=(steps,...  4.19 us
    unnamed x40, local copies, waits for them, and re-layouts  3.5 us
  transfers between devices with their start and end apart: 29, of which 13 were waited for; matrix products, arithmetic and copies ran while one was open for 1% of the time, Pallas kernels for 31%

profile of v6, /device:TPU:0, one launch (start us, length us, event | category | flops | bytes accessed | tf_op | source)
XLA Modules:
  0.0 114.2 jit_solution(10586063376326245949)
XLA Ops:
  0.7 1.9 %pack_first.1.refs_5_ = bf16[144,768]{1,0:T(8,128)(2,1)} custom-call(f32[128,1536]{1,0:T(8,128)} %refs_5_.1, f32[9,128]{1,0:T(8,128)} %refs_9_.1), custom_call_target="tpu_custom_call" | custom-call | tf_op jit(solution)/shard_map/pack_first/pallas_call | solution.py:104
  2.6 3.0 %collective-permute-start.1 = (bf16[144,768]{1,0:T(8,128)(2,1)}, bf16[144,768]{1,0:T(8,128)(2,1)S(1)}, u32[]{:S(2)}, u32[]{:S(2)}) collective-permute-start(bf16[144,768]{1,0:T(8,128)(2,1)} %pack_first.1.refs_5_), channel_id=1, source_target_pairs={{0,2},{1,3},{2,0},{3,1},{4,6},{5,7},{6,4},{7,5},{8,10},{9,11},{10,... | collective-permute-start | bytes 663560 | tf_op jit(solution)/shard_map/ppermute | solution.py:723
  11.3 1.7 %collective-permute-start.4 = (bf16[128,768]{1,0:T(8,128)(2,1)}, bf16[128,768]{1,0:T(8,128)(2,1)}, u32[]{:S(2)}, u32[]{:S(2)}) collective-permute-start(bf16[128,768]{1,0:T(8,128)(2,1)} %get-tuple-element.124.refs_5_), channel_id=1, source_target_pairs={{0,2},{1,3},{2,0},{3,1},{4,6},{5,7},{6,4},{7,5},{8,10},{9,11},{10,... | collective-permute-start | bytes 589832 | tf_op jit(solution)/shard_map/ppermute | solution.py:723
  14.6 6.1 %forward_attention.2 = (bf16[256,1024]{1,0:T(8,128)(2,1)S(1)}, f32[2,8,1024]{2,1,0:T(8,128)S(1)}, bf16[2,1024,128]{2,1,0:T(8,128)(2,1)S(1)}, bf16[2,1024,128]{2,...) custom-call(s32[2]{0:T(128)S(1)} %pad_add_fusion.refs_0_.place, ...), custom_call_target="tpu_custom_call" | custom-call | flops 1 | bytes 1 | tf_op jit(solution)/shard_map/forward_attention/pallas_call | solution.py:337
  22.6 6.2 %forward_attention.3 = (bf16[256,1024]{1,0:T(8,128)(2,1)S(1)}, f32[2,8,1024]{2,1,0:T(8,128)S(1)}, bf16[2,1024,128]{2,1,0:T(8,128)(2,1)S(1)}, bf16[2,1024,128]{2,...) custom-call(s32[2]{0:T(128)S(1)} %pad_add_fusion.refs_0_.place, ...), custom_call_target="tpu_custom_call" | custom-call | flops 1 | bytes 1 | tf_op jit(solution)/shard_map/forward_attention/pallas_call | solution.py:337
  30.6 9.9 %middle.1 = (bf16[1024,512]{1,0:T(8,128)(2,1)S(1)}, f32[1024,512]{1,0:T(8,128)S(1)}, bf16[512,1024]{1,0:T(8,128)(2,1)S(1)}, f32[16,512]{1,0:T(8,128)S(1)}, bf16[...) custom-call(s32[2]{0:T(128)S(1)} %pad_add_fusion.refs_0_.place, ...), custom_call_target="tpu_custom_call" | custom-call | flops 10000000000 | bytes 12000000 | tf_op jit(solution)/shard_map/middle/pallas_call | solution.py:481
  40.5 6.3 %backward_attention.2 = (bf16[1,384,1024]{2,1,0:T(8,128)(2,1)S(1)}, f32[16,512]{1,0:T(8,128)S(1)}, bf16[256,1920]{1,0:T(8,128)(2,1)S(1)}, bf16[256,1920]{1,0:T(8,128)(2,1)S(1)}) custom-call(s32[2]{0:T(128)S(1)} %pad_add_fusion.refs_0_.place, s32[8,1024]{1,0:T(8,128)S(1)} %get-tuple-element.112.refs_0_.refs_3_.cells_ref, ...), custom_call_target="tpu_custom_call" | custom-call | flops 5000000000 | bytes 8000000 | tf_op jit(solution)/shard_map/backward_attention/pallas_call | solution.py:588
  47.1 2.3 %turn_back.1 = bf16[1024,512]{1,0:T(8,128)(2,1)} custom-call(s32[1]{0:T(128)} %get-tuple-element.109.start, bf16[1024,512]{1,0:T(8,128)(2,1)S(1)} %get-tuple-element.139.source, bf16[1,384,1024]{2,1,0:T(8,128)(2,1)S(1)} %get-tuple-element.147.refs_0_.trio_a), custom_call_target="tpu_custom_call" | custom-call | flops 1 | bytes 1 | tf_op jit(solution)/shard_map/turn_back/pallas_call | solution.py:230
  49.7 1.8 %collective-permute-start.11 = (bf16[128,1920]{1,0:T(8,128)(2,1)S(1)}, bf16[128,1920]{1,0:T(8,128)(2,1)S(1)}, u32[]{:S(2)}, u32[]{:S(2)}) collective-permute-start(bf16[128,1920]{1,0:T(8,128)(2,1)S(1)} %get-tuple-element.194.refs_12_), channel_id=1, source_target_pairs={{0,2},{1,3},{2,0},{3,1},{4,6},{5,7},{6,4},{7,5},{8,10},{9,11},{10,... | collective-permute-start | bytes 1474568 | tf_op jit(solution)/shard_map/ppermute | solution.py:723
  51.6 12.5 %backward_attention.3 = (bf16[3,384,1024]{2,1,0:T(8,128)(2,1)S(1)}, f32[16,512]{1,0:T(8,128)}, bf16[256,1280]{1,0:T(8,128)(2,1)S(1)}, bf16[256,1280]{1,0:T(8,128)(2,1)S(1)}) custom-call(s32[2]{0:T(128)S(1)} %pad_add_fusion.refs_0_.place, s32[8,1024]{1,0:T(8,128)S(1)} %get-tuple-element.112.refs_0_.refs_3_.cells_ref, ...), custom_call_target="tpu_custom_call" | custom-call | flops 15000000512 | bytes 8000000 | tf_op jit(solution)/shard_map/backward_attention/pallas_call | solution.py:588
  66.8 4.7 %input_gradient.1 = f32[1024,512]{1,0:T(8,128)} custom-call(s32[1]{0:T(128)} %get-tuple-element.109.start, bf16[512,768]{1,0:T(8,128)(2,1)S(1)} %get-tuple-element.148.w_a, bf16[512,768]{1,0:T(8,128)(2,1)S(1)} %get-tuple-element.149.w_b, f32[1024,512]{1,0:T(8,128)S(1)} %get-tuple-element.150.dh1_ref, ...), custom_call_target="tpu_custom_call" | custom-call | flops 1 | bytes 1 | tf_op jit(solution)/shard_map/input_gradient/pallas_call | solution.py:614
  72.8 1.6 %collective-permute-start.13 = (bf16[32,1920]{1,0:T(8,128)(2,1)S(1)}, bf16[32,1920]{1,0:T(8,128)(2,1)S(1)}, u32[]{:S(2)}, u32[]{:S(2)}) collective-permute-start(bf16[32,1920]{1,0:T(8,128)(2,1)S(1)} %get-tuple-element.201), channel_id=1, source_target_pairs={{0,8},{4,12},{8,0},{12,4},{16,24},{20,28},{24,16},{28,20},{1,9},{5... | collective-permute-start | bytes 368648 | tf_op jit(solution)/shard_map/ppermute | solution.py:723
  74.4 1.7 %collective-permute-done.14 = bf16[128,1280]{1,0:T(8,128)(2,1)S(1)} collective-permute-done((bf16[128,1280]{1,0:T(8,128)(2,1)S(1)}, bf16[128,1280]{1,0:T(8,128)(2,1)S(1)}, u32[]{:S(2)}, u32[]{:S(2)}) %collective-permute-start.14) | collective-permute-done | bytes 327712 | tf_op jit(solution)/shard_map/ppermute | solution.py:723
  77.8 2.7 %collective-permute-start.15 = (bf16[16,1920]{1,0:T(8,128)(2,1)S(1)}, bf16[16,1920]{1,0:T(8,128)(2,1)S(1)}, u32[]{:S(2)}, u32[]{:S(2)}) collective-permute-start(bf16[16,1920]{1,0:T(8,128)(2,1)S(1)} %add_convert_fusion.13), channel_id=1, source_target_pairs={{0,16},{4,20},{8,24},{12,28},{16,0},{20,4},{24,8},{28,12},{1,17},{... | collective-permute-start | bytes 184328 | tf_op jit(solution)/shard_map/ppermute | solution.py:723
  81.7 1.6 %collective-permute-start.18 = (bf16[32,1280]{1,0:T(8,128)(2,1)S(1)}, bf16[32,1280]{1,0:T(8,128)(2,1)S(1)}, u32[]{:S(2)}, u32[]{:S(2)}) collective-permute-start(bf16[32,1280]{1,0:T(8,128)(2,1)S(1)} %get-tuple-element.204), channel_id=1, source_target_pairs={{0,8},{4,12},{8,0},{12,4},{16,24},{20,28},{24,16},{28,20},{1,9},{5... | collective-permute-start | bytes 245768 | tf_op jit(solution)/shard_map/ppermute | solution.py:723
  83.4 2.6 %collective-permute-start.17 = (bf16[16,1920]{1,0:T(8,128)(2,1)S(1)}, bf16[16,1920]{1,0:T(8,128)(2,1)S(1)}, u32[]{:S(2)}, u32[]{:S(2)}) collective-permute-start(bf16[16,1920]{1,0:T(8,128)(2,1)S(1)} %add_convert_fusion.12), channel_id=1, source_target_pairs={{0,16},{4,20},{8,24},{12,28},{16,0},{20,4},{24,8},{28,12},{1,17},{... | collective-permute-start | bytes 184328 | tf_op jit(solution)/shard_map/ppermute | solution.py:723
  86.6 2.3 %collective-permute-start.20 = (bf16[16,1280]{1,0:T(8,128)(2,1)S(1)}, bf16[16,1280]{1,0:T(8,128)(2,1)S(1)}, u32[]{:S(2)}, u32[]{:S(2)}) collective-permute-start(bf16[16,1280]{1,0:T(8,128)(2,1)S(1)} %get-tuple-element.206), channel_id=1, source_target_pairs={{0,16},{4,20},{8,24},{12,28},{16,0},{20,4},{24,8},{28,12},{1,17},{... | collective-permute-start | bytes 122888 | tf_op jit(solution)/shard_map/ppermute | solution.py:723
  89.0 2.2 %collective-permute-start.19 = (bf16[32,1920]{1,0:T(8,128)(2,1)S(1)}, bf16[32,1920]{1,0:T(8,128)(2,1)S(1)}, u32[]{:S(2)}, u32[]{:S(2)}) collective-permute-start(bf16[32,1920]{1,0:T(8,128)(2,1)S(1)} %pad_maximum_fusion.2), channel_id=1, source_target_pairs={{0,8},{4,12},{8,0},{12,4},{16,24},{20,28},{24,16},{28,20},{1,9},{5... | collective-permute-start | bytes 368648 | tf_op jit(solution)/shard_map/ppermute | solution.py:723
  91.9 2.2 %collective-permute-start.21 = (bf16[16,1152]{1,0:T(8,128)(2,1)S(1)}, bf16[16,1152]{1,0:T(8,128)(2,1)S(1)}, u32[]{:S(2)}, u32[]{:S(2)}) collective-permute-start(bf16[16,1152]{1,0:T(8,128)(2,1)S(1)} %add_convert_fusion.17), channel_id=1, source_target_pairs={{0,16},{4,20},{8,24},{12,28},{16,0},{20,4},{24,8},{28,12},{1,17},{... | collective-permute-start | bytes 110600 | tf_op jit(solution)/shard_map/ppermute | solution.py:723
  94.1 2.7 %collective-permute-done.21 = bf16[16,1152]{1,0:T(8,128)(2,1)S(1)} collective-permute-done((bf16[16,1152]{1,0:T(8,128)(2,1)S(1)}, bf16[16,1152]{1,0:T(8,128)(2,1)S(1)}, u32[]{:S(2)}, u32[]{:S(2)}) %collective-permute-start.21) | collective-permute-done | bytes 36896 | tf_op jit(solution)/shard_map/ppermute | solution.py:723
  96.8 1.8 %collective-permute-start.22 = (bf16[32,1152]{1,0:T(8,128)(2,1)S(1)}, bf16[32,1152]{1,0:T(8,128)(2,1)S(1)}, u32[]{:S(2)}, u32[]{:S(2)}) collective-permute-start(bf16[32,1152]{1,0:T(8,128)(2,1)S(1)} %pad_maximum_fusion.3), channel_id=1, source_target_pairs={{0,8},{4,12},{8,0},{12,4},{16,24},{20,28},{24,16},{28,20},{1,9},{5... | collective-permute-start | bytes 221192 | tf_op jit(solution)/shard_map/ppermute | solution.py:723
  105.7 1.6 %collective-permute-start.26 = (f32[8,128]{1,0:T(8,128)S(1)}, f32[8,128]{1,0:T(8,128)S(1)}, u32[]{:S(2)}, u32[]{:S(2)}) collective-permute-start(f32[8,128]{1,0:T(8,128)S(1)} %add_add_fusion), channel_id=1, source_target_pairs={{0,4},{4,0},{8,12},{12,8},{16,20},{20,16},{24,28},{28,24},{1,5},{5... | collective-permute-start | bytes 12296 | tf_op jit(solution)/shard_map/ppermute | solution.py:723
  107.2 2.4 %collective-permute-done.26 = f32[8,128]{1,0:T(8,128)S(1)} collective-permute-done((f32[8,128]{1,0:T(8,128)S(1)}, f32[8,128]{1,0:T(8,128)S(1)}, u32[]{:S(2)}, u32[]{:S(2)}) %collective-permute-start.26) | collective-permute-done | bytes 4128 | tf_op jit(solution)/shard_map/ppermute | solution.py:723
  109.8 4.2 %adam.1 = (f32[128,1536]{1,0:T(8,128)}, f32[128,512]{1,0:T(8,128)}, f32[128,512]{1,0:T(8,128)}, f32[128,512]{1,0:T(8,128)}, f32[9,128]{1,0:T(8,128)}, /*index=5*...) custom-call(s32[2]{0:T(128)S(1)} %pad_add_fusion.refs_0_.place, ...), custom_call_target="tpu_custom_call" | custom-call | tf_op jit(solution)/shard_map/adam/pallas_call | solution.py:710
  (107 shorter events, 26.8 us)
Async XLA Ops:
  2.6 8.7 %collective-permute-start.1 = (bf16[144,768]{1,0:T(8,128)(2,1)}, bf16[144,768]{1,0:T(8,128)(2,1)S(1)}, u32[]{:S(2)}, u32[]{:S(2)}) collective-permute-start(bf16[144,768]{1,0:T(8,128)(2,1)} %pack_first.1.refs_5_), channel_id=1, source_target_pairs={{0,2},{1,3},{2,0},{3,1},{4,6},{5,7},{6,4},{7,5},{8,10},{9,11},{10,... | collective-permute-start | bytes 663560 | tf_op jit(solution)/shard_map/ppermute | solution.py:723
  5.6 7.7 %collective-permute-start = (bf16[144,768]{1,0:T(8,128)(2,1)}, bf16[144,768]{1,0:T(8,128)(2,1)}, u32[]{:S(2)}, u32[]{:S(2)}) collective-permute-start(bf16[144,768]{1,0:T(8,128)(2,1)} %pack_first.1.refs_5_), channel_id=1, source_target_pairs={{0,1},{1,0},{2,3},{3,2},{4,5},{5,4},{6,7},{7,6},{8,9},{9,8},{10,11... | collective-permute-start | bytes 663560 | tf_op jit(solution)/shard_map/ppermute | solution.py:723
  11.3 9.5 %collective-permute-start.4 = (bf16[128,768]{1,0:T(8,128)(2,1)}, bf16[128,768]{1,0:T(8,128)(2,1)}, u32[]{:S(2)}, u32[]{:S(2)}) collective-permute-start(bf16[128,768]{1,0:T(8,128)(2,1)} %get-tuple-element.124.refs_5_), channel_id=1, source_target_pairs={{0,2},{1,3},{2,0},{3,1},{4,6},{5,7},{6,4},{7,5},{8,10},{9,11},{10,... | collective-permute-start | bytes 589832 | tf_op jit(solution)/shard_map/ppermute | solution.py:723
  13.0 15.8 %collective-permute-start.6 = (bf16[128,1536]{1,0:T(8,128)(2,1)}, bf16[128,1536]{1,0:T(8,128)(2,1)S(1)}, u32[]{:S(2)}, u32[]{:S(2)}) collective-permute-start(bf16[128,1536]{1,0:T(8,128)(2,1)} %get-tuple-element.128.refs_6_), channel_id=1, source_target_pairs={{0,2},{1,3},{2,0},{3,1},{4,6},{5,7},{6,4},{7,5},{8,10},{9,11},{10,... | collective-permute-start | bytes 1179656 | tf_op jit(solution)/shard_map/ppermute | solution.py:723
  13.3 8.1 %collective-permute-start.3 = (bf16[128,768]{1,0:T(8,128)(2,1)}, bf16[128,768]{1,0:T(8,128)(2,1)}, u32[]{:S(2)}, u32[]{:S(2)}) collective-permute-start(bf16[128,768]{1,0:T(8,128)(2,1)} %get-tuple-element.124.refs_5_), channel_id=1, source_target_pairs={{0,1},{1,0},{2,3},{3,2},{4,5},{5,4},{6,7},{7,6},{8,9},{9,8},{10,11... | collective-permute-start | bytes 589832 | tf_op jit(solution)/shard_map/ppermute | solution.py:723
  21.3 7.9 %collective-permute-start.7 = (bf16[128,1536]{1,0:T(8,128)(2,1)}, bf16[128,1536]{1,0:T(8,128)(2,1)S(1)}, u32[]{:S(2)}, u32[]{:S(2)}) collective-permute-start(bf16[128,1536]{1,0:T(8,128)(2,1)} %get-tuple-element.128.refs_6_), channel_id=1, source_target_pairs={{0,1},{1,0},{2,3},{3,2},{4,5},{5,4},{6,7},{7,6},{8,9},{9,8},{10,11... | collective-permute-start | bytes 1179656 | tf_op jit(solution)/shard_map/ppermute | solution.py:723
  49.7 14.3 %collective-permute-start.11 = (bf16[128,1920]{1,0:T(8,128)(2,1)S(1)}, bf16[128,1920]{1,0:T(8,128)(2,1)S(1)}, u32[]{:S(2)}, u32[]{:S(2)}) collective-permute-start(bf16[128,1920]{1,0:T(8,128)(2,1)S(1)} %get-tuple-element.194.refs_12_), channel_id=1, source_target_pairs={{0,2},{1,3},{2,0},{3,1},{4,6},{5,7},{6,4},{7,5},{8,10},{9,11},{10,... | collective-permute-start | bytes 1474568 | tf_op jit(solution)/shard_map/ppermute | solution.py:723
  64.2 8.4 %collective-permute-start.12 = (bf16[64,1920]{1,0:T(8,128)(2,1)S(1)}, bf16[64,1920]{1,0:T(8,128)(2,1)S(1)}, u32[]{:S(2)}, u32[]{:S(2)}) collective-permute-start(bf16[64,1920]{1,0:T(8,128)(2,1)S(1)} %get-tuple-element.198.refs_1_), channel_id=1, source_target_pairs={{0,4},{4,0},{8,12},{12,8},{16,20},{20,16},{24,28},{28,24},{1,5},{5... | collective-permute-start | bytes 737288 | tf_op jit(solution)/shard_map/ppermute | solution.py:723
  66.3 9.8 %collective-permute-start.14 = (bf16[128,1280]{1,0:T(8,128)(2,1)S(1)}, bf16[128,1280]{1,0:T(8,128)(2,1)S(1)}, u32[]{:S(2)}, u32[]{:S(2)}) collective-permute-start(bf16[128,1280]{1,0:T(8,128)(2,1)S(1)} %get-tuple-element.196.refs_0_), channel_id=1, source_target_pairs={{0,2},{1,3},{2,0},{3,1},{4,6},{5,7},{6,4},{7,5},{8,10},{9,11},{10,... | collective-permute-start | bytes 983048 | tf_op jit(solution)/shard_map/ppermute | solution.py:723
  72.8 5.0 %collective-permute-start.13 = (bf16[32,1920]{1,0:T(8,128)(2,1)S(1)}, bf16[32,1920]{1,0:T(8,128)(2,1)S(1)}, u32[]{:S(2)}, u32[]{:S(2)}) collective-permute-start(bf16[32,1920]{1,0:T(8,128)(2,1)S(1)} %get-tuple-element.201), channel_id=1, source_target_pairs={{0,8},{4,12},{8,0},{12,4},{16,24},{20,28},{24,16},{28,20},{1,9},{5... | collective-permute-start | bytes 368648 | tf_op jit(solution)/shard_map/ppermute | solution.py:723
  76.2 5.5 %collective-permute-start.16 = (bf16[64,1280]{1,0:T(8,128)(2,1)S(1)}, bf16[64,1280]{1,0:T(8,128)(2,1)S(1)}, u32[]{:S(2)}, u32[]{:S(2)}) collective-permute-start(bf16[64,1280]{1,0:T(8,128)(2,1)S(1)} %get-tuple-element.200), channel_id=1, source_target_pairs={{0,4},{4,0},{8,12},{12,8},{16,20},{20,16},{24,28},{28,24},{1,5},{5... | collective-permute-start | bytes 491528 | tf_op jit(solution)/shard_map/ppermute | solution.py:723
  77.8 5.6 %collective-permute-start.15 = (bf16[16,1920]{1,0:T(8,128)(2,1)S(1)}, bf16[16,1920]{1,0:T(8,128)(2,1)S(1)}, u32[]{:S(2)}, u32[]{:S(2)}) collective-permute-start(bf16[16,1920]{1,0:T(8,128)(2,1)S(1)} %add_convert_fusion.13), channel_id=1, source_target_pairs={{0,16},{4,20},{8,24},{12,28},{16,0},{20,4},{24,8},{28,12},{1,17},{... | collective-permute-start | bytes 184328 | tf_op jit(solution)/shard_map/ppermute | solution.py:723
  81.7 4.9 %collective-permute-start.18 = (bf16[32,1280]{1,0:T(8,128)(2,1)S(1)}, bf16[32,1280]{1,0:T(8,128)(2,1)S(1)}, u32[]{:S(2)}, u32[]{:S(2)}) collective-permute-start(bf16[32,1280]{1,0:T(8,128)(2,1)S(1)} %get-tuple-element.204), channel_id=1, source_target_pairs={{0,8},{4,12},{8,0},{12,4},{16,24},{20,28},{24,16},{28,20},{1,9},{5... | collective-permute-start | bytes 245768 | tf_op jit(solution)/shard_map/ppermute | solution.py:723
  83.4 5.5 %collective-permute-start.17 = (bf16[16,1920]{1,0:T(8,128)(2,1)S(1)}, bf16[16,1920]{1,0:T(8,128)(2,1)S(1)}, u32[]{:S(2)}, u32[]{:S(2)}) collective-permute-start(bf16[16,1920]{1,0:T(8,128)(2,1)S(1)} %add_convert_fusion.12), channel_id=1, source_target_pairs={{0,16},{4,20},{8,24},{12,28},{16,0},{20,4},{24,8},{28,12},{1,17},{... | collective-permute-start | bytes 184328 | tf_op jit(solution)/shard_map/ppermute | solution.py:723
  86.6 5.2 %collective-permute-start.20 = (bf16[16,1280]{1,0:T(8,128)(2,1)S(1)}, bf16[16,1280]{1,0:T(8,128)(2,1)S(1)}, u32[]{:S(2)}, u32[]{:S(2)}) collective-permute-start(bf16[16,1280]{1,0:T(8,128)(2,1)S(1)} %get-tuple-element.206), channel_id=1, source_target_pairs={{0,16},{4,20},{8,24},{12,28},{16,0},{20,4},{24,8},{28,12},{1,17},{... | collective-permute-start | bytes 122888 | tf_op jit(solution)/shard_map/ppermute | solution.py:723
  89.0 5.1 %collective-permute-start.19 = (bf16[32,1920]{1,0:T(8,128)(2,1)S(1)}, bf16[32,1920]{1,0:T(8,128)(2,1)S(1)}, u32[]{:S(2)}, u32[]{:S(2)}) collective-permute-start(bf16[32,1920]{1,0:T(8,128)(2,1)S(1)} %pad_maximum_fusion.2), channel_id=1, source_target_pairs={{0,8},{4,12},{8,0},{12,4},{16,24},{20,28},{24,16},{28,20},{1,9},{5... | collective-permute-start | bytes 368648 | tf_op jit(solution)/shard_map/ppermute | solution.py:723
  91.9 4.9 %collective-permute-start.21 = (bf16[16,1152]{1,0:T(8,128)(2,1)S(1)}, bf16[16,1152]{1,0:T(8,128)(2,1)S(1)}, u32[]{:S(2)}, u32[]{:S(2)}) collective-permute-start(bf16[16,1152]{1,0:T(8,128)(2,1)S(1)} %add_convert_fusion.17), channel_id=1, source_target_pairs={{0,16},{4,20},{8,24},{12,28},{16,0},{20,4},{24,8},{28,12},{1,17},{... | collective-permute-start | bytes 110600 | tf_op jit(solution)/shard_map/ppermute | solution.py:723
  96.8 4.4 %collective-permute-start.22 = (bf16[32,1152]{1,0:T(8,128)(2,1)S(1)}, bf16[32,1152]{1,0:T(8,128)(2,1)S(1)}, u32[]{:S(2)}, u32[]{:S(2)}) collective-permute-start(bf16[32,1152]{1,0:T(8,128)(2,1)S(1)} %pad_maximum_fusion.3), channel_id=1, source_target_pairs={{0,8},{4,12},{8,0},{12,4},{16,24},{20,28},{24,16},{28,20},{1,9},{5... | collective-permute-start | bytes 221192 | tf_op jit(solution)/shard_map/ppermute | solution.py:723
  98.6 11.1 %collective-permute-start.27 = (bf16[64,1920]{1,0:T(8,128)(2,1)S(1)}, bf16[64,1920]{1,0:T(8,128)(2,1)S(1)}, u32[]{:S(2)}, u32[]{:S(2)}) collective-permute-start(bf16[64,1920]{1,0:T(8,128)(2,1)S(1)} %pad_maximum_fusion.early.refs_0_), channel_id=1, source_target_pairs={{0,4},{4,0},{8,12},{12,8},{16,20},{20,16},{24,28},{28,24},{1,5},{5... | collective-permute-start | bytes 737288 | tf_op jit(solution)/shard_map/ppermute | solution.py:723
  101.9 3.4 %collective-permute-start.25 = (f32[8,128]{1,0:T(8,128)S(1)}, f32[8,128]{1,0:T(8,128)S(1)}, u32[]{:S(2)}, u32[]{:S(2)}) collective-permute-start(f32[8,128]{1,0:T(8,128)S(1)} %half_squares.1), channel_id=1, source_target_pairs={{0,3},{1,2},{2,1},{3,0},{4,7},{5,6},{6,5},{7,4},{8,11},{9,10},{10,... | collective-permute-start | bytes 12296 | tf_op jit(solution)/shard_map/ppermute | solution.py:723
  102.0 3.7 %collective-permute-start.24 = (f32[8,128]{1,0:T(8,128)S(1)}, f32[8,128]{1,0:T(8,128)S(1)}, u32[]{:S(2)}, u32[]{:S(2)}) collective-permute-start(f32[8,128]{1,0:T(8,128)S(1)} %half_squares.1), channel_id=1, source_target_pairs={{0,2},{1,3},{2,0},{3,1},{4,6},{5,7},{6,4},{7,5},{8,10},{9,11},{10,... | collective-permute-start | bytes 12296 | tf_op jit(solution)/shard_map/ppermute | solution.py:723
  102.6 3.1 %collective-permute-start.23 = (f32[8,128]{1,0:T(8,128)S(1)}, f32[8,128]{1,0:T(8,128)S(1)}, u32[]{:S(2)}, u32[]{:S(2)}) collective-permute-start(f32[8,128]{1,0:T(8,128)S(1)} %half_squares.1), channel_id=1, source_target_pairs={{0,1},{1,0},{2,3},{3,2},{4,5},{5,4},{6,7},{7,6},{8,9},{9,8},{10,11... | collective-permute-start | bytes 12296 | tf_op jit(solution)/shard_map/ppermute | solution.py:723
  103.9 5.9 %collective-permute-start.28 = (bf16[64,1152]{1,0:T(8,128)(2,1)S(1)}, bf16[64,1152]{1,0:T(8,128)(2,1)S(1)}, u32[]{:S(2)}, u32[]{:S(2)}) collective-permute-start(bf16[64,1152]{1,0:T(8,128)(2,1)S(1)} %pad_maximum_fusion.1.late.refs_2_), channel_id=1, source_target_pairs={{0,4},{4,0},{8,12},{12,8},{16,20},{20,16},{24,28},{28,24},{1,5},{5... | collective-permute-start | bytes 442376 | tf_op jit(solution)/shard_map/ppermute | solution.py:723
  105.7 4.0 %collective-permute-start.26 = (f32[8,128]{1,0:T(8,128)S(1)}, f32[8,128]{1,0:T(8,128)S(1)}, u32[]{:S(2)}, u32[]{:S(2)}) collective-permute-start(f32[8,128]{1,0:T(8,128)S(1)} %add_add_fusion), channel_id=1, source_target_pairs={{0,4},{4,0},{8,12},{12,8},{16,20},{20,16},{24,28},{28,24},{1,5},{5... | collective-permute-start | bytes 12296 | tf_op jit(solution)/shard_map/ppermute | solution.py:723
  (25 other events, 472.0 us)
